TPU v7x, 32 devices: a whole 2x2x4 slice. The times are simulated.
32 devices in a mesh: vox: 8 (over z, x), chan: 4 (over y, core).
Axes of the slice: x: 2, y: 2, z: 4, core: 2. Of those that a mesh axis runs over, the one named last changes fastest.
Arguments:
- model_blocks: bfloat16 [2944, 128, 128], P(('vox', 'chan')), may hold values from -0.15625 to 0.15625
- start_image: float32 [256, 32, 128], P('vox'), may hold values from 0 to 2
- measured: float32 [256, 32, 128], P(('vox', 'chan')), may hold values from -6 to 6
- step_size: float32 [32], replicated, may hold values from 0.05 to 0.25
- sent_tiles: int32 [8, 8, 4], P('vox'), may hold values from -1 to 31, as said below
- block_rows: int32 [2944], P(('vox', 'chan')), may hold values from 0 to 7
- block_slots: int32 [2944], P(('vox', 'chan')), may hold values from 0 to 31, as said below
Outputs:
- estimate: float32 [256, 32, 128], P('vox')
- residual: float32 [256, 32, 128], P(('vox', 'chan'))
Inputs may be any that keep to these rules, and one draw needn't show every extreme that they name: `sent_tiles`: an entry is -1 for an unused slot, else a tile of slab j; the used slots of one pair (j, v) come first, hold distinct tiles, number 1 to 4, and slab v always uses all 4 slots for itself. `block_slots`: every block names a used slot of its own device's vox index v, that is sent_tiles[j, v, s] is not -1.
All inputs are finite; a program needn't handle non-finite values.
Results may differ from a plain program's by a relative error of at most 0.0045.
Values may be sent and summed in bfloat16 or wider, within the bound.
No kernel may reach another device: no remote copies, remote signals or barrier semaphores. Data moves between devices by JAX's collectives and lax.ppermute only.
A program may use at most 64 MiB of HBM per device.

v0:
```python
import jax
import jax.numpy as jnp
from jax import lax
from jax.sharding import PartitionSpec as P

ITERATIONS = 4


def shards(model_blocks, start_image, measured, step_size, sent_tiles, block_rows, block_slots):
    vox_count = lax.axis_size("vox")
    send_table = sent_tiles[0]
    capacity = send_table.shape[1]
    tile_count = start_image.shape[0]
    wave_count = start_image.shape[1]
    block_width = start_image.shape[2]
    row_count = measured.shape[0]
    block_count = model_blocks.shape[0]
    row_hot = (block_rows[None, :] == jnp.arange(row_count, dtype=jnp.int32)[:, None]).astype(
        jnp.float32
    )
    slot_hot = (
        block_slots[None, :] == jnp.arange(vox_count * capacity, dtype=jnp.int32)[:, None]
    ).astype(jnp.float32)
    tile_range = jnp.arange(tile_count, dtype=jnp.int32)[:, None]
    return_hot = (send_table.reshape(1, -1) == tile_range).astype(jnp.float32)
    step_gains = step_size[None, :, None]
    estimate = start_image
    residual = measured
    for iteration in range(ITERATIONS):
        rounded = estimate.astype(jnp.bfloat16)
        outgoing = jnp.take(rounded, jnp.maximum(send_table, 0), axis=0)
        arrived = lax.all_to_all(outgoing, "vox", split_axis=0, concat_axis=0, tiled=True)
        flat_tiles = arrived.reshape(vox_count * capacity, wave_count, block_width)
        forward_picked = jnp.take(flat_tiles, block_slots, axis=0)
        products = jnp.einsum(
            "bwv,bsv->bws", forward_picked, model_blocks, preferred_element_type=jnp.float32
        )
        summed = jnp.dot(
            row_hot,
            products.reshape(block_count, wave_count * block_width),
            precision=lax.Precision.HIGHEST,
        )
        residual = measured - summed.reshape(row_count, wave_count, block_width)
        narrow = residual.astype(jnp.bfloat16)
        picked = jnp.take(narrow, block_rows, axis=0)
        adjoint_terms = jnp.einsum(
            "bws,bsv->bwv", picked, model_blocks, preferred_element_type=jnp.float32
        )
        slot_sums = jnp.dot(
            slot_hot,
            adjoint_terms.reshape(block_count, wave_count * block_width),
            precision=lax.Precision.HIGHEST,
        )
        slot_sums = slot_sums.reshape(vox_count, capacity, wave_count, block_width)
        returned = lax.all_to_all(slot_sums, "vox", split_axis=0, concat_axis=0, tiled=True)
        local_sum = jnp.dot(
            return_hot,
            returned.reshape(-1, wave_count * block_width),
            precision=lax.Precision.HIGHEST,
        )
        slab_total = lax.psum(local_sum, "chan")
        estimate = jnp.maximum(
            estimate + step_gains * slab_total.reshape(tile_count, wave_count, block_width), 0.0
        )
    return (estimate, residual)


def solution(mesh):
    in_specs = (
        P(("vox", "chan"), None, None),
        P("vox", None, None),
        P(("vox", "chan"), None, None),
        P(),
        P("vox", None, None),
        P(("vox", "chan")),
        P(("vox", "chan")),
    )
    out_specs = (P("vox", None, None), P(("vox", "chan"), None, None))
    return jax.shard_map(shards, mesh=mesh, in_specs=in_specs, out_specs=out_specs, check_vma=False)
```

profile of v0, /device:TPU:0, one launch (start us, length us, event | category | flops | bytes accessed | tf_op | source)
XLA Modules:
  0.0 344.9 jit_solution(13415879437430342901)
XLA Ops:
  11.6 7.3 %all-to-all-start = ((bf16[8,4,32,128]{3,2,1,0:T(8,128)(2,1)}), bf16[8,4,32,128]{3,2,1,0:T(8,128)(2,1)S(1)}, u32[]{:S(2)}, u32[]{:S(2)}) async-start(bf16[8,4,32,128]{3,2,1,0:T(8,128)(2,1)} %broadcast_select_fusion.3), calls=%async_computation | async-start | bytes 524288 | tf_op jit(solution)/shard_map/all_to_all | solution.py:32
  20.3 7.5 %all-to-all-done = bf16[8,4,32,128]{3,2,1,0:T(8,128)(2,1)S(1)} async-done(((bf16[8,4,32,128]{3,2,1,0:T(8,128)(2,1)}), bf16[8,4,32,128]{3,2,1,0:T(8,128)(2,1)S(1)}, u32[]{:S(2)}, u32[]{:S(2)}) %all-to-all-start) | async-done | bytes 262176 | tf_op jit(solution)/shard_map/all_to_all | solution.py:32
  29.3 2.8 fusion.55
  36.1 2.1 fusion.53
  41.3 4.2 %all-to-all-start.1 = ((f32[8,4,32,128]{3,2,1,0:T(8,128)}), f32[8,4,32,128]{3,2,1,0:T(8,128)}, u32[]{:S(2)}, u32[]{:S(2)}) async-start(f32[8,4,32,128]{3,2,1,0:T(8,128)} %copy.76), calls=%async_computation.1 | async-start | bytes 1048576 | tf_op jit(solution)/shard_map/all_to_all | solution.py:55
  47.0 12.2 %all-to-all-done.1 = f32[8,4,32,128]{3,2,1,0:T(8,128)} async-done(((f32[8,4,32,128]{3,2,1,0:T(8,128)}), f32[8,4,32,128]{3,2,1,0:T(8,128)}, u32[]{:S(2)}, u32[]{:S(2)}) %all-to-all-start.1) | async-done | bytes 524320 | tf_op jit(solution)/shard_map/all_to_all | solution.py:55
  59.2 1.7 convolution_bitcast_fusion.3
  61.9 32.4 %all-reduce.5.cloned.1.call-done = f32[32,32,128]{2,1,0:T(8,128)} async-done(((f32[32,32,128]{2,1,0:T(8,128)}), f32[32,32,128]{2,1,0:T(8,128)}) %all-reduce.5.cloned.1.call-update) | async-done | bytes 524304 | tf_op jit(solution)/shard_map/psum | solution.py:61
  94.2 1.9 fusion.81
  97.8 13.5 %all_to_all.40 = bf16[8,4,32,128]{3,2,1,0:T(8,128)(2,1)S(1)} all-to-all(bf16[8,4,32,128]{3,2,1,0:T(8,128)(2,1)S(1)} %broadcast_select_fusion.2), channel_id=1, replica_groups=mesh['vox'=8,'chan'=4] {'vox'}, dimensions={0} | all-to-all | bytes 524288 | tf_op jit(solution)/shard_map/all_to_all | solution.py:32
  111.3 1.7 gather_fusion.4
  113.1 2.8 fusion.51
  118.3 1.7 gather_fusion.5
  120.0 2.1 fusion.49
  124.4 16.9 %all_to_all.41 = f32[8,4,32,128]{3,2,1,0:T(8,128)S(1)} all-to-all(f32[8,4,32,128]{3,2,1,0:T(8,128)S(1)} %copy.83), channel_id=1, replica_groups=mesh['vox'=8,'chan'=4] {'vox'}, dimensions={0} | all-to-all | bytes 1048576 | tf_op jit(solution)/shard_map/all_to_all | solution.py:55
  143.0 31.6 %all-reduce.7.cloned.1.call-done = f32[32,32,128]{2,1,0:T(8,128)} async-done(((f32[32,32,128]{2,1,0:T(8,128)}), f32[32,32,128]{2,1,0:T(8,128)}) %all-reduce.7.cloned.1.call-update) | async-done | bytes 524304 | tf_op jit(solution)/shard_map/psum | solution.py:61
  174.5 2.3 fusion.120
  178.5 13.5 %all_to_all.42 = bf16[8,4,32,128]{3,2,1,0:T(8,128)(2,1)S(1)} all-to-all(bf16[8,4,32,128]{3,2,1,0:T(8,128)(2,1)S(1)} %broadcast_select_fusion.1), channel_id=1, replica_groups=mesh['vox'=8,'chan'=4] {'vox'}, dimensions={0} | all-to-all | bytes 524288 | tf_op jit(solution)/shard_map/all_to_all | solution.py:32
  193.7 2.8 fusion.47
  200.6 2.1 fusion.45
  205.0 16.9 %all_to_all.43 = f32[8,4,32,128]{3,2,1,0:T(8,128)S(1)} all-to-all(f32[8,4,32,128]{3,2,1,0:T(8,128)S(1)} %copy.90), channel_id=1, replica_groups=mesh['vox'=8,'chan'=4] {'vox'}, dimensions={0} | all-to-all | bytes 1048576 | tf_op jit(solution)/shard_map/all_to_all | solution.py:55
  223.6 31.6 %all-reduce.9.cloned.1.call-done = f32[32,32,128]{2,1,0:T(8,128)} async-done(((f32[32,32,128]{2,1,0:T(8,128)}), f32[32,32,128]{2,1,0:T(8,128)}) %all-reduce.9.cloned.1.call-update) | async-done | bytes 524304 | tf_op jit(solution)/shard_map/psum | solution.py:61
  255.2 1.9 fusion.82
  258.8 13.5 %all_to_all.44 = bf16[8,4,32,128]{3,2,1,0:T(8,128)(2,1)S(1)} all-to-all(bf16[8,4,32,128]{3,2,1,0:T(8,128)(2,1)S(1)} %broadcast_select_fusion), channel_id=1, replica_groups=mesh['vox'=8,'chan'=4] {'vox'}, dimensions={0} | all-to-all | bytes 524288 | tf_op jit(solution)/shard_map/all_to_all | solution.py:32
  272.3 1.7 gather_fusion.10
  274.0 2.8 fusion.43
  277.8 2.1 fusion.121
  279.9 1.7 gather_fusion.11
  281.7 2.1 fusion.41
  286.0 16.9 %all_to_all.45 = f32[8,4,32,128]{3,2,1,0:T(8,128)S(1)} all-to-all(f32[8,4,32,128]{3,2,1,0:T(8,128)S(1)} %copy.97), channel_id=1, replica_groups=mesh['vox'=8,'chan'=4] {'vox'}, dimensions={0} | all-to-all | bytes 1048576 | tf_op jit(solution)/shard_map/all_to_all | solution.py:55
  306.2 30.0 %all-reduce.11.cloned.1.call-done = f32[32,32,128]{2,1,0:T(8,128)} async-done(((f32[32,32,128]{2,1,0:T(8,128)}), f32[32,32,128]{2,1,0:T(8,128)}) %all-reduce.11.cloned.1.call-update) | async-done | bytes 524304 | tf_op jit(solution)/shard_map/psum | solution.py:61
  336.2 2.2 add_maximum_fusion
  (129 shorter events, 44.1 us)
Async XLA Ops:
  7.2 22.1 %copy-start = (bf16[92,128,128]{2,1,0:T(8,128)(2,1)S(1)}, bf16[92,128,128]{2,1,0:T(8,128)(2,1)}, u32[]{:S(2)}) copy-start(bf16[92,128,128]{2,1,0:T(8,128)(2,1)} %param.13) | copy-start | bytes 9043972
  7.2 11.7 %copy-start.13 = (s32[92]{0:T(128)S(1)}, s32[92]{0:T(128)}, u32[]{:S(2)}) copy-start(s32[92]{0:T(128)} %param.18) | copy-start | bytes 1108
  7.2 11.7 %copy-start.18 = (s32[92]{0:T(128)S(1)}, s32[92]{0:T(128)}, u32[]{:S(2)}) copy-start(s32[92]{0:T(128)} %param.19) | copy-start | bytes 1108
  11.6 16.2 %all-to-all-start = ((bf16[8,4,32,128]{3,2,1,0:T(8,128)(2,1)}), bf16[8,4,32,128]{3,2,1,0:T(8,128)(2,1)S(1)}, u32[]{:S(2)}, u32[]{:S(2)}) async-start(bf16[8,4,32,128]{3,2,1,0:T(8,128)(2,1)} %broadcast_select_fusion.3), calls=%async_computation | async-start | bytes 524288 | tf_op jit(solution)/shard_map/all_to_all | solution.py:32
  18.9 13.3 %copy-start.11 = (s32[1024]{0:T(1024)}, s32[1024]{0:T(1024)S(1)}, u32[]{:S(2)}) copy-start(s32[1024]{0:T(1024)S(1)} %pad_clamp_fusion.1) | copy-start | bytes 12292
  18.9 15.7 %copy-start.10 = (s32[1024]{0:T(1024)}, s32[1024]{0:T(1024)S(1)}, u32[]{:S(2)}) copy-start(s32[1024]{0:T(1024)S(1)} %pad_clamp_fusion) | copy-start | bytes 12292
  19.6 16.5 %copy-start.23 = (pred[92]{0:T(512)(128)(4,1)}, pred[92]{0:T(512)(128)(4,1)S(1)}, u32[]{:S(2)}) copy-start(pred[92]{0:T(512)(128)(4,1)S(1)} %compare_and_fusion) | copy-start | bytes 280
  20.3 9.1 %copy-start.27 = (pred[92]{0:T(512)(128)(4,1)}, pred[92]{0:T(512)(128)(4,1)S(1)}, u32[]{:S(2)}) copy-start(pred[92]{0:T(512)(128)(4,1)S(1)} %compare_and_fusion.1) | copy-start | bytes 280
  32.1 0.9 copy-start.5
  40.4 5.1 %copy-start.9 = (s32[1,8,4]{1,2,0:T(4,128)S(1)}, s32[1,8,4]{1,2,0:T(4,128)}, u32[]{:S(2)}) copy-start(s32[1,8,4]{1,2,0:T(4,128)} %param.17) | copy-start | bytes 388
  41.3 17.9 %all-to-all-start.1 = ((f32[8,4,32,128]{3,2,1,0:T(8,128)}), f32[8,4,32,128]{3,2,1,0:T(8,128)}, u32[]{:S(2)}, u32[]{:S(2)}) async-start(f32[8,4,32,128]{3,2,1,0:T(8,128)} %copy.76), calls=%async_computation.1 | async-start | bytes 1048576 | tf_op jit(solution)/shard_map/all_to_all | solution.py:55
  45.5 48.8 %copy-start.3 = (f32[32,32,128]{2,1,0:T(8,128)S(1)}, f32[32,32,128]{2,1,0:T(8,128)}, u32[]{:S(2)}) copy-start(f32[32,32,128]{2,1,0:T(8,128)} %param.14) | copy-start | bytes 1572868
  45.5 48.8 %all-reduce.5.cloned.1.call-start = ((), (), s32[]{:S(2)}) async-start(), calls=%async_computation.8 | async-start | bytes 1048576 | tf_op jit(solution)/shard_map/psum | solution.py:61
  61.8 112.7 %all-reduce.7.cloned.1.call-start = ((), (), s32[]{:S(2)}) async-start(), calls=%async_computation.9 | async-start | bytes 1048576 | tf_op jit(solution)/shard_map/psum | solution.py:61
  96.1 16.9 %copy-start.28 = (pred[92]{0:T(512)(128)(4,1)S(1)}, pred[92]{0:T(512)(128)(4,1)}, u32[]{:S(2)}) copy-start(pred[92]{0:T(512)(128)(4,1)} %copy-done.27) | copy-start | bytes 280
  115.9 0.9 copy-start.6
  115.9 0.9 copy-start.15
  116.8 3.2 copy-start.24
  141.3 33.2 %copy-start.4 = (f32[32,32,128]{2,1,0:T(8,128)S(1)}, f32[32,32,128]{2,1,0:T(8,128)}, u32[]{:S(2)}) copy-start(f32[32,32,128]{2,1,0:T(8,128)} %param.14) | copy-start | bytes 1572868
  142.9 112.2 %all-reduce.9.cloned.1.call-start = ((), (), s32[]{:S(2)}) async-start(), calls=%async_computation.10 | async-start | bytes 1048576 | tf_op jit(solution)/shard_map/psum | solution.py:61
  176.8 16.9 %copy-start.29 = (pred[92]{0:T(512)(128)(4,1)S(1)}, pred[92]{0:T(512)(128)(4,1)}, u32[]{:S(2)}) copy-start(pred[92]{0:T(512)(128)(4,1)} %copy-done.27) | copy-start | bytes 280
  196.5 0.9 copy-start.7
  196.5 0.9 copy-start.16
  197.5 3.2 copy-start.25
  221.9 33.3 %copy-start.1 = (f32[32,32,128]{2,1,0:T(8,128)S(1)}, f32[32,32,128]{2,1,0:T(8,128)}, u32[]{:S(2)}) copy-start(f32[32,32,128]{2,1,0:T(8,128)} %get-tuple-element.14) | copy-start | bytes 1572868
  223.6 112.6 %all-reduce.11.cloned.1.call-start = ((), (), s32[]{:S(2)}) async-start(), calls=%async_computation.11 | async-start | bytes 1048576 | tf_op jit(solution)/shard_map/psum | solution.py:61
  257.1 16.9 %copy-start.30 = (pred[92]{0:T(512)(128)(4,1)S(1)}, pred[92]{0:T(512)(128)(4,1)}, u32[]{:S(2)}) copy-start(pred[92]{0:T(512)(128)(4,1)} %copy-done.27) | copy-start | bytes 280
  276.8 0.9 copy-start.8
  276.8 0.9 copy-start.17
  277.8 3.9 %copy-start.26 = (pred[92]{0:T(512)(128)(4,1)S(1)}, pred[92]{0:T(512)(128)(4,1)}, u32[]{:S(2)}) copy-start(pred[92]{0:T(512)(128)(4,1)} %copy-done.23) | copy-start | bytes 280
  302.9 33.2 %copy-start.2 = (f32[32,32,128]{2,1,0:T(8,128)S(1)}, f32[32,32,128]{2,1,0:T(8,128)}, u32[]{:S(2)}) copy-start(f32[32,32,128]{2,1,0:T(8,128)} %get-tuple-element.14) | copy-start | bytes 1572868
  302.9 33.2 %copy-start.12 = (f32[32]{0:T(128)S(1)}, f32[32]{0:T(128)}, u32[]{:S(2)}) copy-start(f32[32]{0:T(128)} %param.16) | copy-start | bytes 388
  (5 other events, 3.6 us)
Sparse Core Ops, SparseCore 0:
  61.9 32.2 all-reduce.4
  143.0 31.4 all-reduce.6
  223.7 31.4 all-reduce.8
  304.7 31.3 all-reduce.10
where the time goes:
time: 346 us; the launch traced here: 345 us
  waiting for transfers between devices  145 us (42%)
  blocking collectives  91.3 us (26%)
  matrix products  36 us (10%)
  local copies, waits for them, and re-layouts  33.1 us (10%)
  between operations  14.2 us (4%)
  other arithmetic  13.5 us (4%)
  starting transfers between devices  11.6 us (3%)
    psum x4, waiting for transfers between devices, shards(): slab_total = lax.psum(local_sum, 'chan')  125 us
    all_to_all x3, blocking collectives, shards(): lax.all_to_all(slot_sums, 'vox', split_axis=0, concat_axis=0, tiled=True)  50.7 us
    all_to_all x3, blocking collectives, shards(): lax.all_to_all(outgoing, 'vox', split_axis=0, concat_axis=0, tiled=True)  40.6 us
    all_to_all x1, waiting for transfers between devices, shards(): lax.all_to_all(slot_sums, 'vox', split_axis=0, concat_axis=0, tiled=True)  12.2 us
    dot_general x4, matrix products, shards(): jnp.einsum('bwv,bsv->bws', forward_picked, model_blocks, preferred_elemen...  11.3 us
    unnamed x68, local copies, waits for them, and re-layouts  11.2 us
    dot_general x4, matrix products, shards(): jnp.einsum('bws,bsv->bwv', picked, model_blocks, preferred_element_type=j...  8.28 us
    all_to_all x1, waiting for transfers between devices, shards(): lax.all_to_all(outgoing, 'vox', split_axis=0, concat_axis=0, tiled=True)  7.49 us
  transfers between devices with their start and end apart: 6, of which 6 were waited for; matrix products, arithmetic and copies ran while one was open for 1% of the time, Pallas kernels for 0%

commit v1 on v0

v1 whole, which is shorter than its diff:
```python
import functools
import math

import jax
import jax.numpy as jnp
from jax import lax
from jax.experimental import pallas as pl
from jax.experimental.pallas import tpu as pltpu
from jax.sharding import PartitionSpec as P

ITERATIONS = 4
LOW = 8


VMEM = pl.BlockSpec(memory_space=pltpu.VMEM)
SMEM = pl.BlockSpec(memory_space=pltpu.SMEM)
PARAMS = pltpu.CompilerParams(vmem_limit_bytes=32 * 1024 * 1024)


def model_kernel(vox_count, chan_count, per, low, slots, rows, model, measured, *refs):
    arrived = refs[:low]
    own, *sent = refs[low : low + chan_count]
    residual, tiles, narrow, sums = refs[low + chan_count :]
    wide = vox_count * per
    for e in range(vox_count):
        for d in range(chan_count):
            place = d * wide + e * per
            tiles[place : place + per] = arrived[e % low][e // low, d * per : (d + 1) * per]
    residual[...] = measured[...]
    sums[...] = jnp.zeros_like(sums)
    count = model.shape[0]
    for k in range(count):
        part = lax.dot_general(
            tiles[slots[k]],
            model[k],
            (((1,), (1,)), ((), ())),
            preferred_element_type=jnp.float32,
        )
        residual[rows[k]] -= part
    narrow[...] = residual[...].astype(jnp.bfloat16)
    for k in range(count):
        part = jnp.dot(narrow[rows[k]], model[k], preferred_element_type=jnp.float32)
        sums[slots[k]] += part
    own[...] = sums[:wide]
    for d, out in enumerate(sent, 1):
        out[...] = sums[d * wide : (d + 1) * wide].astype(jnp.bfloat16)


def reduce_kernel(vox_count, chan_count, per, low, own, *refs):
    received, outs = refs[: chan_count - 1], refs[chan_count - 1 :]
    total = own[...]
    for piece in received:
        total = total + piece[...].astype(jnp.float32)
    total = total.astype(jnp.bfloat16)
    for e in range(vox_count):
        outs[e % low][e // low] = total[e * per : (e + 1) * per]


def place_of(ids, table, per, d, e, p):
    return jnp.maximum(table[ids[0] ^ e, (ids[1] ^ d) * per + p], 0)


def pick_kernel(vox_count, chan_count, per, low, ids, table, image, *outs):
    for e in range(vox_count):
        for d in range(chan_count):
            for p in range(per):
                tile = place_of(ids, table, per, d, e, p)
                outs[e % low][e // low, d * per + p] = image[tile].astype(jnp.bfloat16)


def update_kernel(vox_count, chan_count, per, low, ids, table, gains, image, *refs):
    received = refs[:chan_count]
    estimate, *outs = refs[chan_count:-1]
    gradient = refs[-1]
    gradient[...] = jnp.zeros_like(gradient)
    for d in range(chan_count):
        for e in range(vox_count):
            for p in range(per):
                tile = place_of(ids, table, per, d, e, p)
                gradient[tile] += received[d][e * per + p].astype(jnp.float32)
    estimate[...] = jnp.maximum(image[...] + gains[...][None] * gradient[...], 0.0)
    if outs:
        pick_kernel(vox_count, chan_count, per, low, ids, table, estimate, *outs)


def shards(model_blocks, start_image, measured, step_size, sent_tiles, block_rows, block_slots):
    vox_count = lax.axis_size("vox")
    chan_count = lax.axis_size("chan")
    vox, chan = lax.axis_index("vox"), lax.axis_index("chan")
    table = sent_tiles[0]
    capacity = table.shape[1]
    per = capacity // chan_count
    tile_count, wave_count, width = start_image.shape
    row_count = measured.shape[0]
    slot_count = vox_count * capacity
    wide = vox_count * per
    low = math.gcd(vox_count, LOW)
    high = vox_count // low
    tile = (wave_count, width)
    ids = jnp.stack([vox, chan]).astype(jnp.int32)
    slab, slot = block_slots // capacity, block_slots % capacity
    places = (((slot // per) ^ chan) * vox_count + (slab ^ vox)) * per + slot % per
    gains = jnp.broadcast_to(step_size[:, None], tile)

    def shape(count, dtype):
        return jax.ShapeDtypeStruct((count, *tile), dtype)

    def group(count):
        return [jax.ShapeDtypeStruct((high, count, *tile), jnp.bfloat16)] * low

    def swap(array, axis, size, step):
        if step == 0:
            return array
        return lax.ppermute(array, axis, [(i, i ^ step) for i in range(size)])

    def exchange(pieces):
        pieces = [swap(piece, "vox", vox_count, e) for e, piece in enumerate(pieces)]
        if high == 1:
            return pieces
        both = jnp.stack(pieces)
        both = [swap(both[:, e], "vox", vox_count, e * low) for e in range(high)]
        return list(jnp.stack(both, axis=1))

    apply_model = pl.pallas_call(
        functools.partial(model_kernel, vox_count, chan_count, per, low),
        out_shape=(
            shape(wide, jnp.float32),
            *[shape(wide, jnp.bfloat16)] * (chan_count - 1),
            shape(row_count, jnp.float32),
        ),
        in_specs=[SMEM, SMEM, VMEM, VMEM] + [VMEM] * low,
        out_specs=[VMEM] * (chan_count + 1),
        scratch_shapes=[
            pltpu.VMEM((slot_count, *tile), jnp.bfloat16),
            pltpu.VMEM((row_count, *tile), jnp.bfloat16),
            pltpu.VMEM((slot_count, *tile), jnp.float32),
        ],
        compiler_params=PARAMS,
        name="model",
    )
    reduce_parts = pl.pallas_call(
        functools.partial(reduce_kernel, vox_count, chan_count, per, low),
        out_shape=group(per),
        in_specs=[VMEM] * chan_count,
        out_specs=[VMEM] * low,
        compiler_params=PARAMS,
        name="reduce",
    )
    pick = pl.pallas_call(
        functools.partial(pick_kernel, vox_count, chan_count, per, low),
        out_shape=group(capacity),
        in_specs=[SMEM, SMEM, VMEM],
        out_specs=[VMEM] * low,
        compiler_params=PARAMS,
        name="pick",
    )

    def update(last):
        outs = [] if last else group(capacity)
        return pl.pallas_call(
            functools.partial(update_kernel, vox_count, chan_count, per, low),
            out_shape=[shape(tile_count, jnp.float32)] + outs,
            in_specs=[SMEM, SMEM, VMEM, VMEM] + [VMEM] * chan_count,
            out_specs=[VMEM] * (len(outs) + 1),
            scratch_shapes=[pltpu.VMEM((tile_count, *tile), jnp.float32)],
            compiler_params=PARAMS,
            name="update",
        )

    estimate = start_image
    outgoing = pick(ids, table, start_image)
    for iteration in range(ITERATIONS):
        own, *rest = apply_model(
            places, block_rows, model_blocks, measured, *exchange(outgoing)
        )
        *partial, residual = rest
        received = [swap(piece, "chan", chan_count, d) for d, piece in enumerate(partial, 1)]
        totals = reduce_parts(own, *received)
        returned = jnp.stack(exchange(totals), axis=1).reshape(wide, *tile)
        spread = [swap(returned, "chan", chan_count, d) for d in range(chan_count)]
        estimate, *outgoing = update(iteration == ITERATIONS - 1)(
            ids, table, gains, estimate, *spread
        )
    return (estimate, residual)


def solution(mesh):
    in_specs = (
        P(("vox", "chan"), None, None),
        P("vox", None, None),
        P(("vox", "chan"), None, None),
        P(),
        P("vox", None, None),
        P(("vox", "chan")),
        P(("vox", "chan")),
    )
    out_specs = (P("vox", None, None), P(("vox", "chan"), None, None))
    return jax.shard_map(shards, mesh=mesh, in_specs=in_specs, out_specs=out_specs, check_vma=False)
```

time: 346 us -> 194 us (0.56)
  starting transfers between devices: 11.6 us -> 106 us
  blocking collectives: 91.3 us -> 0 us
  waiting for transfers between devices: 145 us -> 60.7 us
  matrix products: 36 us -> 0 us
  local copies, waits for them, and re-layouts: 33.1 us -> 5.56 us
  Pallas kernels: 0 us -> 20.2 us
  between operations: 14.2 us -> 0.86 us
  other arithmetic: 13.5 us -> 0.74 us
    psum x4 -> x0, waiting for transfers between devices: 125 us -> none  [shards(): slab_total = lax.psum(local_sum, 'chan')]
    ppermute x0 -> x80, starting transfers between devices: none -> 106 us  [swap(): return lax.ppermute(array, axis, [(i, i ^ step) for i in range(size)])]
    all_to_all x6 -> x0, blocking collectives: 91.3 us -> none  [the longest x3 50.7 us: shards(): lax.all_to_all(slot_sums, 'vox', split_axis=0, concat_axis=0, tiled=True)]
    ppermute x0 -> x80, waiting for transfers between devices: none -> 60.7 us  [swap(): return lax.ppermute(array, axis, [(i, i ^ step) for i in range(size)])]
    dot_general x20 -> x0, matrix products: 36 us -> none  [the longest x4 11.3 us: shards(): jnp.einsum('bwv,bsv->bws', forward_picked, model_blocks, preferred_elemen...]
    pallas_call x0 -> x13, Pallas kernels: none -> 20.2 us  [the longest x4 14.7 us: shards(): apply_model(places, block_rows, model_blocks, measured, *exchange(outgoing))]
    all_to_all x2 -> x0, waiting for transfers between devices: 19.7 us -> none  [the longest x1 12.2 us: shards(): lax.all_to_all(slot_sums, 'vox', split_axis=0, concat_axis=0, tiled=True)]
    gather x12 -> x0, local copies, waits for them, and re-layouts: 18.6 us -> none  [the longest x4 6.7 us: shards(): picked = jnp.take(narrow, block_rows, axis=0)]
  transfers between devices with their start and end apart: 6 -> 80, of which waited for: 6 -> 36; matrix products, arithmetic and copies ran while one was open for 1% -> 0% of each run, Pallas kernels for 0% -> 0%
where the time goes in v1:
time: 194 us
  starting transfers between devices  106 us (55%)
  waiting for transfers between devices  60.7 us (31%)
  Pallas kernels  20.2 us (10%)
  local copies, waits for them, and re-layouts  5.56 us (3%)
    ppermute x80, starting transfers between devices, swap(): return lax.ppermute(array, axis, [(i, i ^ step) for i in range(size)])  106 us
    ppermute x80, waiting for transfers between devices, swap(): return lax.ppermute(array, axis, [(i, i ^ step) for i in range(size)])  60.7 us
    pallas_call x4, Pallas kernels, shards(): apply_model(places, block_rows, model_blocks, measured, *exchange(outgoing))  14.7 us
    pallas_call x4, Pallas kernels, shards(): update(iteration == ITERATIONS - 1)(ids, table, gains, estimate, *spread)  4.68 us
    unnamed x46, local copies, waits for them, and re-layouts  4.67 us
  transfers between devices with their start and end apart: 80, of which 36 were waited for; matrix products, arithmetic and copies ran while one was open for 0% of the time, Pallas kernels for 0%

profile of v1, /device:TPU:0, one launch (start us, length us, event | category | flops | bytes accessed | tf_op | source)
XLA Modules:
  0.0 193.9 jit_solution(11453361324627568590)
XLA Ops:
  3.3 3.0 %collective-permute-start = (bf16[1,4,32,128]{3,2,1,0:T(8,128)(2,1)S(1)}, bf16[1,4,32,128]{3,2,1,0:T(8,128)(2,1)S(1)}, u32[]{:S(2)}, u32[]{:S(2)}) collective-permute-start(bf16[1,4,32,128]{3,2,1,0:T(8,128)(2,1)S(1)} %get-tuple-element.87), channel_id=1, source_target_pairs={{0,4},{4,0},{8,12},{12,8},{16,20},{20,16},{24,28},{28,24},{1,5},{5... | collective-permute-start | bytes 98312 | tf_op jit(solution)/shard_map/ppermute | solution.py:114
  7.8 3.0 %collective-permute-start.3 = (bf16[1,4,32,128]{3,2,1,0:T(8,128)(2,1)S(1)}, bf16[1,4,32,128]{3,2,1,0:T(8,128)(2,1)S(1)}, u32[]{:S(2)}, u32[]{:S(2)}) collective-permute-start(bf16[1,4,32,128]{3,2,1,0:T(8,128)(2,1)S(1)} %get-tuple-element.90), channel_id=1, source_target_pairs={{0,16},{4,20},{8,24},{12,28},{16,0},{20,4},{24,8},{28,12},{1,17},{... | collective-permute-start | bytes 98312 | tf_op jit(solution)/shard_map/ppermute | solution.py:114
  12.1 3.6 %collective-permute-start.5 = (bf16[1,4,32,128]{3,2,1,0:T(8,128)(2,1)S(1)}, bf16[1,4,32,128]{3,2,1,0:T(8,128)(2,1)S(1)}, u32[]{:S(2)}, u32[]{:S(2)}) collective-permute-start(bf16[1,4,32,128]{3,2,1,0:T(8,128)(2,1)S(1)} %get-tuple-element.92), channel_id=1, source_target_pairs={{0,24},{4,28},{8,16},{12,20},{16,8},{20,12},{24,0},{28,4},{1,25},{... | collective-permute-start | bytes 98312 | tf_op jit(solution)/shard_map/ppermute | solution.py:114
  18.0 4.4 %collective-permute-done.6.refs_7_ = bf16[1,4,32,128]{3,2,1,0:T(8,128)(2,1)S(1)} collective-permute-done((bf16[1,4,32,128]{3,2,1,0:T(8,128)(2,1)S(1)}, bf16[1,4,32,128]{3,2,1,0:T(8,128)(2,1)S(1)}, u32[]{:S(2)}, u32[]{:S(2)}) %collective-permute-start.6) | collective-permute-done | bytes 32800 | tf_op jit(solution)/shard_map/ppermute | solution.py:114
  25.7 3.7 %model.8 = (f32[8,32,128]{2,1,0:T(8,128)S(1)}, bf16[8,32,128]{2,1,0:T(8,128)(2,1)S(1)}, bf16[8,32,128]{2,1,0:T(8,128)(2,1)S(1)}, bf16[8,32,128]{2,1,0:T(8,128)(2,1)S(1)}, f32[8,32,128]{2,1,0:T(8,128)}) custom-call(s32[92]{0:T(128)S(1)} %fusion.2.slots, s32[92]{0:T(128)S(1)} %copy-done.6, bf16[92,128,128]{2,1,0:T(8,128)(2,1)S(1)} %copy-done, ...), custom_call_target="tpu_custom_call" | custom-call | tf_op jit(solution)/shard_map/model/pallas_call | solution.py:173
  31.3 2.6 %collective-permute-done.8.refs_1_ = bf16[8,32,128]{2,1,0:T(8,128)(2,1)S(1)} collective-permute-done((bf16[8,32,128]{2,1,0:T(8,128)(2,1)S(1)}, bf16[8,32,128]{2,1,0:T(8,128)(2,1)S(1)}, u32[]{:S(2)}, u32[]{:S(2)}) %collective-permute-start.8) | collective-permute-done | bytes 65568 | tf_op jit(solution)/shard_map/ppermute | solution.py:114
  35.6 3.0 %collective-permute-start.12 = (bf16[1,1,32,128]{3,2,1,0:T(8,128)(2,1)S(1)}, bf16[1,1,32,128]{3,2,1,0:T(8,128)(2,1)S(1)}, u32[]{:S(2)}, u32[]{:S(2)}) collective-permute-start(bf16[1,1,32,128]{3,2,1,0:T(8,128)(2,1)S(1)} %get-tuple-element.101), channel_id=1, source_target_pairs={{0,12},{4,8},{8,4},{12,0},{16,28},{20,24},{24,20},{28,16},{1,13},{... | collective-permute-start | bytes 24584 | tf_op jit(solution)/shard_map/ppermute | solution.py:114
  38.6 2.9 %collective-permute-start.14 = (bf16[1,1,32,128]{3,2,1,0:T(8,128)(2,1)S(1)}, bf16[1,1,32,128]{3,2,1,0:T(8,128)(2,1)S(1)}, u32[]{:S(2)}, u32[]{:S(2)}) collective-permute-start(bf16[1,1,32,128]{3,2,1,0:T(8,128)(2,1)S(1)} %get-tuple-element.103), channel_id=1, source_target_pairs={{0,20},{4,16},{8,28},{12,24},{16,4},{20,0},{24,12},{28,8},{1,21},{... | collective-permute-start | bytes 24584 | tf_op jit(solution)/shard_map/ppermute | solution.py:114
  41.9 4.4 %collective-permute-start.16 = (bf16[1,1,32,128]{3,2,1,0:T(8,128)(2,1)S(1)}, bf16[1,1,32,128]{3,2,1,0:T(8,128)(2,1)S(1)}, u32[]{:S(2)}, u32[]{:S(2)}) collective-permute-start(bf16[1,1,32,128]{3,2,1,0:T(8,128)(2,1)S(1)} %get-tuple-element.105), channel_id=1, source_target_pairs={{0,28},{4,24},{8,20},{12,16},{16,12},{20,8},{24,4},{28,0},{1,29},{... | collective-permute-start | bytes 24584 | tf_op jit(solution)/shard_map/ppermute | solution.py:114
  50.1 2.5 %collective-permute-done.19.refs_3_ = bf16[8,32,128]{2,1,0:T(8,128)(2,1)S(1)} collective-permute-done((bf16[8,32,128]{2,1,0:T(8,128)(2,1)S(1)}, bf16[8,32,128]{2,1,0:T(8,128)(2,1)S(1)}, u32[]{:S(2)}, u32[]{:S(2)}) %collective-permute-start.19) | collective-permute-done | bytes 65568 | tf_op jit(solution)/shard_map/ppermute | solution.py:114
  62.4 3.6 %collective-permute-start.25 = (bf16[1,4,32,128]{3,2,1,0:T(8,128)(2,1)S(1)}, bf16[1,4,32,128]{3,2,1,0:T(8,128)(2,1)S(1)}, u32[]{:S(2)}, u32[]{:S(2)}) collective-permute-start(bf16[1,4,32,128]{3,2,1,0:T(8,128)(2,1)S(1)} %get-tuple-element.113), channel_id=1, source_target_pairs={{0,24},{4,28},{8,16},{12,20},{16,8},{20,12},{24,0},{28,4},{1,25},{... | collective-permute-start | bytes 98312 | tf_op jit(solution)/shard_map/ppermute | solution.py:114
  68.2 4.4 %collective-permute-done.26.refs_7_ = bf16[1,4,32,128]{3,2,1,0:T(8,128)(2,1)S(1)} collective-permute-done((bf16[1,4,32,128]{3,2,1,0:T(8,128)(2,1)S(1)}, bf16[1,4,32,128]{3,2,1,0:T(8,128)(2,1)S(1)}, u32[]{:S(2)}, u32[]{:S(2)}) %collective-permute-start.26) | collective-permute-done | bytes 32800 | tf_op jit(solution)/shard_map/ppermute | solution.py:114
  72.6 3.7 %model.10 = (f32[8,32,128]{2,1,0:T(8,128)S(1)}, bf16[8,32,128]{2,1,0:T(8,128)(2,1)S(1)}, bf16[8,32,128]{2,1,0:T(8,128)(2,1)S(1)}, bf16[8,32,128]{2,1,0:T(8,128)(2,1)S(1)}, f32[8,32,128]{2,1,0:T(8,128)}) custom-call(s32[92]{0:T(128)S(1)} %fusion.2.slots, s32[92]{0:T(128)S(1)} %copy-done.7, bf16[92,128,128]{2,1,0:T(8,128)(2,1)S(1)} %copy-done.1, ...), custom_call_target="tpu_custom_call" | custom-call | tf_op jit(solution)/shard_map/model/pallas_call | solution.py:173
  78.1 3.0 %collective-permute-done.28.refs_1_ = bf16[8,32,128]{2,1,0:T(8,128)(2,1)S(1)} collective-permute-done((bf16[8,32,128]{2,1,0:T(8,128)(2,1)S(1)}, bf16[8,32,128]{2,1,0:T(8,128)(2,1)S(1)}, u32[]{:S(2)}, u32[]{:S(2)}) %collective-permute-start.28) | collective-permute-done | bytes 65568 | tf_op jit(solution)/shard_map/ppermute | solution.py:114
  82.4 2.9 %collective-permute-start.32 = (bf16[1,1,32,128]{3,2,1,0:T(8,128)(2,1)S(1)}, bf16[1,1,32,128]{3,2,1,0:T(8,128)(2,1)S(1)}, u32[]{:S(2)}, u32[]{:S(2)}) collective-permute-start(bf16[1,1,32,128]{3,2,1,0:T(8,128)(2,1)S(1)} %get-tuple-element.122), channel_id=1, source_target_pairs={{0,12},{4,8},{8,4},{12,0},{16,28},{20,24},{24,20},{28,16},{1,13},{... | collective-permute-start | bytes 24584 | tf_op jit(solution)/shard_map/ppermute | solution.py:114
  85.4 2.9 %collective-permute-start.34 = (bf16[1,1,32,128]{3,2,1,0:T(8,128)(2,1)S(1)}, bf16[1,1,32,128]{3,2,1,0:T(8,128)(2,1)S(1)}, u32[]{:S(2)}, u32[]{:S(2)}) collective-permute-start(bf16[1,1,32,128]{3,2,1,0:T(8,128)(2,1)S(1)} %get-tuple-element.124), channel_id=1, source_target_pairs={{0,20},{4,16},{8,28},{12,24},{16,4},{20,0},{24,12},{28,8},{1,21},{... | collective-permute-start | bytes 24584 | tf_op jit(solution)/shard_map/ppermute | solution.py:114
  88.7 4.4 %collective-permute-start.36 = (bf16[1,1,32,128]{3,2,1,0:T(8,128)(2,1)S(1)}, bf16[1,1,32,128]{3,2,1,0:T(8,128)(2,1)S(1)}, u32[]{:S(2)}, u32[]{:S(2)}) collective-permute-start(bf16[1,1,32,128]{3,2,1,0:T(8,128)(2,1)S(1)} %get-tuple-element.126), channel_id=1, source_target_pairs={{0,28},{4,24},{8,20},{12,16},{16,12},{20,8},{24,4},{28,0},{1,29},{... | collective-permute-start | bytes 24584 | tf_op jit(solution)/shard_map/ppermute | solution.py:114
  108.2 3.6 %collective-permute-start.45 = (bf16[1,4,32,128]{3,2,1,0:T(8,128)(2,1)S(1)}, bf16[1,4,32,128]{3,2,1,0:T(8,128)(2,1)S(1)}, u32[]{:S(2)}, u32[]{:S(2)}) collective-permute-start(bf16[1,4,32,128]{3,2,1,0:T(8,128)(2,1)S(1)} %get-tuple-element.134), channel_id=1, source_target_pairs={{0,24},{4,28},{8,16},{12,20},{16,8},{20,12},{24,0},{28,4},{1,25},{... | collective-permute-start | bytes 98312 | tf_op jit(solution)/shard_map/ppermute | solution.py:114
  114.0 4.4 %collective-permute-done.46.refs_7_ = bf16[1,4,32,128]{3,2,1,0:T(8,128)(2,1)S(1)} collective-permute-done((bf16[1,4,32,128]{3,2,1,0:T(8,128)(2,1)S(1)}, bf16[1,4,32,128]{3,2,1,0:T(8,128)(2,1)S(1)}, u32[]{:S(2)}, u32[]{:S(2)}) %collective-permute-start.46) | collective-permute-done | bytes 32800 | tf_op jit(solution)/shard_map/ppermute | solution.py:114
  118.4 3.7 %model.12 = (f32[8,32,128]{2,1,0:T(8,128)S(1)}, bf16[8,32,128]{2,1,0:T(8,128)(2,1)S(1)}, bf16[8,32,128]{2,1,0:T(8,128)(2,1)S(1)}, bf16[8,32,128]{2,1,0:T(8,128)(2,1)S(1)}, f32[8,32,128]{2,1,0:T(8,128)}) custom-call(s32[92]{0:T(128)S(1)} %fusion.2.slots, s32[92]{0:T(128)S(1)} %copy-done.7, bf16[92,128,128]{2,1,0:T(8,128)(2,1)S(1)} %copy-done.1, ...), custom_call_target="tpu_custom_call" | custom-call | tf_op jit(solution)/shard_map/model/pallas_call | solution.py:173
  123.9 2.8 %collective-permute-done.48.refs_1_ = bf16[8,32,128]{2,1,0:T(8,128)(2,1)S(1)} collective-permute-done((bf16[8,32,128]{2,1,0:T(8,128)(2,1)S(1)}, bf16[8,32,128]{2,1,0:T(8,128)(2,1)S(1)}, u32[]{:S(2)}, u32[]{:S(2)}) %collective-permute-start.48) | collective-permute-done | bytes 65568 | tf_op jit(solution)/shard_map/ppermute | solution.py:114
  128.4 2.9 %collective-permute-start.52 = (bf16[1,1,32,128]{3,2,1,0:T(8,128)(2,1)S(1)}, bf16[1,1,32,128]{3,2,1,0:T(8,128)(2,1)S(1)}, u32[]{:S(2)}, u32[]{:S(2)}) collective-permute-start(bf16[1,1,32,128]{3,2,1,0:T(8,128)(2,1)S(1)} %get-tuple-element.143), channel_id=1, source_target_pairs={{0,12},{4,8},{8,4},{12,0},{16,28},{20,24},{24,20},{28,16},{1,13},{... | collective-permute-start | bytes 24584 | tf_op jit(solution)/shard_map/ppermute | solution.py:114
  131.3 2.9 %collective-permute-start.54 = (bf16[1,1,32,128]{3,2,1,0:T(8,128)(2,1)S(1)}, bf16[1,1,32,128]{3,2,1,0:T(8,128)(2,1)S(1)}, u32[]{:S(2)}, u32[]{:S(2)}) collective-permute-start(bf16[1,1,32,128]{3,2,1,0:T(8,128)(2,1)S(1)} %get-tuple-element.145), channel_id=1, source_target_pairs={{0,20},{4,16},{8,28},{12,24},{16,4},{20,0},{24,12},{28,8},{1,21},{... | collective-permute-start | bytes 24584 | tf_op jit(solution)/shard_map/ppermute | solution.py:114
  134.7 4.3 %collective-permute-start.56 = (bf16[1,1,32,128]{3,2,1,0:T(8,128)(2,1)S(1)}, bf16[1,1,32,128]{3,2,1,0:T(8,128)(2,1)S(1)}, u32[]{:S(2)}, u32[]{:S(2)}) collective-permute-start(bf16[1,1,32,128]{3,2,1,0:T(8,128)(2,1)S(1)} %get-tuple-element.147), channel_id=1, source_target_pairs={{0,28},{4,24},{8,20},{12,16},{16,12},{20,8},{24,4},{28,0},{1,29},{... | collective-permute-start | bytes 24584 | tf_op jit(solution)/shard_map/ppermute | solution.py:114
  142.9 2.5 %collective-permute-done.59.refs_3_ = bf16[8,32,128]{2,1,0:T(8,128)(2,1)S(1)} collective-permute-done((bf16[8,32,128]{2,1,0:T(8,128)(2,1)S(1)}, bf16[8,32,128]{2,1,0:T(8,128)(2,1)S(1)}, u32[]{:S(2)}, u32[]{:S(2)}) %collective-permute-start.59) | collective-permute-done | bytes 65568 | tf_op jit(solution)/shard_map/ppermute | solution.py:114
  154.5 3.7 %collective-permute-start.65 = (bf16[1,4,32,128]{3,2,1,0:T(8,128)(2,1)S(1)}, bf16[1,4,32,128]{3,2,1,0:T(8,128)(2,1)S(1)}, u32[]{:S(2)}, u32[]{:S(2)}) collective-permute-start(bf16[1,4,32,128]{3,2,1,0:T(8,128)(2,1)S(1)} %get-tuple-element.155), channel_id=1, source_target_pairs={{0,24},{4,28},{8,16},{12,20},{16,8},{20,12},{24,0},{28,4},{1,25},{... | collective-permute-start | bytes 98312 | tf_op jit(solution)/shard_map/ppermute | solution.py:114
  160.4 4.4 %collective-permute-done.66.refs_7_ = bf16[1,4,32,128]{3,2,1,0:T(8,128)(2,1)S(1)} collective-permute-done((bf16[1,4,32,128]{3,2,1,0:T(8,128)(2,1)S(1)}, bf16[1,4,32,128]{3,2,1,0:T(8,128)(2,1)S(1)}, u32[]{:S(2)}, u32[]{:S(2)}) %collective-permute-start.66) | collective-permute-done | bytes 32800 | tf_op jit(solution)/shard_map/ppermute | solution.py:114
  164.7 3.7 %model.14 = (f32[8,32,128]{2,1,0:T(8,128)S(1)}, bf16[8,32,128]{2,1,0:T(8,128)(2,1)S(1)}, bf16[8,32,128]{2,1,0:T(8,128)(2,1)S(1)}, bf16[8,32,128]{2,1,0:T(8,128)(2,1)S(1)}, f32[8,32,128]{2,1,0:T(8,128)}) custom-call(s32[92]{0:T(128)S(1)} %fusion.2.slots, s32[92]{0:T(128)S(1)} %copy-done.7, bf16[92,128,128]{2,1,0:T(8,128)(2,1)S(1)} %copy-done.1, ...), custom_call_target="tpu_custom_call" | custom-call | tf_op jit(solution)/shard_map/model/pallas_call | solution.py:173
  170.3 3.0 %collective-permute-done.68.refs_1_ = bf16[8,32,128]{2,1,0:T(8,128)(2,1)S(1)} collective-permute-done((bf16[8,32,128]{2,1,0:T(8,128)(2,1)S(1)}, bf16[8,32,128]{2,1,0:T(8,128)(2,1)S(1)}, u32[]{:S(2)}, u32[]{:S(2)}) %collective-permute-start.68) | collective-permute-done | bytes 65568 | tf_op jit(solution)/shard_map/ppermute | solution.py:114
  174.6 2.9 %collective-permute-start.72 = (bf16[1,1,32,128]{3,2,1,0:T(8,128)(2,1)S(1)}, bf16[1,1,32,128]{3,2,1,0:T(8,128)(2,1)S(1)}, u32[]{:S(2)}, u32[]{:S(2)}) collective-permute-start(bf16[1,1,32,128]{3,2,1,0:T(8,128)(2,1)S(1)} %get-tuple-element.164), channel_id=1, source_target_pairs={{0,12},{4,8},{8,4},{12,0},{16,28},{20,24},{24,20},{28,16},{1,13},{... | collective-permute-start | bytes 24584 | tf_op jit(solution)/shard_map/ppermute | solution.py:114
  177.5 2.9 %collective-permute-start.74 = (bf16[1,1,32,128]{3,2,1,0:T(8,128)(2,1)S(1)}, bf16[1,1,32,128]{3,2,1,0:T(8,128)(2,1)S(1)}, u32[]{:S(2)}, u32[]{:S(2)}) collective-permute-start(bf16[1,1,32,128]{3,2,1,0:T(8,128)(2,1)S(1)} %get-tuple-element.166), channel_id=1, source_target_pairs={{0,20},{4,16},{8,28},{12,24},{16,4},{20,0},{24,12},{28,8},{1,21},{... | collective-permute-start | bytes 24584 | tf_op jit(solution)/shard_map/ppermute | solution.py:114
  180.9 4.3 %collective-permute-start.76 = (bf16[1,1,32,128]{3,2,1,0:T(8,128)(2,1)S(1)}, bf16[1,1,32,128]{3,2,1,0:T(8,128)(2,1)S(1)}, u32[]{:S(2)}, u32[]{:S(2)}) collective-permute-start(bf16[1,1,32,128]{3,2,1,0:T(8,128)(2,1)S(1)} %get-tuple-element.168), channel_id=1, source_target_pairs={{0,28},{4,24},{8,20},{12,16},{16,12},{20,8},{24,4},{28,0},{1,29},{... | collective-permute-start | bytes 24584 | tf_op jit(solution)/shard_map/ppermute | solution.py:114
  (195 shorter events, 83.0 us)
Async XLA Ops:
  3.3 8.9 %collective-permute-start = (bf16[1,4,32,128]{3,2,1,0:T(8,128)(2,1)S(1)}, bf16[1,4,32,128]{3,2,1,0:T(8,128)(2,1)S(1)}, u32[]{:S(2)}, u32[]{:S(2)}) collective-permute-start(bf16[1,4,32,128]{3,2,1,0:T(8,128)(2,1)S(1)} %get-tuple-element.87), channel_id=1, source_target_pairs={{0,4},{4,0},{8,12},{12,8},{16,20},{20,16},{24,28},{28,24},{1,5},{5... | collective-permute-start | bytes 98312 | tf_op jit(solution)/shard_map/ppermute | solution.py:114
  6.3 9.5 %collective-permute-start.1 = (bf16[1,4,32,128]{3,2,1,0:T(8,128)(2,1)S(1)}, bf16[1,4,32,128]{3,2,1,0:T(8,128)(2,1)S(1)}, u32[]{:S(2)}, u32[]{:S(2)}) collective-permute-start(bf16[1,4,32,128]{3,2,1,0:T(8,128)(2,1)S(1)} %get-tuple-element.88), channel_id=1, source_target_pairs={{0,8},{4,12},{8,0},{12,4},{16,24},{20,28},{24,16},{28,20},{1,9},{5... | collective-permute-start | bytes 98312 | tf_op jit(solution)/shard_map/ppermute | solution.py:114
  7.8 8.6 %collective-permute-start.2 = (bf16[1,4,32,128]{3,2,1,0:T(8,128)(2,1)S(1)}, bf16[1,4,32,128]{3,2,1,0:T(8,128)(2,1)S(1)}, u32[]{:S(2)}, u32[]{:S(2)}) collective-permute-start(bf16[1,4,32,128]{3,2,1,0:T(8,128)(2,1)S(1)} %get-tuple-element.89), channel_id=1, source_target_pairs={{0,12},{4,8},{8,4},{12,0},{16,28},{20,24},{24,20},{28,16},{1,13},{... | collective-permute-start | bytes 98312 | tf_op jit(solution)/shard_map/ppermute | solution.py:114
  7.8 8.6 %collective-permute-start.3 = (bf16[1,4,32,128]{3,2,1,0:T(8,128)(2,1)S(1)}, bf16[1,4,32,128]{3,2,1,0:T(8,128)(2,1)S(1)}, u32[]{:S(2)}, u32[]{:S(2)}) collective-permute-start(bf16[1,4,32,128]{3,2,1,0:T(8,128)(2,1)S(1)} %get-tuple-element.90), channel_id=1, source_target_pairs={{0,16},{4,20},{8,24},{12,28},{16,0},{20,4},{24,8},{28,12},{1,17},{... | collective-permute-start | bytes 98312 | tf_op jit(solution)/shard_map/ppermute | solution.py:114
  15.7 6.6 %collective-permute-start.6 = (bf16[1,4,32,128]{3,2,1,0:T(8,128)(2,1)S(1)}, bf16[1,4,32,128]{3,2,1,0:T(8,128)(2,1)S(1)}, u32[]{:S(2)}, u32[]{:S(2)}) collective-permute-start(bf16[1,4,32,128]{3,2,1,0:T(8,128)(2,1)S(1)} %get-tuple-element.93), channel_id=1, source_target_pairs={{0,28},{4,24},{8,20},{12,16},{16,12},{20,8},{24,4},{28,0},{1,29},{... | collective-permute-start | bytes 98312 | tf_op jit(solution)/shard_map/ppermute | solution.py:114
  35.6 10.6 %collective-permute-start.12 = (bf16[1,1,32,128]{3,2,1,0:T(8,128)(2,1)S(1)}, bf16[1,1,32,128]{3,2,1,0:T(8,128)(2,1)S(1)}, u32[]{:S(2)}, u32[]{:S(2)}) collective-permute-start(bf16[1,1,32,128]{3,2,1,0:T(8,128)(2,1)S(1)} %get-tuple-element.101), channel_id=1, source_target_pairs={{0,12},{4,8},{8,4},{12,0},{16,28},{20,24},{24,20},{28,16},{1,13},{... | collective-permute-start | bytes 24584 | tf_op jit(solution)/shard_map/ppermute | solution.py:114
  38.6 7.7 %collective-permute-start.13 = (bf16[1,1,32,128]{3,2,1,0:T(8,128)(2,1)S(1)}, bf16[1,1,32,128]{3,2,1,0:T(8,128)(2,1)S(1)}, u32[]{:S(2)}, u32[]{:S(2)}) collective-permute-start(bf16[1,1,32,128]{3,2,1,0:T(8,128)(2,1)S(1)} %get-tuple-element.102), channel_id=1, source_target_pairs={{0,16},{4,20},{8,24},{12,28},{16,0},{20,4},{24,8},{28,12},{1,17},{... | collective-permute-start | bytes 24584 | tf_op jit(solution)/shard_map/ppermute | solution.py:114
  38.6 7.7 %collective-permute-start.14 = (bf16[1,1,32,128]{3,2,1,0:T(8,128)(2,1)S(1)}, bf16[1,1,32,128]{3,2,1,0:T(8,128)(2,1)S(1)}, u32[]{:S(2)}, u32[]{:S(2)}) collective-permute-start(bf16[1,1,32,128]{3,2,1,0:T(8,128)(2,1)S(1)} %get-tuple-element.103), channel_id=1, source_target_pairs={{0,20},{4,16},{8,28},{12,24},{16,4},{20,0},{24,12},{28,8},{1,21},{... | collective-permute-start | bytes 24584 | tf_op jit(solution)/shard_map/ppermute | solution.py:114
  55.1 7.2 %collective-permute-start.20 = (bf16[1,4,32,128]{3,2,1,0:T(8,128)(2,1)S(1)}, bf16[1,4,32,128]{3,2,1,0:T(8,128)(2,1)S(1)}, u32[]{:S(2)}, u32[]{:S(2)}) collective-permute-start(bf16[1,4,32,128]{3,2,1,0:T(8,128)(2,1)S(1)} %get-tuple-element.108), channel_id=1, source_target_pairs={{0,4},{4,0},{8,12},{12,8},{16,20},{20,16},{24,28},{28,24},{1,5},{5... | collective-permute-start | bytes 98312 | tf_op jit(solution)/shard_map/ppermute | solution.py:114
  56.5 9.4 %collective-permute-start.21 = (bf16[1,4,32,128]{3,2,1,0:T(8,128)(2,1)S(1)}, bf16[1,4,32,128]{3,2,1,0:T(8,128)(2,1)S(1)}, u32[]{:S(2)}, u32[]{:S(2)}) collective-permute-start(bf16[1,4,32,128]{3,2,1,0:T(8,128)(2,1)S(1)} %get-tuple-element.109), channel_id=1, source_target_pairs={{0,8},{4,12},{8,0},{12,4},{16,24},{20,28},{24,16},{28,20},{1,9},{5... | collective-permute-start | bytes 98312 | tf_op jit(solution)/shard_map/ppermute | solution.py:114
  56.5 9.8 %collective-permute-start.22 = (bf16[1,4,32,128]{3,2,1,0:T(8,128)(2,1)S(1)}, bf16[1,4,32,128]{3,2,1,0:T(8,128)(2,1)S(1)}, u32[]{:S(2)}, u32[]{:S(2)}) collective-permute-start(bf16[1,4,32,128]{3,2,1,0:T(8,128)(2,1)S(1)} %get-tuple-element.110), channel_id=1, source_target_pairs={{0,12},{4,8},{8,4},{12,0},{16,28},{20,24},{24,20},{28,16},{1,13},{... | collective-permute-start | bytes 98312 | tf_op jit(solution)/shard_map/ppermute | solution.py:114
  58.7 7.7 %collective-permute-start.23 = (bf16[1,4,32,128]{3,2,1,0:T(8,128)(2,1)S(1)}, bf16[1,4,32,128]{3,2,1,0:T(8,128)(2,1)S(1)}, u32[]{:S(2)}, u32[]{:S(2)}) collective-permute-start(bf16[1,4,32,128]{3,2,1,0:T(8,128)(2,1)S(1)} %get-tuple-element.111), channel_id=1, source_target_pairs={{0,16},{4,20},{8,24},{12,28},{16,0},{20,4},{24,8},{28,12},{1,17},{... | collective-permute-start | bytes 98312 | tf_op jit(solution)/shard_map/ppermute | solution.py:114
  65.9 6.6 %collective-permute-start.26 = (bf16[1,4,32,128]{3,2,1,0:T(8,128)(2,1)S(1)}, bf16[1,4,32,128]{3,2,1,0:T(8,128)(2,1)S(1)}, u32[]{:S(2)}, u32[]{:S(2)}) collective-permute-start(bf16[1,4,32,128]{3,2,1,0:T(8,128)(2,1)S(1)} %get-tuple-element.114), channel_id=1, source_target_pairs={{0,28},{4,24},{8,20},{12,16},{16,12},{20,8},{24,4},{28,0},{1,29},{... | collective-permute-start | bytes 98312 | tf_op jit(solution)/shard_map/ppermute | solution.py:114
  82.4 10.6 %collective-permute-start.32 = (bf16[1,1,32,128]{3,2,1,0:T(8,128)(2,1)S(1)}, bf16[1,1,32,128]{3,2,1,0:T(8,128)(2,1)S(1)}, u32[]{:S(2)}, u32[]{:S(2)}) collective-permute-start(bf16[1,1,32,128]{3,2,1,0:T(8,128)(2,1)S(1)} %get-tuple-element.122), channel_id=1, source_target_pairs={{0,12},{4,8},{8,4},{12,0},{16,28},{20,24},{24,20},{28,16},{1,13},{... | collective-permute-start | bytes 24584 | tf_op jit(solution)/shard_map/ppermute | solution.py:114
  85.4 7.7 %collective-permute-start.33 = (bf16[1,1,32,128]{3,2,1,0:T(8,128)(2,1)S(1)}, bf16[1,1,32,128]{3,2,1,0:T(8,128)(2,1)S(1)}, u32[]{:S(2)}, u32[]{:S(2)}) collective-permute-start(bf16[1,1,32,128]{3,2,1,0:T(8,128)(2,1)S(1)} %get-tuple-element.123), channel_id=1, source_target_pairs={{0,16},{4,20},{8,24},{12,28},{16,0},{20,4},{24,8},{28,12},{1,17},{... | collective-permute-start | bytes 24584 | tf_op jit(solution)/shard_map/ppermute | solution.py:114
  85.4 7.7 %collective-permute-start.34 = (bf16[1,1,32,128]{3,2,1,0:T(8,128)(2,1)S(1)}, bf16[1,1,32,128]{3,2,1,0:T(8,128)(2,1)S(1)}, u32[]{:S(2)}, u32[]{:S(2)}) collective-permute-start(bf16[1,1,32,128]{3,2,1,0:T(8,128)(2,1)S(1)} %get-tuple-element.124), channel_id=1, source_target_pairs={{0,20},{4,16},{8,28},{12,24},{16,4},{20,0},{24,12},{28,8},{1,21},{... | collective-permute-start | bytes 24584 | tf_op jit(solution)/shard_map/ppermute | solution.py:114
  101.0 7.2 %collective-permute-start.40 = (bf16[1,4,32,128]{3,2,1,0:T(8,128)(2,1)S(1)}, bf16[1,4,32,128]{3,2,1,0:T(8,128)(2,1)S(1)}, u32[]{:S(2)}, u32[]{:S(2)}) collective-permute-start(bf16[1,4,32,128]{3,2,1,0:T(8,128)(2,1)S(1)} %get-tuple-element.129), channel_id=1, source_target_pairs={{0,4},{4,0},{8,12},{12,8},{16,20},{20,16},{24,28},{28,24},{1,5},{5... | collective-permute-start | bytes 98312 | tf_op jit(solution)/shard_map/ppermute | solution.py:114
  102.3 9.5 %collective-permute-start.41 = (bf16[1,4,32,128]{3,2,1,0:T(8,128)(2,1)S(1)}, bf16[1,4,32,128]{3,2,1,0:T(8,128)(2,1)S(1)}, u32[]{:S(2)}, u32[]{:S(2)}) collective-permute-start(bf16[1,4,32,128]{3,2,1,0:T(8,128)(2,1)S(1)} %get-tuple-element.130), channel_id=1, source_target_pairs={{0,8},{4,12},{8,0},{12,4},{16,24},{20,28},{24,16},{28,20},{1,9},{5... | collective-permute-start | bytes 98312 | tf_op jit(solution)/shard_map/ppermute | solution.py:114
  102.3 9.8 %collective-permute-start.42 = (bf16[1,4,32,128]{3,2,1,0:T(8,128)(2,1)S(1)}, bf16[1,4,32,128]{3,2,1,0:T(8,128)(2,1)S(1)}, u32[]{:S(2)}, u32[]{:S(2)}) collective-permute-start(bf16[1,4,32,128]{3,2,1,0:T(8,128)(2,1)S(1)} %get-tuple-element.131), channel_id=1, source_target_pairs={{0,12},{4,8},{8,4},{12,0},{16,28},{20,24},{24,20},{28,16},{1,13},{... | collective-permute-start | bytes 98312 | tf_op jit(solution)/shard_map/ppermute | solution.py:114
  104.5 7.7 %collective-permute-start.43 = (bf16[1,4,32,128]{3,2,1,0:T(8,128)(2,1)S(1)}, bf16[1,4,32,128]{3,2,1,0:T(8,128)(2,1)S(1)}, u32[]{:S(2)}, u32[]{:S(2)}) collective-permute-start(bf16[1,4,32,128]{3,2,1,0:T(8,128)(2,1)S(1)} %get-tuple-element.132), channel_id=1, source_target_pairs={{0,16},{4,20},{8,24},{12,28},{16,0},{20,4},{24,8},{28,12},{1,17},{... | collective-permute-start | bytes 98312 | tf_op jit(solution)/shard_map/ppermute | solution.py:114
  111.8 6.6 %collective-permute-start.46 = (bf16[1,4,32,128]{3,2,1,0:T(8,128)(2,1)S(1)}, bf16[1,4,32,128]{3,2,1,0:T(8,128)(2,1)S(1)}, u32[]{:S(2)}, u32[]{:S(2)}) collective-permute-start(bf16[1,4,32,128]{3,2,1,0:T(8,128)(2,1)S(1)} %get-tuple-element.135), channel_id=1, source_target_pairs={{0,28},{4,24},{8,20},{12,16},{16,12},{20,8},{24,4},{28,0},{1,29},{... | collective-permute-start | bytes 98312 | tf_op jit(solution)/shard_map/ppermute | solution.py:114
  128.4 10.6 %collective-permute-start.52 = (bf16[1,1,32,128]{3,2,1,0:T(8,128)(2,1)S(1)}, bf16[1,1,32,128]{3,2,1,0:T(8,128)(2,1)S(1)}, u32[]{:S(2)}, u32[]{:S(2)}) collective-permute-start(bf16[1,1,32,128]{3,2,1,0:T(8,128)(2,1)S(1)} %get-tuple-element.143), channel_id=1, source_target_pairs={{0,12},{4,8},{8,4},{12,0},{16,28},{20,24},{24,20},{28,16},{1,13},{... | collective-permute-start | bytes 24584 | tf_op jit(solution)/shard_map/ppermute | solution.py:114
  131.3 7.7 %collective-permute-start.53 = (bf16[1,1,32,128]{3,2,1,0:T(8,128)(2,1)S(1)}, bf16[1,1,32,128]{3,2,1,0:T(8,128)(2,1)S(1)}, u32[]{:S(2)}, u32[]{:S(2)}) collective-permute-start(bf16[1,1,32,128]{3,2,1,0:T(8,128)(2,1)S(1)} %get-tuple-element.144), channel_id=1, source_target_pairs={{0,16},{4,20},{8,24},{12,28},{16,0},{20,4},{24,8},{28,12},{1,17},{... | collective-permute-start | bytes 24584 | tf_op jit(solution)/shard_map/ppermute | solution.py:114
  131.3 7.7 %collective-permute-start.54 = (bf16[1,1,32,128]{3,2,1,0:T(8,128)(2,1)S(1)}, bf16[1,1,32,128]{3,2,1,0:T(8,128)(2,1)S(1)}, u32[]{:S(2)}, u32[]{:S(2)}) collective-permute-start(bf16[1,1,32,128]{3,2,1,0:T(8,128)(2,1)S(1)} %get-tuple-element.145), channel_id=1, source_target_pairs={{0,20},{4,16},{8,28},{12,24},{16,4},{20,0},{24,12},{28,8},{1,21},{... | collective-permute-start | bytes 24584 | tf_op jit(solution)/shard_map/ppermute | solution.py:114
  147.3 7.2 %collective-permute-start.60 = (bf16[1,4,32,128]{3,2,1,0:T(8,128)(2,1)S(1)}, bf16[1,4,32,128]{3,2,1,0:T(8,128)(2,1)S(1)}, u32[]{:S(2)}, u32[]{:S(2)}) collective-permute-start(bf16[1,4,32,128]{3,2,1,0:T(8,128)(2,1)S(1)} %get-tuple-element.150), channel_id=1, source_target_pairs={{0,4},{4,0},{8,12},{12,8},{16,20},{20,16},{24,28},{28,24},{1,5},{5... | collective-permute-start | bytes 98312 | tf_op jit(solution)/shard_map/ppermute | solution.py:114
  148.6 9.5 %collective-permute-start.61 = (bf16[1,4,32,128]{3,2,1,0:T(8,128)(2,1)S(1)}, bf16[1,4,32,128]{3,2,1,0:T(8,128)(2,1)S(1)}, u32[]{:S(2)}, u32[]{:S(2)}) collective-permute-start(bf16[1,4,32,128]{3,2,1,0:T(8,128)(2,1)S(1)} %get-tuple-element.151), channel_id=1, source_target_pairs={{0,8},{4,12},{8,0},{12,4},{16,24},{20,28},{24,16},{28,20},{1,9},{5... | collective-permute-start | bytes 98312 | tf_op jit(solution)/shard_map/ppermute | solution.py:114
  148.6 9.9 %collective-permute-start.62 = (bf16[1,4,32,128]{3,2,1,0:T(8,128)(2,1)S(1)}, bf16[1,4,32,128]{3,2,1,0:T(8,128)(2,1)S(1)}, u32[]{:S(2)}, u32[]{:S(2)}) collective-permute-start(bf16[1,4,32,128]{3,2,1,0:T(8,128)(2,1)S(1)} %get-tuple-element.152), channel_id=1, source_target_pairs={{0,12},{4,8},{8,4},{12,0},{16,28},{20,24},{24,20},{28,16},{1,13},{... | collective-permute-start | bytes 98312 | tf_op jit(solution)/shard_map/ppermute | solution.py:114
  150.9 7.7 %collective-permute-start.63 = (bf16[1,4,32,128]{3,2,1,0:T(8,128)(2,1)S(1)}, bf16[1,4,32,128]{3,2,1,0:T(8,128)(2,1)S(1)}, u32[]{:S(2)}, u32[]{:S(2)}) collective-permute-start(bf16[1,4,32,128]{3,2,1,0:T(8,128)(2,1)S(1)} %get-tuple-element.153), channel_id=1, source_target_pairs={{0,16},{4,20},{8,24},{12,28},{16,0},{20,4},{24,8},{28,12},{1,17},{... | collective-permute-start | bytes 98312 | tf_op jit(solution)/shard_map/ppermute | solution.py:114
  158.1 6.6 %collective-permute-start.66 = (bf16[1,4,32,128]{3,2,1,0:T(8,128)(2,1)S(1)}, bf16[1,4,32,128]{3,2,1,0:T(8,128)(2,1)S(1)}, u32[]{:S(2)}, u32[]{:S(2)}) collective-permute-start(bf16[1,4,32,128]{3,2,1,0:T(8,128)(2,1)S(1)} %get-tuple-element.156), channel_id=1, source_target_pairs={{0,28},{4,24},{8,20},{12,16},{16,12},{20,8},{24,4},{28,0},{1,29},{... | collective-permute-start | bytes 98312 | tf_op jit(solution)/shard_map/ppermute | solution.py:114
  174.6 10.6 %collective-permute-start.72 = (bf16[1,1,32,128]{3,2,1,0:T(8,128)(2,1)S(1)}, bf16[1,1,32,128]{3,2,1,0:T(8,128)(2,1)S(1)}, u32[]{:S(2)}, u32[]{:S(2)}) collective-permute-start(bf16[1,1,32,128]{3,2,1,0:T(8,128)(2,1)S(1)} %get-tuple-element.164), channel_id=1, source_target_pairs={{0,12},{4,8},{8,4},{12,0},{16,28},{20,24},{24,20},{28,16},{1,13},{... | collective-permute-start | bytes 24584 | tf_op jit(solution)/shard_map/ppermute | solution.py:114
  177.5 7.7 %collective-permute-start.73 = (bf16[1,1,32,128]{3,2,1,0:T(8,128)(2,1)S(1)}, bf16[1,1,32,128]{3,2,1,0:T(8,128)(2,1)S(1)}, u32[]{:S(2)}, u32[]{:S(2)}) collective-permute-start(bf16[1,1,32,128]{3,2,1,0:T(8,128)(2,1)S(1)} %get-tuple-element.165), channel_id=1, source_target_pairs={{0,16},{4,20},{8,24},{12,28},{16,0},{20,4},{24,8},{28,12},{1,17},{... | collective-permute-start | bytes 24584 | tf_op jit(solution)/shard_map/ppermute | solution.py:114
  177.5 7.7 %collective-permute-start.74 = (bf16[1,1,32,128]{3,2,1,0:T(8,128)(2,1)S(1)}, bf16[1,1,32,128]{3,2,1,0:T(8,128)(2,1)S(1)}, u32[]{:S(2)}, u32[]{:S(2)}) collective-permute-start(bf16[1,1,32,128]{3,2,1,0:T(8,128)(2,1)S(1)} %get-tuple-element.166), channel_id=1, source_target_pairs={{0,20},{4,16},{8,28},{12,24},{16,4},{20,0},{24,12},{28,8},{1,21},{... | collective-permute-start | bytes 24584 | tf_op jit(solution)/shard_map/ppermute | solution.py:114
  (57 other events, 517.0 us)

commit v2 on v1

v2 whole, which is shorter than its diff:
```python
import functools

import jax
import jax.numpy as jnp
from jax import lax
from jax.experimental import pallas as pl
from jax.experimental.pallas import tpu as pltpu
from jax.sharding import PartitionSpec as P

ITERATIONS = 4


VMEM = pl.BlockSpec(memory_space=pltpu.VMEM)
SMEM = pl.BlockSpec(memory_space=pltpu.SMEM)
PARAMS = pltpu.CompilerParams(vmem_limit_bytes=32 * 1024 * 1024)


def stages_of(count):
    stages, radix, stride = [], 2, 1
    while stride < count:
        radix = min(radix, count // stride)
        stages.insert(0, (radix, stride))
        stride, radix = stride * radix, radix * 2
    rest = stages[0][1]
    where = {e: divmod(e, rest) for e in range(count)}
    moves, arrays = [], stages[0][0]
    for radix, stride in stages[1:]:
        for digit in range(1, radix):
            chosen = [e for e in range(count) if e // stride % radix == digit]
            moves.append((digit * stride, [where[e] for e in chosen]))
            where.update({e: (arrays, i) for i, e in enumerate(chosen)})
            arrays += 1
    return stages[0], moves, where


def model_kernel(where, chan_count, per, slots, rows, model, measured, *refs):
    pieces = 1 + max(array for array, _ in where.values())
    arrived = refs[:pieces]
    own, *sent = refs[pieces : pieces + chan_count]
    residual, tiles, narrow, sums = refs[pieces + chan_count :]
    wide = len(where) * per
    for e, (array, i) in where.items():
        for d in range(chan_count):
            place = d * wide + e * per
            tiles[place : place + per] = arrived[array][i, d * per : (d + 1) * per]
    residual[...] = measured[...]
    sums[...] = jnp.zeros_like(sums)
    count = model.shape[0]
    for k in range(count):
        part = lax.dot_general(
            tiles[slots[k]],
            model[k],
            (((1,), (1,)), ((), ())),
            preferred_element_type=jnp.float32,
        )
        residual[rows[k]] -= part
    narrow[...] = residual[...].astype(jnp.bfloat16)
    for k in range(count):
        part = jnp.dot(narrow[rows[k]], model[k], preferred_element_type=jnp.float32)
        sums[slots[k]] += part
    own[...] = sums[:wide]
    for d, out in enumerate(sent, 1):
        out[...] = sums[d * wide : (d + 1) * wide].astype(jnp.bfloat16)


def reduce_kernel(vox_count, chan_count, per, rest, own, *refs):
    received, outs = refs[: chan_count - 1], refs[chan_count - 1 :]
    total = own[...]
    for piece in received:
        total = total + piece[...].astype(jnp.float32)
    total = total.astype(jnp.bfloat16)
    for e in range(vox_count):
        outs[e // rest][e % rest] = total[e * per : (e + 1) * per]


def place_of(ids, table, per, d, e, p):
    return jnp.maximum(table[ids[0] ^ e, (ids[1] ^ d) * per + p], 0)


def pick_kernel(vox_count, chan_count, per, rest, ids, table, image, *outs):
    for e in range(vox_count):
        for d in range(chan_count):
            for p in range(per):
                tile = place_of(ids, table, per, d, e, p)
                outs[e // rest][e % rest, d * per + p] = image[tile].astype(jnp.bfloat16)


def update_kernel(vox_count, chan_count, per, rest, ids, table, gains, image, *refs):
    received = refs[:chan_count]
    estimate, *outs = refs[chan_count:-1]
    gradient = refs[-1]
    gradient[...] = jnp.zeros_like(gradient)
    for d in range(chan_count):
        for e in range(vox_count):
            for p in range(per):
                tile = place_of(ids, table, per, d, e, p)
                gradient[tile] += received[d][e * per + p].astype(jnp.float32)
    estimate[...] = jnp.maximum(image[...] + gains[...][None] * gradient[...], 0.0)
    if outs:
        pick_kernel(vox_count, chan_count, per, rest, ids, table, estimate, *outs)


def shards(model_blocks, start_image, measured, step_size, sent_tiles, block_rows, block_slots):
    vox_count = lax.axis_size("vox")
    chan_count = lax.axis_size("chan")
    vox, chan = lax.axis_index("vox"), lax.axis_index("chan")
    table = sent_tiles[0]
    capacity = table.shape[1]
    per = capacity // chan_count
    tile_count, wave_count, width = start_image.shape
    row_count = measured.shape[0]
    slot_count = vox_count * capacity
    wide = vox_count * per
    (first, rest), moves, where = stages_of(vox_count)
    tile = (wave_count, width)
    ids = jnp.stack([vox, chan]).astype(jnp.int32)
    slab, slot = block_slots // capacity, block_slots % capacity
    places = (((slot // per) ^ chan) * vox_count + (slab ^ vox)) * per + slot % per
    gains = jnp.broadcast_to(step_size[:, None], tile)

    def shape(count, dtype):
        return jax.ShapeDtypeStruct((count, *tile), dtype)

    def group(count):
        return [jax.ShapeDtypeStruct((rest, count, *tile), jnp.bfloat16)] * first

    def swap(array, axis, size, step):
        if step == 0:
            return array
        return lax.ppermute(array, axis, [(i, i ^ step) for i in range(size)])

    def exchange(pieces):
        pieces = [swap(piece, "vox", vox_count, h * rest) for h, piece in enumerate(pieces)]
        for step, chosen in moves:
            moved = jnp.stack([pieces[array][i] for array, i in chosen])
            pieces.append(swap(moved, "vox", vox_count, step))
        return pieces

    apply_model = pl.pallas_call(
        functools.partial(model_kernel, where, chan_count, per),
        out_shape=(
            shape(wide, jnp.float32),
            *[shape(wide, jnp.bfloat16)] * (chan_count - 1),
            shape(row_count, jnp.float32),
        ),
        in_specs=[SMEM, SMEM, VMEM, VMEM] + [VMEM] * (first + len(moves)),
        out_specs=[VMEM] * (chan_count + 1),
        scratch_shapes=[
            pltpu.VMEM((slot_count, *tile), jnp.bfloat16),
            pltpu.VMEM((row_count, *tile), jnp.bfloat16),
            pltpu.VMEM((slot_count, *tile), jnp.float32),
        ],
        compiler_params=PARAMS,
        name="model",
    )
    reduce_parts = pl.pallas_call(
        functools.partial(reduce_kernel, vox_count, chan_count, per, rest),
        out_shape=group(per),
        in_specs=[VMEM] * chan_count,
        out_specs=[VMEM] * first,
        compiler_params=PARAMS,
        name="reduce",
    )
    pick = pl.pallas_call(
        functools.partial(pick_kernel, vox_count, chan_count, per, rest),
        out_shape=group(capacity),
        in_specs=[SMEM, SMEM, VMEM],
        out_specs=[VMEM] * first,
        compiler_params=PARAMS,
        name="pick",
    )

    def update(last):
        outs = [] if last else group(capacity)
        return pl.pallas_call(
            functools.partial(update_kernel, vox_count, chan_count, per, rest),
            out_shape=[shape(tile_count, jnp.float32)] + outs,
            in_specs=[SMEM, SMEM, VMEM, VMEM] + [VMEM] * chan_count,
            out_specs=[VMEM] * (len(outs) + 1),
            scratch_shapes=[pltpu.VMEM((tile_count, *tile), jnp.float32)],
            compiler_params=PARAMS,
            name="update",
        )

    estimate = start_image
    outgoing = pick(ids, table, start_image)
    for iteration in range(ITERATIONS):
        own, *partial, residual = apply_model(
            places, block_rows, model_blocks, measured, *exchange(outgoing)
        )
        received = [swap(piece, "chan", chan_count, d) for d, piece in enumerate(partial, 1)]
        totals = reduce_parts(own, *received)
        pieces = exchange(totals)
        returned = jnp.concatenate([pieces[array][i] for array, i in where.values()])
        spread = [swap(returned, "chan", chan_count, d) for d in range(chan_count)]
        estimate, *outgoing = update(iteration == ITERATIONS - 1)(
            ids, table, gains, estimate, *spread
        )
    return (estimate, residual)


def solution(mesh):
    in_specs = (
        P(("vox", "chan"), None, None),
        P("vox", None, None),
        P(("vox", "chan"), None, None),
        P(),
        P("vox", None, None),
        P(("vox", "chan")),
        P(("vox", "chan")),
    )
    out_specs = (P("vox", None, None), P(("vox", "chan"), None, None))
    return jax.shard_map(shards, mesh=mesh, in_specs=in_specs, out_specs=out_specs, check_vma=False)
```

time: 194 us -> 177 us (0.912)
  starting transfers between devices: 106 us -> 64.5 us
  waiting for transfers between devices: 60.7 us -> 84.3 us
    ppermute x80 -> x56, starting transfers between devices: 106 us -> 64.5 us  [swap(): return lax.ppermute(array, axis, [(i, i ^ step) for i in range(size)])]
    ppermute x80 -> x56, waiting for transfers between devices: 60.7 us -> 84.3 us  [swap(): return lax.ppermute(array, axis, [(i, i ^ step) for i in range(size)])]
  transfers between devices with their start and end apart: 80 -> 56, of which waited for: 36 -> 43; matrix products, arithmetic and copies ran while one was open for 0% -> 0% of each run, Pallas kernels for 0% -> 0%
where the time goes in v2:
time: 177 us; the launch traced here: 176 us
  waiting for transfers between devices  84.3 us (48%)
  starting transfers between devices  64.5 us (36%)
  Pallas kernels  20.2 us (11%)
  local copies, waits for them, and re-layouts  5.59 us (3%)
    ppermute x56, waiting for transfers between devices, swap(): return lax.ppermute(array, axis, [(i, i ^ step) for i in range(size)])  84.3 us
    ppermute x56, starting transfers between devices, swap(): return lax.ppermute(array, axis, [(i, i ^ step) for i in range(size)])  64.5 us
    pallas_call x4, Pallas kernels, shards(): apply_model(places, block_rows, model_blocks, measured, *exchange(outgoing))  14.7 us
    pallas_call x4, Pallas kernels, shards(): update(iteration == ITERATIONS - 1)(ids, table, gains, estimate, *spread)  4.67 us
    unnamed x46, local copies, waits for them, and re-layouts  4.65 us
  transfers between devices with their start and end apart: 56, of which 43 were waited for; matrix products, arithmetic and copies ran while one was open for 0% of the time, Pallas kernels for 0%

profile of v2, /device:TPU:0, one launch (start us, length us, event | category | flops | bytes accessed | tf_op | source)
XLA Modules:
  0.0 176.3 jit_solution(16842388485360408160)
XLA Ops:
  3.2 3.1 %collective-permute-start = (bf16[2,4,32,128]{3,2,1,0:T(8,128)(2,1)S(1)}, bf16[2,4,32,128]{3,2,1,0:T(8,128)(2,1)S(1)}, u32[]{:S(2)}, u32[]{:S(2)}) collective-permute-start(bf16[2,4,32,128]{3,2,1,0:T(8,128)(2,1)S(1)} %get-tuple-element.55), channel_id=1, source_target_pairs={{0,8},{4,12},{8,0},{12,4},{16,24},{20,28},{24,16},{28,20},{1,9},{5... | collective-permute-start | bytes 196616 | tf_op jit(solution)/shard_map/ppermute | solution.py:130
  6.3 2.6 %collective-permute-start.1 = (bf16[2,4,32,128]{3,2,1,0:T(8,128)(2,1)S(1)}, bf16[2,4,32,128]{3,2,1,0:T(8,128)(2,1)S(1)}, u32[]{:S(2)}, u32[]{:S(2)}) collective-permute-start(bf16[2,4,32,128]{3,2,1,0:T(8,128)(2,1)S(1)} %get-tuple-element.56), channel_id=1, source_target_pairs={{0,16},{4,20},{8,24},{12,28},{16,0},{20,4},{24,8},{28,12},{1,17},{... | collective-permute-start | bytes 196616 | tf_op jit(solution)/shard_map/ppermute | solution.py:130
  8.9 4.6 %collective-permute-done.1.refs_2_ = bf16[2,4,32,128]{3,2,1,0:T(8,128)(2,1)S(1)} collective-permute-done((bf16[2,4,32,128]{3,2,1,0:T(8,128)(2,1)S(1)}, bf16[2,4,32,128]{3,2,1,0:T(8,128)(2,1)S(1)}, u32[]{:S(2)}, u32[]{:S(2)}) %collective-permute-start.1) | collective-permute-done | bytes 65568 | tf_op jit(solution)/shard_map/ppermute | solution.py:130
  17.2 2.8 %collective-permute-done.3.refs_4_ = bf16[4,4,32,128]{3,2,1,0:T(8,128)(2,1)S(1)} collective-permute-done((bf16[4,4,32,128]{3,2,1,0:T(8,128)(2,1)S(1)}, bf16[4,4,32,128]{3,2,1,0:T(8,128)(2,1)S(1)}, u32[]{:S(2)}, u32[]{:S(2)}) %collective-permute-start.3) | collective-permute-done | bytes 131104 | tf_op jit(solution)/shard_map/ppermute | solution.py:130
  23.4 3.7 %model.8 = (f32[8,32,128]{2,1,0:T(8,128)S(1)}, bf16[8,32,128]{2,1,0:T(8,128)(2,1)S(1)}, bf16[8,32,128]{2,1,0:T(8,128)(2,1)S(1)}, bf16[8,32,128]{2,1,0:T(8,128)(2,1)S(1)}, f32[8,32,128]{2,1,0:T(8,128)}) custom-call(s32[92]{0:T(128)S(1)} %fusion.2.slots, s32[92]{0:T(128)S(1)} %copy-done.6, bf16[92,128,128]{2,1,0:T(8,128)(2,1)S(1)} %copy-done, ...), custom_call_target="tpu_custom_call" | custom-call | tf_op jit(solution)/shard_map/model/pallas_call | solution.py:188
  29.0 2.6 %collective-permute-done.5.refs_1_ = bf16[8,32,128]{2,1,0:T(8,128)(2,1)S(1)} collective-permute-done((bf16[8,32,128]{2,1,0:T(8,128)(2,1)S(1)}, bf16[8,32,128]{2,1,0:T(8,128)(2,1)S(1)}, u32[]{:S(2)}, u32[]{:S(2)}) %collective-permute-start.5) | collective-permute-done | bytes 65568 | tf_op jit(solution)/shard_map/ppermute | solution.py:130
  32.8 2.3 %collective-permute-start.8 = (bf16[2,1,32,128]{3,2,1,0:T(8,128)(2,1)S(1)}, bf16[2,1,32,128]{3,2,1,0:T(8,128)(2,1)S(1)}, u32[]{:S(2)}, u32[]{:S(2)}) collective-permute-start(bf16[2,1,32,128]{3,2,1,0:T(8,128)(2,1)S(1)} %get-tuple-element.64), channel_id=1, source_target_pairs={{0,16},{4,20},{8,24},{12,28},{16,0},{20,4},{24,8},{28,12},{1,17},{... | collective-permute-start | bytes 49160 | tf_op jit(solution)/shard_map/ppermute | solution.py:130
  37.5 3.2 %collective-permute-done.9 = bf16[2,1,32,128]{3,2,1,0:T(8,128)(2,1)S(1)} collective-permute-done((bf16[2,1,32,128]{3,2,1,0:T(8,128)(2,1)S(1)}, bf16[2,1,32,128]{3,2,1,0:T(8,128)(2,1)S(1)}, u32[]{:S(2)}, u32[]{:S(2)}) %collective-permute-start.9) | collective-permute-done | bytes 16416 | tf_op jit(solution)/shard_map/ppermute | solution.py:130
  42.3 2.4 %collective-permute-done.10 = bf16[4,1,32,128]{3,2,1,0:T(8,128)(2,1)S(1)} collective-permute-done((bf16[4,1,32,128]{3,2,1,0:T(8,128)(2,1)S(1)}, bf16[4,1,32,128]{3,2,1,0:T(8,128)(2,1)S(1)}, u32[]{:S(2)}, u32[]{:S(2)}) %collective-permute-start.10) | collective-permute-done | bytes 32800 | tf_op jit(solution)/shard_map/ppermute | solution.py:130
  46.7 2.5 %collective-permute-done.13.refs_3_ = bf16[8,32,128]{2,1,0:T(8,128)(2,1)S(1)} collective-permute-done((bf16[8,32,128]{2,1,0:T(8,128)(2,1)S(1)}, bf16[8,32,128]{2,1,0:T(8,128)(2,1)S(1)}, u32[]{:S(2)}, u32[]{:S(2)}) %collective-permute-start.13) | collective-permute-done | bytes 65568 | tf_op jit(solution)/shard_map/ppermute | solution.py:130
  51.8 2.6 %collective-permute-start.15 = (bf16[2,4,32,128]{3,2,1,0:T(8,128)(2,1)S(1)}, bf16[2,4,32,128]{3,2,1,0:T(8,128)(2,1)S(1)}, u32[]{:S(2)}, u32[]{:S(2)}) collective-permute-start(bf16[2,4,32,128]{3,2,1,0:T(8,128)(2,1)S(1)} %get-tuple-element.69), channel_id=1, source_target_pairs={{0,16},{4,20},{8,24},{12,28},{16,0},{20,4},{24,8},{28,12},{1,17},{... | collective-permute-start | bytes 196616 | tf_op jit(solution)/shard_map/ppermute | solution.py:130
  56.9 2.9 %collective-permute-done.15.refs_2_ = bf16[2,4,32,128]{3,2,1,0:T(8,128)(2,1)S(1)} collective-permute-done((bf16[2,4,32,128]{3,2,1,0:T(8,128)(2,1)S(1)}, bf16[2,4,32,128]{3,2,1,0:T(8,128)(2,1)S(1)}, u32[]{:S(2)}, u32[]{:S(2)}) %collective-permute-start.15) | collective-permute-done | bytes 65568 | tf_op jit(solution)/shard_map/ppermute | solution.py:130
  62.1 3.5 %collective-permute-done.17.refs_4_ = bf16[4,4,32,128]{3,2,1,0:T(8,128)(2,1)S(1)} collective-permute-done((bf16[4,4,32,128]{3,2,1,0:T(8,128)(2,1)S(1)}, bf16[4,4,32,128]{3,2,1,0:T(8,128)(2,1)S(1)}, u32[]{:S(2)}, u32[]{:S(2)}) %collective-permute-start.17) | collective-permute-done | bytes 131104 | tf_op jit(solution)/shard_map/ppermute | solution.py:130
  65.6 3.7 %model.10 = (f32[8,32,128]{2,1,0:T(8,128)S(1)}, bf16[8,32,128]{2,1,0:T(8,128)(2,1)S(1)}, bf16[8,32,128]{2,1,0:T(8,128)(2,1)S(1)}, bf16[8,32,128]{2,1,0:T(8,128)(2,1)S(1)}, f32[8,32,128]{2,1,0:T(8,128)}) custom-call(s32[92]{0:T(128)S(1)} %fusion.2.slots, s32[92]{0:T(128)S(1)} %copy-done.7, bf16[92,128,128]{2,1,0:T(8,128)(2,1)S(1)} %copy-done.1, ...), custom_call_target="tpu_custom_call" | custom-call | tf_op jit(solution)/shard_map/model/pallas_call | solution.py:188
  71.1 3.0 %collective-permute-done.19.refs_1_ = bf16[8,32,128]{2,1,0:T(8,128)(2,1)S(1)} collective-permute-done((bf16[8,32,128]{2,1,0:T(8,128)(2,1)S(1)}, bf16[8,32,128]{2,1,0:T(8,128)(2,1)S(1)}, u32[]{:S(2)}, u32[]{:S(2)}) %collective-permute-start.19) | collective-permute-done | bytes 65568 | tf_op jit(solution)/shard_map/ppermute | solution.py:130
  80.7 2.1 %collective-permute-done.23 = bf16[2,1,32,128]{3,2,1,0:T(8,128)(2,1)S(1)} collective-permute-done((bf16[2,1,32,128]{3,2,1,0:T(8,128)(2,1)S(1)}, bf16[2,1,32,128]{3,2,1,0:T(8,128)(2,1)S(1)}, u32[]{:S(2)}, u32[]{:S(2)}) %collective-permute-start.23) | collective-permute-done | bytes 16416 | tf_op jit(solution)/shard_map/ppermute | solution.py:130
  84.4 2.4 %collective-permute-done.24 = bf16[4,1,32,128]{3,2,1,0:T(8,128)(2,1)S(1)} collective-permute-done((bf16[4,1,32,128]{3,2,1,0:T(8,128)(2,1)S(1)}, bf16[4,1,32,128]{3,2,1,0:T(8,128)(2,1)S(1)}, u32[]{:S(2)}, u32[]{:S(2)}) %collective-permute-start.24) | collective-permute-done | bytes 32800 | tf_op jit(solution)/shard_map/ppermute | solution.py:130
  93.0 2.5 %collective-permute-start.29 = (bf16[2,4,32,128]{3,2,1,0:T(8,128)(2,1)S(1)}, bf16[2,4,32,128]{3,2,1,0:T(8,128)(2,1)S(1)}, u32[]{:S(2)}, u32[]{:S(2)}) collective-permute-start(bf16[2,4,32,128]{3,2,1,0:T(8,128)(2,1)S(1)} %get-tuple-element.82), channel_id=1, source_target_pairs={{0,16},{4,20},{8,24},{12,28},{16,0},{20,4},{24,8},{28,12},{1,17},{... | collective-permute-start | bytes 196616 | tf_op jit(solution)/shard_map/ppermute | solution.py:130
  98.1 2.8 %collective-permute-done.29.refs_2_ = bf16[2,4,32,128]{3,2,1,0:T(8,128)(2,1)S(1)} collective-permute-done((bf16[2,4,32,128]{3,2,1,0:T(8,128)(2,1)S(1)}, bf16[2,4,32,128]{3,2,1,0:T(8,128)(2,1)S(1)}, u32[]{:S(2)}, u32[]{:S(2)}) %collective-permute-start.29) | collective-permute-done | bytes 65568 | tf_op jit(solution)/shard_map/ppermute | solution.py:130
  103.3 3.5 %collective-permute-done.31.refs_4_ = bf16[4,4,32,128]{3,2,1,0:T(8,128)(2,1)S(1)} collective-permute-done((bf16[4,4,32,128]{3,2,1,0:T(8,128)(2,1)S(1)}, bf16[4,4,32,128]{3,2,1,0:T(8,128)(2,1)S(1)}, u32[]{:S(2)}, u32[]{:S(2)}) %collective-permute-start.31) | collective-permute-done | bytes 131104 | tf_op jit(solution)/shard_map/ppermute | solution.py:130
  106.7 3.7 %model.12 = (f32[8,32,128]{2,1,0:T(8,128)S(1)}, bf16[8,32,128]{2,1,0:T(8,128)(2,1)S(1)}, bf16[8,32,128]{2,1,0:T(8,128)(2,1)S(1)}, bf16[8,32,128]{2,1,0:T(8,128)(2,1)S(1)}, f32[8,32,128]{2,1,0:T(8,128)}) custom-call(s32[92]{0:T(128)S(1)} %fusion.2.slots, s32[92]{0:T(128)S(1)} %copy-done.7, bf16[92,128,128]{2,1,0:T(8,128)(2,1)S(1)} %copy-done.1, ...), custom_call_target="tpu_custom_call" | custom-call | tf_op jit(solution)/shard_map/model/pallas_call | solution.py:188
  112.3 3.0 %collective-permute-done.33.refs_1_ = bf16[8,32,128]{2,1,0:T(8,128)(2,1)S(1)} collective-permute-done((bf16[8,32,128]{2,1,0:T(8,128)(2,1)S(1)}, bf16[8,32,128]{2,1,0:T(8,128)(2,1)S(1)}, u32[]{:S(2)}, u32[]{:S(2)}) %collective-permute-start.33) | collective-permute-done | bytes 65568 | tf_op jit(solution)/shard_map/ppermute | solution.py:130
  125.6 2.4 %collective-permute-done.38 = bf16[4,1,32,128]{3,2,1,0:T(8,128)(2,1)S(1)} collective-permute-done((bf16[4,1,32,128]{3,2,1,0:T(8,128)(2,1)S(1)}, bf16[4,1,32,128]{3,2,1,0:T(8,128)(2,1)S(1)}, u32[]{:S(2)}, u32[]{:S(2)}) %collective-permute-start.38) | collective-permute-done | bytes 32800 | tf_op jit(solution)/shard_map/ppermute | solution.py:130
  130.0 2.5 %collective-permute-done.41.refs_3_ = bf16[8,32,128]{2,1,0:T(8,128)(2,1)S(1)} collective-permute-done((bf16[8,32,128]{2,1,0:T(8,128)(2,1)S(1)}, bf16[8,32,128]{2,1,0:T(8,128)(2,1)S(1)}, u32[]{:S(2)}, u32[]{:S(2)}) %collective-permute-start.41) | collective-permute-done | bytes 65568 | tf_op jit(solution)/shard_map/ppermute | solution.py:130
  134.5 2.5 %collective-permute-start.43 = (bf16[2,4,32,128]{3,2,1,0:T(8,128)(2,1)S(1)}, bf16[2,4,32,128]{3,2,1,0:T(8,128)(2,1)S(1)}, u32[]{:S(2)}, u32[]{:S(2)}) collective-permute-start(bf16[2,4,32,128]{3,2,1,0:T(8,128)(2,1)S(1)} %get-tuple-element.95), channel_id=1, source_target_pairs={{0,16},{4,20},{8,24},{12,28},{16,0},{20,4},{24,8},{28,12},{1,17},{... | collective-permute-start | bytes 196616 | tf_op jit(solution)/shard_map/ppermute | solution.py:130
  139.6 2.8 %collective-permute-done.43.refs_2_ = bf16[2,4,32,128]{3,2,1,0:T(8,128)(2,1)S(1)} collective-permute-done((bf16[2,4,32,128]{3,2,1,0:T(8,128)(2,1)S(1)}, bf16[2,4,32,128]{3,2,1,0:T(8,128)(2,1)S(1)}, u32[]{:S(2)}, u32[]{:S(2)}) %collective-permute-start.43) | collective-permute-done | bytes 65568 | tf_op jit(solution)/shard_map/ppermute | solution.py:130
  144.7 3.4 %collective-permute-done.45.refs_4_ = bf16[4,4,32,128]{3,2,1,0:T(8,128)(2,1)S(1)} collective-permute-done((bf16[4,4,32,128]{3,2,1,0:T(8,128)(2,1)S(1)}, bf16[4,4,32,128]{3,2,1,0:T(8,128)(2,1)S(1)}, u32[]{:S(2)}, u32[]{:S(2)}) %collective-permute-start.45) | collective-permute-done | bytes 131104 | tf_op jit(solution)/shard_map/ppermute | solution.py:130
  148.2 3.7 %model.14 = (f32[8,32,128]{2,1,0:T(8,128)S(1)}, bf16[8,32,128]{2,1,0:T(8,128)(2,1)S(1)}, bf16[8,32,128]{2,1,0:T(8,128)(2,1)S(1)}, bf16[8,32,128]{2,1,0:T(8,128)(2,1)S(1)}, f32[8,32,128]{2,1,0:T(8,128)}) custom-call(s32[92]{0:T(128)S(1)} %fusion.2.slots, s32[92]{0:T(128)S(1)} %copy-done.7, bf16[92,128,128]{2,1,0:T(8,128)(2,1)S(1)} %copy-done.1, ...), custom_call_target="tpu_custom_call" | custom-call | tf_op jit(solution)/shard_map/model/pallas_call | solution.py:188
  153.7 3.0 %collective-permute-done.47.refs_1_ = bf16[8,32,128]{2,1,0:T(8,128)(2,1)S(1)} collective-permute-done((bf16[8,32,128]{2,1,0:T(8,128)(2,1)S(1)}, bf16[8,32,128]{2,1,0:T(8,128)(2,1)S(1)}, u32[]{:S(2)}, u32[]{:S(2)}) %collective-permute-start.47) | collective-permute-done | bytes 65568 | tf_op jit(solution)/shard_map/ppermute | solution.py:130
  163.4 2.1 %collective-permute-done.51 = bf16[2,1,32,128]{3,2,1,0:T(8,128)(2,1)S(1)} collective-permute-done((bf16[2,1,32,128]{3,2,1,0:T(8,128)(2,1)S(1)}, bf16[2,1,32,128]{3,2,1,0:T(8,128)(2,1)S(1)}, u32[]{:S(2)}, u32[]{:S(2)}) %collective-permute-start.51) | collective-permute-done | bytes 16416 | tf_op jit(solution)/shard_map/ppermute | solution.py:130
  167.1 2.4 %collective-permute-done.52 = bf16[4,1,32,128]{3,2,1,0:T(8,128)(2,1)S(1)} collective-permute-done((bf16[4,1,32,128]{3,2,1,0:T(8,128)(2,1)S(1)}, bf16[4,1,32,128]{3,2,1,0:T(8,128)(2,1)S(1)}, u32[]{:S(2)}, u32[]{:S(2)}) %collective-permute-start.52) | collective-permute-done | bytes 32800 | tf_op jit(solution)/shard_map/ppermute | solution.py:130
  171.5 2.2 %collective-permute-done.55.refs_3_ = bf16[8,32,128]{2,1,0:T(8,128)(2,1)S(1)} collective-permute-done((bf16[8,32,128]{2,1,0:T(8,128)(2,1)S(1)}, bf16[8,32,128]{2,1,0:T(8,128)(2,1)S(1)}, u32[]{:S(2)}, u32[]{:S(2)}) %collective-permute-start.55) | collective-permute-done | bytes 65568 | tf_op jit(solution)/shard_map/ppermute | solution.py:130
  (187 shorter events, 83.0 us)
Async XLA Ops:
  3.2 5.7 %collective-permute-start = (bf16[2,4,32,128]{3,2,1,0:T(8,128)(2,1)S(1)}, bf16[2,4,32,128]{3,2,1,0:T(8,128)(2,1)S(1)}, u32[]{:S(2)}, u32[]{:S(2)}) collective-permute-start(bf16[2,4,32,128]{3,2,1,0:T(8,128)(2,1)S(1)} %get-tuple-element.55), channel_id=1, source_target_pairs={{0,8},{4,12},{8,0},{12,4},{16,24},{20,28},{24,16},{28,20},{1,9},{5... | collective-permute-start | bytes 196616 | tf_op jit(solution)/shard_map/ppermute | solution.py:130
  6.3 7.3 %collective-permute-start.1 = (bf16[2,4,32,128]{3,2,1,0:T(8,128)(2,1)S(1)}, bf16[2,4,32,128]{3,2,1,0:T(8,128)(2,1)S(1)}, u32[]{:S(2)}, u32[]{:S(2)}) collective-permute-start(bf16[2,4,32,128]{3,2,1,0:T(8,128)(2,1)S(1)} %get-tuple-element.56), channel_id=1, source_target_pairs={{0,16},{4,20},{8,24},{12,28},{16,0},{20,4},{24,8},{28,12},{1,17},{... | collective-permute-start | bytes 196616 | tf_op jit(solution)/shard_map/ppermute | solution.py:130
  8.9 6.1 %collective-permute-start.2 = (bf16[2,4,32,128]{3,2,1,0:T(8,128)(2,1)S(1)}, bf16[2,4,32,128]{3,2,1,0:T(8,128)(2,1)S(1)}, u32[]{:S(2)}, u32[]{:S(2)}) collective-permute-start(bf16[2,4,32,128]{3,2,1,0:T(8,128)(2,1)S(1)} %get-tuple-element.57), channel_id=1, source_target_pairs={{0,24},{4,28},{8,16},{12,20},{16,8},{20,12},{24,0},{28,4},{1,25},{... | collective-permute-start | bytes 196616 | tf_op jit(solution)/shard_map/ppermute | solution.py:130
  15.0 5.0 %collective-permute-start.3 = (bf16[4,4,32,128]{3,2,1,0:T(8,128)(2,1)S(1)}, bf16[4,4,32,128]{3,2,1,0:T(8,128)(2,1)S(1)}, u32[]{:S(2)}, u32[]{:S(2)}) collective-permute-start(bf16[4,4,32,128]{3,2,1,0:T(8,128)(2,1)S(1)} %pad_maximum_fusion), channel_id=1, source_target_pairs={{0,4},{4,0},{8,12},{12,8},{16,20},{20,16},{24,28},{28,24},{1,5},{5... | collective-permute-start | bytes 393224 | tf_op jit(solution)/shard_map/ppermute | solution.py:130
  32.8 4.7 %collective-permute-start.8 = (bf16[2,1,32,128]{3,2,1,0:T(8,128)(2,1)S(1)}, bf16[2,1,32,128]{3,2,1,0:T(8,128)(2,1)S(1)}, u32[]{:S(2)}, u32[]{:S(2)}) collective-permute-start(bf16[2,1,32,128]{3,2,1,0:T(8,128)(2,1)S(1)} %get-tuple-element.64), channel_id=1, source_target_pairs={{0,16},{4,20},{8,24},{12,28},{16,0},{20,4},{24,8},{28,12},{1,17},{... | collective-permute-start | bytes 49160 | tf_op jit(solution)/shard_map/ppermute | solution.py:130
  35.2 5.5 %collective-permute-start.9 = (bf16[2,1,32,128]{3,2,1,0:T(8,128)(2,1)S(1)}, bf16[2,1,32,128]{3,2,1,0:T(8,128)(2,1)S(1)}, u32[]{:S(2)}, u32[]{:S(2)}) collective-permute-start(bf16[2,1,32,128]{3,2,1,0:T(8,128)(2,1)S(1)} %get-tuple-element.65), channel_id=1, source_target_pairs={{0,24},{4,28},{8,16},{12,20},{16,8},{20,12},{24,0},{28,4},{1,25},{... | collective-permute-start | bytes 49160 | tf_op jit(solution)/shard_map/ppermute | solution.py:130
  44.8 5.8 %collective-permute-start.12 = (bf16[8,32,128]{2,1,0:T(8,128)(2,1)S(1)}, bf16[8,32,128]{2,1,0:T(8,128)(2,1)S(1)}, u32[]{:S(2)}, u32[]{:S(2)}) collective-permute-start(bf16[8,32,128]{2,1,0:T(8,128)(2,1)S(1)} %constant_dynamic-update-slice_fusion.refs_0_), channel_id=1, source_target_pairs={{0,2},{1,3},{2,0},{3,1},{4,6},{5,7},{6,4},{7,5},{8,10},{9,11},{10,... | collective-permute-start | bytes 196616 | tf_op jit(solution)/shard_map/ppermute | solution.py:130
  51.7 5.2 %collective-permute-start.14 = (bf16[2,4,32,128]{3,2,1,0:T(8,128)(2,1)S(1)}, bf16[2,4,32,128]{3,2,1,0:T(8,128)(2,1)S(1)}, u32[]{:S(2)}, u32[]{:S(2)}) collective-permute-start(bf16[2,4,32,128]{3,2,1,0:T(8,128)(2,1)S(1)} %get-tuple-element.68), channel_id=1, source_target_pairs={{0,8},{4,12},{8,0},{12,4},{16,24},{20,28},{24,16},{28,20},{1,9},{5... | collective-permute-start | bytes 196616 | tf_op jit(solution)/shard_map/ppermute | solution.py:130
  51.8 8.0 %collective-permute-start.15 = (bf16[2,4,32,128]{3,2,1,0:T(8,128)(2,1)S(1)}, bf16[2,4,32,128]{3,2,1,0:T(8,128)(2,1)S(1)}, u32[]{:S(2)}, u32[]{:S(2)}) collective-permute-start(bf16[2,4,32,128]{3,2,1,0:T(8,128)(2,1)S(1)} %get-tuple-element.69), channel_id=1, source_target_pairs={{0,16},{4,20},{8,24},{12,28},{16,0},{20,4},{24,8},{28,12},{1,17},{... | collective-permute-start | bytes 196616 | tf_op jit(solution)/shard_map/ppermute | solution.py:130
  54.3 6.2 %collective-permute-start.16 = (bf16[2,4,32,128]{3,2,1,0:T(8,128)(2,1)S(1)}, bf16[2,4,32,128]{3,2,1,0:T(8,128)(2,1)S(1)}, u32[]{:S(2)}, u32[]{:S(2)}) collective-permute-start(bf16[2,4,32,128]{3,2,1,0:T(8,128)(2,1)S(1)} %get-tuple-element.70), channel_id=1, source_target_pairs={{0,24},{4,28},{8,16},{12,20},{16,8},{20,12},{24,0},{28,4},{1,25},{... | collective-permute-start | bytes 196616 | tf_op jit(solution)/shard_map/ppermute | solution.py:130
  60.5 5.0 %collective-permute-start.17 = (bf16[4,4,32,128]{3,2,1,0:T(8,128)(2,1)S(1)}, bf16[4,4,32,128]{3,2,1,0:T(8,128)(2,1)S(1)}, u32[]{:S(2)}, u32[]{:S(2)}) collective-permute-start(bf16[4,4,32,128]{3,2,1,0:T(8,128)(2,1)S(1)} %pad_maximum_fusion.1), channel_id=1, source_target_pairs={{0,4},{4,0},{8,12},{12,8},{16,20},{20,16},{24,28},{28,24},{1,5},{5... | collective-permute-start | bytes 393224 | tf_op jit(solution)/shard_map/ppermute | solution.py:130
  69.2 4.9 %collective-permute-start.19 = (bf16[8,32,128]{2,1,0:T(8,128)(2,1)S(1)}, bf16[8,32,128]{2,1,0:T(8,128)(2,1)S(1)}, u32[]{:S(2)}, u32[]{:S(2)}) collective-permute-start(bf16[8,32,128]{2,1,0:T(8,128)(2,1)S(1)} %get-tuple-element.73), channel_id=1, source_target_pairs={{0,2},{1,3},{2,0},{3,1},{4,6},{5,7},{6,4},{7,5},{8,10},{9,11},{10,... | collective-permute-start | bytes 196616 | tf_op jit(solution)/shard_map/ppermute | solution.py:130
  69.9 4.9 %collective-permute-start.20 = (bf16[8,32,128]{2,1,0:T(8,128)(2,1)S(1)}, bf16[8,32,128]{2,1,0:T(8,128)(2,1)S(1)}, u32[]{:S(2)}, u32[]{:S(2)}) collective-permute-start(bf16[8,32,128]{2,1,0:T(8,128)(2,1)S(1)} %get-tuple-element.74), channel_id=1, source_target_pairs={{0,3},{1,2},{2,1},{3,0},{4,7},{5,6},{6,5},{7,4},{8,11},{9,10},{10,... | collective-permute-start | bytes 196616 | tf_op jit(solution)/shard_map/ppermute | solution.py:130
  76.1 4.6 %collective-permute-start.22 = (bf16[2,1,32,128]{3,2,1,0:T(8,128)(2,1)S(1)}, bf16[2,1,32,128]{3,2,1,0:T(8,128)(2,1)S(1)}, u32[]{:S(2)}, u32[]{:S(2)}) collective-permute-start(bf16[2,1,32,128]{3,2,1,0:T(8,128)(2,1)S(1)} %get-tuple-element.77), channel_id=1, source_target_pairs={{0,16},{4,20},{8,24},{12,28},{16,0},{20,4},{24,8},{28,12},{1,17},{... | collective-permute-start | bytes 49160 | tf_op jit(solution)/shard_map/ppermute | solution.py:130
  77.3 5.5 %collective-permute-start.23 = (bf16[2,1,32,128]{3,2,1,0:T(8,128)(2,1)S(1)}, bf16[2,1,32,128]{3,2,1,0:T(8,128)(2,1)S(1)}, u32[]{:S(2)}, u32[]{:S(2)}) collective-permute-start(bf16[2,1,32,128]{3,2,1,0:T(8,128)(2,1)S(1)} %get-tuple-element.78), channel_id=1, source_target_pairs={{0,24},{4,28},{8,16},{12,20},{16,8},{20,12},{24,0},{28,4},{1,25},{... | collective-permute-start | bytes 49160 | tf_op jit(solution)/shard_map/ppermute | solution.py:130
  87.0 5.0 %collective-permute-start.26 = (bf16[8,32,128]{2,1,0:T(8,128)(2,1)S(1)}, bf16[8,32,128]{2,1,0:T(8,128)(2,1)S(1)}, u32[]{:S(2)}, u32[]{:S(2)}) collective-permute-start(bf16[8,32,128]{2,1,0:T(8,128)(2,1)S(1)} %constant_dynamic-update-slice_fusion.8.refs_0_), channel_id=1, source_target_pairs={{0,2},{1,3},{2,0},{3,1},{4,6},{5,7},{6,4},{7,5},{8,10},{9,11},{10,... | collective-permute-start | bytes 196616 | tf_op jit(solution)/shard_map/ppermute | solution.py:130
  92.9 5.2 %collective-permute-start.28 = (bf16[2,4,32,128]{3,2,1,0:T(8,128)(2,1)S(1)}, bf16[2,4,32,128]{3,2,1,0:T(8,128)(2,1)S(1)}, u32[]{:S(2)}, u32[]{:S(2)}) collective-permute-start(bf16[2,4,32,128]{3,2,1,0:T(8,128)(2,1)S(1)} %get-tuple-element.81), channel_id=1, source_target_pairs={{0,8},{4,12},{8,0},{12,4},{16,24},{20,28},{24,16},{28,20},{1,9},{5... | collective-permute-start | bytes 196616 | tf_op jit(solution)/shard_map/ppermute | solution.py:130
  93.0 7.9 %collective-permute-start.29 = (bf16[2,4,32,128]{3,2,1,0:T(8,128)(2,1)S(1)}, bf16[2,4,32,128]{3,2,1,0:T(8,128)(2,1)S(1)}, u32[]{:S(2)}, u32[]{:S(2)}) collective-permute-start(bf16[2,4,32,128]{3,2,1,0:T(8,128)(2,1)S(1)} %get-tuple-element.82), channel_id=1, source_target_pairs={{0,16},{4,20},{8,24},{12,28},{16,0},{20,4},{24,8},{28,12},{1,17},{... | collective-permute-start | bytes 196616 | tf_op jit(solution)/shard_map/ppermute | solution.py:130
  95.5 6.2 %collective-permute-start.30 = (bf16[2,4,32,128]{3,2,1,0:T(8,128)(2,1)S(1)}, bf16[2,4,32,128]{3,2,1,0:T(8,128)(2,1)S(1)}, u32[]{:S(2)}, u32[]{:S(2)}) collective-permute-start(bf16[2,4,32,128]{3,2,1,0:T(8,128)(2,1)S(1)} %get-tuple-element.83), channel_id=1, source_target_pairs={{0,24},{4,28},{8,16},{12,20},{16,8},{20,12},{24,0},{28,4},{1,25},{... | collective-permute-start | bytes 196616 | tf_op jit(solution)/shard_map/ppermute | solution.py:130
  101.7 5.0 %collective-permute-start.31 = (bf16[4,4,32,128]{3,2,1,0:T(8,128)(2,1)S(1)}, bf16[4,4,32,128]{3,2,1,0:T(8,128)(2,1)S(1)}, u32[]{:S(2)}, u32[]{:S(2)}) collective-permute-start(bf16[4,4,32,128]{3,2,1,0:T(8,128)(2,1)S(1)} %pad_maximum_fusion.2), channel_id=1, source_target_pairs={{0,4},{4,0},{8,12},{12,8},{16,20},{20,16},{24,28},{28,24},{1,5},{5... | collective-permute-start | bytes 393224 | tf_op jit(solution)/shard_map/ppermute | solution.py:130
  110.4 4.9 %collective-permute-start.33 = (bf16[8,32,128]{2,1,0:T(8,128)(2,1)S(1)}, bf16[8,32,128]{2,1,0:T(8,128)(2,1)S(1)}, u32[]{:S(2)}, u32[]{:S(2)}) collective-permute-start(bf16[8,32,128]{2,1,0:T(8,128)(2,1)S(1)} %get-tuple-element.86), channel_id=1, source_target_pairs={{0,2},{1,3},{2,0},{3,1},{4,6},{5,7},{6,4},{7,5},{8,10},{9,11},{10,... | collective-permute-start | bytes 196616 | tf_op jit(solution)/shard_map/ppermute | solution.py:130
  117.3 4.6 %collective-permute-start.36 = (bf16[2,1,32,128]{3,2,1,0:T(8,128)(2,1)S(1)}, bf16[2,1,32,128]{3,2,1,0:T(8,128)(2,1)S(1)}, u32[]{:S(2)}, u32[]{:S(2)}) collective-permute-start(bf16[2,1,32,128]{3,2,1,0:T(8,128)(2,1)S(1)} %get-tuple-element.90), channel_id=1, source_target_pairs={{0,16},{4,20},{8,24},{12,28},{16,0},{20,4},{24,8},{28,12},{1,17},{... | collective-permute-start | bytes 49160 | tf_op jit(solution)/shard_map/ppermute | solution.py:130
  118.5 5.5 %collective-permute-start.37 = (bf16[2,1,32,128]{3,2,1,0:T(8,128)(2,1)S(1)}, bf16[2,1,32,128]{3,2,1,0:T(8,128)(2,1)S(1)}, u32[]{:S(2)}, u32[]{:S(2)}) collective-permute-start(bf16[2,1,32,128]{3,2,1,0:T(8,128)(2,1)S(1)} %get-tuple-element.91), channel_id=1, source_target_pairs={{0,24},{4,28},{8,16},{12,20},{16,8},{20,12},{24,0},{28,4},{1,25},{... | collective-permute-start | bytes 49160 | tf_op jit(solution)/shard_map/ppermute | solution.py:130
  128.1 5.3 %collective-permute-start.40 = (bf16[8,32,128]{2,1,0:T(8,128)(2,1)S(1)}, bf16[8,32,128]{2,1,0:T(8,128)(2,1)S(1)}, u32[]{:S(2)}, u32[]{:S(2)}) collective-permute-start(bf16[8,32,128]{2,1,0:T(8,128)(2,1)S(1)} %constant_dynamic-update-slice_fusion.16.refs_0_), channel_id=1, source_target_pairs={{0,2},{1,3},{2,0},{3,1},{4,6},{5,7},{6,4},{7,5},{8,10},{9,11},{10,... | collective-permute-start | bytes 196616 | tf_op jit(solution)/shard_map/ppermute | solution.py:130
  134.4 5.2 %collective-permute-start.42 = (bf16[2,4,32,128]{3,2,1,0:T(8,128)(2,1)S(1)}, bf16[2,4,32,128]{3,2,1,0:T(8,128)(2,1)S(1)}, u32[]{:S(2)}, u32[]{:S(2)}) collective-permute-start(bf16[2,4,32,128]{3,2,1,0:T(8,128)(2,1)S(1)} %get-tuple-element.94), channel_id=1, source_target_pairs={{0,8},{4,12},{8,0},{12,4},{16,24},{20,28},{24,16},{28,20},{1,9},{5... | collective-permute-start | bytes 196616 | tf_op jit(solution)/shard_map/ppermute | solution.py:130
  134.5 7.9 %collective-permute-start.43 = (bf16[2,4,32,128]{3,2,1,0:T(8,128)(2,1)S(1)}, bf16[2,4,32,128]{3,2,1,0:T(8,128)(2,1)S(1)}, u32[]{:S(2)}, u32[]{:S(2)}) collective-permute-start(bf16[2,4,32,128]{3,2,1,0:T(8,128)(2,1)S(1)} %get-tuple-element.95), channel_id=1, source_target_pairs={{0,16},{4,20},{8,24},{12,28},{16,0},{20,4},{24,8},{28,12},{1,17},{... | collective-permute-start | bytes 196616 | tf_op jit(solution)/shard_map/ppermute | solution.py:130
  136.9 6.2 %collective-permute-start.44 = (bf16[2,4,32,128]{3,2,1,0:T(8,128)(2,1)S(1)}, bf16[2,4,32,128]{3,2,1,0:T(8,128)(2,1)S(1)}, u32[]{:S(2)}, u32[]{:S(2)}) collective-permute-start(bf16[2,4,32,128]{3,2,1,0:T(8,128)(2,1)S(1)} %get-tuple-element.96), channel_id=1, source_target_pairs={{0,24},{4,28},{8,16},{12,20},{16,8},{20,12},{24,0},{28,4},{1,25},{... | collective-permute-start | bytes 196616 | tf_op jit(solution)/shard_map/ppermute | solution.py:130
  143.1 5.0 %collective-permute-start.45 = (bf16[4,4,32,128]{3,2,1,0:T(8,128)(2,1)S(1)}, bf16[4,4,32,128]{3,2,1,0:T(8,128)(2,1)S(1)}, u32[]{:S(2)}, u32[]{:S(2)}) collective-permute-start(bf16[4,4,32,128]{3,2,1,0:T(8,128)(2,1)S(1)} %pad_maximum_fusion.3), channel_id=1, source_target_pairs={{0,4},{4,0},{8,12},{12,8},{16,20},{20,16},{24,28},{28,24},{1,5},{5... | collective-permute-start | bytes 393224 | tf_op jit(solution)/shard_map/ppermute | solution.py:130
  151.8 4.9 %collective-permute-start.47 = (bf16[8,32,128]{2,1,0:T(8,128)(2,1)S(1)}, bf16[8,32,128]{2,1,0:T(8,128)(2,1)S(1)}, u32[]{:S(2)}, u32[]{:S(2)}) collective-permute-start(bf16[8,32,128]{2,1,0:T(8,128)(2,1)S(1)} %get-tuple-element.99), channel_id=1, source_target_pairs={{0,2},{1,3},{2,0},{3,1},{4,6},{5,7},{6,4},{7,5},{8,10},{9,11},{10,... | collective-permute-start | bytes 196616 | tf_op jit(solution)/shard_map/ppermute | solution.py:130
  158.7 4.6 %collective-permute-start.50 = (bf16[2,1,32,128]{3,2,1,0:T(8,128)(2,1)S(1)}, bf16[2,1,32,128]{3,2,1,0:T(8,128)(2,1)S(1)}, u32[]{:S(2)}, u32[]{:S(2)}) collective-permute-start(bf16[2,1,32,128]{3,2,1,0:T(8,128)(2,1)S(1)} %get-tuple-element.103), channel_id=1, source_target_pairs={{0,16},{4,20},{8,24},{12,28},{16,0},{20,4},{24,8},{28,12},{1,17},{... | collective-permute-start | bytes 49160 | tf_op jit(solution)/shard_map/ppermute | solution.py:130
  159.9 5.5 %collective-permute-start.51 = (bf16[2,1,32,128]{3,2,1,0:T(8,128)(2,1)S(1)}, bf16[2,1,32,128]{3,2,1,0:T(8,128)(2,1)S(1)}, u32[]{:S(2)}, u32[]{:S(2)}) collective-permute-start(bf16[2,1,32,128]{3,2,1,0:T(8,128)(2,1)S(1)} %get-tuple-element.104), channel_id=1, source_target_pairs={{0,24},{4,28},{8,16},{12,20},{16,8},{20,12},{24,0},{28,4},{1,25},{... | collective-permute-start | bytes 49160 | tf_op jit(solution)/shard_map/ppermute | solution.py:130
  169.6 5.0 %collective-permute-start.54 = (bf16[8,32,128]{2,1,0:T(8,128)(2,1)S(1)}, bf16[8,32,128]{2,1,0:T(8,128)(2,1)S(1)}, u32[]{:S(2)}, u32[]{:S(2)}) collective-permute-start(bf16[8,32,128]{2,1,0:T(8,128)(2,1)S(1)} %constant_dynamic-update-slice_fusion.24.refs_0_), channel_id=1, source_target_pairs={{0,2},{1,3},{2,0},{3,1},{4,6},{5,7},{6,4},{7,5},{8,10},{9,11},{10,... | collective-permute-start | bytes 196616 | tf_op jit(solution)/shard_map/ppermute | solution.py:130
  (33 other events, 350.2 us)

commit v3 on v1

v3 whole, which is shorter than its diff:
```python
import functools

import jax
import jax.numpy as jnp
from jax import lax
from jax.experimental import pallas as pl
from jax.experimental.pallas import tpu as pltpu
from jax.sharding import PartitionSpec as P

ITERATIONS = 4


VMEM = pl.BlockSpec(memory_space=pltpu.VMEM)
SMEM = pl.BlockSpec(memory_space=pltpu.SMEM)
PARAMS = pltpu.CompilerParams(vmem_limit_bytes=32 * 1024 * 1024)


def model_kernel(slots, places, rows, model, measured, tiles, own, *refs):
    *sent, residual, narrow, sums = refs
    wide = own.shape[0]
    count = model.shape[0]
    residual[...] = measured[...]
    sums[...] = jnp.zeros_like(sums)
    for k in range(count):
        part = lax.dot_general(
            tiles[slots[k]],
            model[k],
            (((1,), (1,)), ((), ())),
            preferred_element_type=jnp.float32,
        )
        residual[rows[k]] -= part
    narrow[...] = residual[...].astype(jnp.bfloat16)
    for k in range(count):
        part = jnp.dot(narrow[rows[k]], model[k], preferred_element_type=jnp.float32)
        sums[places[k]] += part
    own[...] = sums[:wide]
    for d, out in enumerate(sent, 1):
        out[...] = sums[d * wide : (d + 1) * wide].astype(jnp.bfloat16)


def reduce_kernel(own, *refs):
    *received, out = refs
    total = own[...]
    for piece in received:
        total = total + piece[...].astype(jnp.float32)
    out[...] = total.astype(jnp.bfloat16)


def pick_kernel(table, image, out):
    vox_count, capacity = table.shape
    for v in range(vox_count):
        for s in range(capacity):
            tile = jnp.maximum(table[v, s], 0)
            out[v * capacity + s] = image[tile].astype(jnp.bfloat16)


def update_kernel(chan_count, ids, table, gains, image, *refs):
    received = refs[:chan_count]
    estimate, *outs = refs[chan_count:-1]
    gradient = refs[-1]
    vox_count, capacity = table.shape
    per = capacity // chan_count
    gradient[...] = jnp.zeros_like(gradient)
    for d in range(chan_count):
        first = (ids[0] ^ d) * per
        for v in range(vox_count):
            for p in range(per):
                tile = jnp.maximum(table[v, first + p], 0)
                gradient[tile] += received[d][v * per + p].astype(jnp.float32)
    estimate[...] = jnp.maximum(image[...] + gains[...][None] * gradient[...], 0.0)
    if outs:
        pick_kernel(table, estimate, *outs)


def shards(model_blocks, start_image, measured, step_size, sent_tiles, block_rows, block_slots):
    vox_count = lax.axis_size("vox")
    chan_count = lax.axis_size("chan")
    chan = lax.axis_index("chan")
    table = sent_tiles[0]
    capacity = table.shape[1]
    per = capacity // chan_count
    tile_count, wave_count, width = start_image.shape
    row_count = measured.shape[0]
    slot_count = vox_count * capacity
    wide = vox_count * per
    tile = (wave_count, width)
    ids = chan.astype(jnp.int32)[None]
    slab, slot = block_slots // capacity, block_slots % capacity
    places = (((slot // per) ^ chan) * vox_count + slab) * per + slot % per
    gains = jnp.broadcast_to(step_size[:, None], tile)

    def shape(count, dtype):
        return jax.ShapeDtypeStruct((count, *tile), dtype)

    def swap(array, step):
        pairs = [(i, i ^ step) for i in range(chan_count)]
        return lax.ppermute(array, "chan", pairs) if step else array

    def exchange(array):
        return lax.all_to_all(array, "vox", split_axis=0, concat_axis=0, tiled=True)

    apply_model = pl.pallas_call(
        model_kernel,
        out_shape=(
            shape(wide, jnp.float32),
            *[shape(wide, jnp.bfloat16)] * (chan_count - 1),
            shape(row_count, jnp.float32),
        ),
        in_specs=[SMEM, SMEM, SMEM, VMEM, VMEM, VMEM],
        out_specs=[VMEM] * (chan_count + 1),
        scratch_shapes=[
            pltpu.VMEM((row_count, *tile), jnp.bfloat16),
            pltpu.VMEM((slot_count, *tile), jnp.float32),
        ],
        compiler_params=PARAMS,
        name="model",
    )
    reduce_parts = pl.pallas_call(
        reduce_kernel,
        out_shape=shape(wide, jnp.bfloat16),
        in_specs=[VMEM] * chan_count,
        out_specs=VMEM,
        compiler_params=PARAMS,
        name="reduce",
    )
    pick = pl.pallas_call(
        pick_kernel,
        out_shape=shape(slot_count, jnp.bfloat16),
        in_specs=[SMEM, VMEM],
        out_specs=VMEM,
        compiler_params=PARAMS,
        name="pick",
    )

    def update(last):
        outs = [] if last else [shape(slot_count, jnp.bfloat16)]
        return pl.pallas_call(
            functools.partial(update_kernel, chan_count),
            out_shape=[shape(tile_count, jnp.float32)] + outs,
            in_specs=[SMEM, SMEM, VMEM, VMEM] + [VMEM] * chan_count,
            out_specs=[VMEM] * (len(outs) + 1),
            scratch_shapes=[pltpu.VMEM((tile_count, *tile), jnp.float32)],
            compiler_params=PARAMS,
            name="update",
        )

    estimate = start_image
    outgoing = [pick(table, start_image)]
    for iteration in range(ITERATIONS):
        tiles = exchange(*outgoing)
        own, *partial, residual = apply_model(
            block_slots, places, block_rows, model_blocks, measured, tiles
        )
        total = reduce_parts(own, *[swap(piece, d) for d, piece in enumerate(partial, 1)])
        returned = exchange(total)
        spread = [swap(returned, d) for d in range(chan_count)]
        estimate, *outgoing = update(iteration == ITERATIONS - 1)(
            ids, table, gains, estimate, *spread
        )
    return (estimate, residual)


def solution(mesh):
    in_specs = (
        P(("vox", "chan"), None, None),
        P("vox", None, None),
        P(("vox", "chan"), None, None),
        P(),
        P("vox", None, None),
        P(("vox", "chan")),
        P(("vox", "chan")),
    )
    out_specs = (P("vox", None, None), P(("vox", "chan"), None, None))
    return jax.shard_map(shards, mesh=mesh, in_specs=in_specs, out_specs=out_specs, check_vma=False)
```

time: 194 us -> 164 us (0.85)
  starting transfers between devices: 106 us -> 22.3 us
  blocking collectives: 0 us -> 76.8 us
  waiting for transfers between devices: 60.7 us -> 36.6 us
    ppermute x80 -> x24, starting transfers between devices: 106 us -> 14.9 us  [swap(): return lax.ppermute(array, 'chan', pairs) if step else array]
    all_to_all x0 -> x7, blocking collectives: none -> 76.8 us  [exchange(): return lax.all_to_all(array, 'vox', split_axis=0, concat_axis=0, tiled=True)]
    ppermute x80 -> x24, waiting for transfers between devices: 60.7 us -> 28.4 us  [swap(): return lax.ppermute(array, 'chan', pairs) if step else array]
    all_to_all x0 -> x1, waiting for transfers between devices: none -> 8.25 us  [exchange(): return lax.all_to_all(array, 'vox', split_axis=0, concat_axis=0, tiled=True)]
    all_to_all x0 -> x1, starting transfers between devices: none -> 7.38 us  [exchange(): return lax.all_to_all(array, 'vox', split_axis=0, concat_axis=0, tiled=True)]
    unnamed x46 -> x20, local copies, waits for them, and re-layouts: 4.67 us -> 5.13 us
  transfers between devices with their start and end apart: 80 -> 25, of which waited for: 36 -> 17; matrix products, arithmetic and copies ran while one was open for 0% -> 0% of each run, Pallas kernels for 0% -> 0%
where the time goes in v3:
time: 164 us
  blocking collectives  76.8 us (47%)
  waiting for transfers between devices  36.6 us (22%)
  starting transfers between devices  22.3 us (14%)
  Pallas kernels  20.8 us (13%)
  local copies, waits for them, and re-layouts  5.96 us (4%)
    all_to_all x7, blocking collectives, exchange(): return lax.all_to_all(array, 'vox', split_axis=0, concat_axis=0, tiled=True)  76.8 us
    ppermute x24, waiting for transfers between devices, swap(): return lax.ppermute(array, 'chan', pairs) if step else array  28.4 us
    ppermute x24, starting transfers between devices, swap(): return lax.ppermute(array, 'chan', pairs) if step else array  14.9 us
    pallas_call x4, Pallas kernels, shards(): apply_model(block_slots, places, block_rows, model_blocks, measured, tiles)  14.8 us
    all_to_all x1, waiting for transfers between devices, exchange(): return lax.all_to_all(array, 'vox', split_axis=0, concat_axis=0, tiled=True)  8.25 us
    all_to_all x1, starting transfers between devices, exchange(): return lax.all_to_all(array, 'vox', split_axis=0, concat_axis=0, tiled=True)  7.38 us
    unnamed x20, local copies, waits for them, and re-layouts  5.13 us
    pallas_call x4, Pallas kernels, shards(): update(iteration == ITERATIONS - 1)(ids, table, gains, estimate, *spread)  4.5 us
  transfers between devices with their start and end apart: 25, of which 17 were waited for; matrix products, arithmetic and copies ran while one was open for 0% of the time, Pallas kernels for 0%

profile of v3, /device:TPU:0, one launch (start us, length us, event | category | flops | bytes accessed | tf_op | source)
XLA Modules:
  0.0 163.8 jit_solution(4454311255401295052)
XLA Ops:
  2.4 1.3 pick.1
  3.8 7.4 %all-to-all-start = ((bf16[32,32,128]{2,1,0:T(8,128)(2,1)}), bf16[32,32,128]{2,1,0:T(8,128)(2,1)S(1)}, u32[]{:S(2)}, u32[]{:S(2)}) async-start(bf16[32,32,128]{2,1,0:T(8,128)(2,1)} %pick.1), calls=%async_computation | async-start | bytes 524288 | tf_op jit(solution)/shard_map/all_to_all | solution.py:100
  11.8 8.2 %all-to-all-done.tiles = bf16[32,32,128]{2,1,0:T(8,128)(2,1)S(1)} async-done(((bf16[32,32,128]{2,1,0:T(8,128)(2,1)}), bf16[32,32,128]{2,1,0:T(8,128)(2,1)S(1)}, u32[]{:S(2)}, u32[]{:S(2)}) %all-to-all-start) | async-done | bytes 262176 | tf_op jit(solution)/shard_map/all_to_all | solution.py:100
  20.1 1.9 %copy-done = bf16[92,128,128]{2,1,0:T(8,128)(2,1)S(1)} copy-done((bf16[92,128,128]{2,1,0:T(8,128)(2,1)S(1)}, bf16[92,128,128]{2,1,0:T(8,128)(2,1)}, u32[]{:S(2)}) %copy-start) | copy-done | bytes 3014680
  24.2 3.7 %model.8 = (f32[8,32,128]{2,1,0:T(8,128)S(1)}, bf16[8,32,128]{2,1,0:T(8,128)(2,1)S(1)}, bf16[8,32,128]{2,1,0:T(8,128)(2,1)S(1)}, bf16[8,32,128]{2,1,0:T(8,128)(2,1)S(1)}, f32[8,32,128]{2,1,0:T(8,128)}) custom-call(s32[92]{0:T(128)S(1)} %copy-done.5, s32[92]{0:T(128)S(1)} %fusion.2.places, s32[92]{0:T(128)S(1)} %copy-done.7, ...), custom_call_target="tpu_custom_call" | custom-call | tf_op jit(solution)/shard_map/model/pallas_call | solution.py:151
  27.9 1.5 collective-permute-start.1
  29.7 2.6 %collective-permute-done.1.refs_1_ = bf16[8,32,128]{2,1,0:T(8,128)(2,1)S(1)} collective-permute-done((bf16[8,32,128]{2,1,0:T(8,128)(2,1)S(1)}, bf16[8,32,128]{2,1,0:T(8,128)(2,1)S(1)}, u32[]{:S(2)}, u32[]{:S(2)}) %collective-permute-start.1) | collective-permute-done | bytes 65568 | tf_op jit(solution)/shard_map/ppermute | solution.py:97
  33.5 10.3 %all_to_all.40.refs_0_ = bf16[8,32,128]{2,1,0:T(8,128)(2,1)S(1)} all-to-all(bf16[8,32,128]{2,1,0:T(8,128)(2,1)S(1)} %reduce.4), channel_id=1, replica_groups=mesh['vox'=8,'chan'=4] {'vox'}, dimensions={0} | all-to-all | bytes 131072 | tf_op jit(solution)/shard_map/all_to_all | solution.py:100
  43.8 1.5 collective-permute-start.4
  45.7 2.5 %collective-permute-done.5.refs_3_ = bf16[8,32,128]{2,1,0:T(8,128)(2,1)S(1)} collective-permute-done((bf16[8,32,128]{2,1,0:T(8,128)(2,1)S(1)}, bf16[8,32,128]{2,1,0:T(8,128)(2,1)S(1)}, u32[]{:S(2)}, u32[]{:S(2)}) %collective-permute-start.5) | collective-permute-done | bytes 65568 | tf_op jit(solution)/shard_map/ppermute | solution.py:97
  48.2 1.4 collective-permute-done.4.refs_2_
  50.6 11.9 %all_to_all.41.tiles = bf16[32,32,128]{2,1,0:T(8,128)(2,1)S(1)} all-to-all(bf16[32,32,128]{2,1,0:T(8,128)(2,1)S(1)} %get-tuple-element.30), channel_id=1, replica_groups=mesh['vox'=8,'chan'=4] {'vox'}, dimensions={0} | all-to-all | bytes 524288 | tf_op jit(solution)/shard_map/all_to_all | solution.py:100
  62.5 3.7 %model.10 = (f32[8,32,128]{2,1,0:T(8,128)S(1)}, bf16[8,32,128]{2,1,0:T(8,128)(2,1)S(1)}, bf16[8,32,128]{2,1,0:T(8,128)(2,1)S(1)}, bf16[8,32,128]{2,1,0:T(8,128)(2,1)S(1)}, f32[8,32,128]{2,1,0:T(8,128)}) custom-call(s32[92]{0:T(128)S(1)} %copy-done.6, s32[92]{0:T(128)S(1)} %fusion.2.places, s32[92]{0:T(128)S(1)} %copy-done.8, ...), custom_call_target="tpu_custom_call" | custom-call | tf_op jit(solution)/shard_map/model/pallas_call | solution.py:151
  66.8 1.3 collective-permute-start.8
  68.1 3.0 %collective-permute-done.7.refs_1_ = bf16[8,32,128]{2,1,0:T(8,128)(2,1)S(1)} collective-permute-done((bf16[8,32,128]{2,1,0:T(8,128)(2,1)S(1)}, bf16[8,32,128]{2,1,0:T(8,128)(2,1)S(1)}, u32[]{:S(2)}, u32[]{:S(2)}) %collective-permute-start.7) | collective-permute-done | bytes 65568 | tf_op jit(solution)/shard_map/ppermute | solution.py:97
  71.8 10.3 %all_to_all.42.refs_0_ = bf16[8,32,128]{2,1,0:T(8,128)(2,1)S(1)} all-to-all(bf16[8,32,128]{2,1,0:T(8,128)(2,1)S(1)} %reduce.5), channel_id=1, replica_groups=mesh['vox'=8,'chan'=4] {'vox'}, dimensions={0} | all-to-all | bytes 131072 | tf_op jit(solution)/shard_map/all_to_all | solution.py:100
  82.7 1.2 collective-permute-start.9
  83.9 2.0 %collective-permute-done.11.refs_3_ = bf16[8,32,128]{2,1,0:T(8,128)(2,1)S(1)} collective-permute-done((bf16[8,32,128]{2,1,0:T(8,128)(2,1)S(1)}, bf16[8,32,128]{2,1,0:T(8,128)(2,1)S(1)}, u32[]{:S(2)}, u32[]{:S(2)}) %collective-permute-start.11) | collective-permute-done | bytes 65568 | tf_op jit(solution)/shard_map/ppermute | solution.py:97
  85.9 1.1 collective-permute-done.10.refs_2_
  87.9 11.9 %all_to_all.43.tiles = bf16[32,32,128]{2,1,0:T(8,128)(2,1)S(1)} all-to-all(bf16[32,32,128]{2,1,0:T(8,128)(2,1)S(1)} %get-tuple-element.36), channel_id=1, replica_groups=mesh['vox'=8,'chan'=4] {'vox'}, dimensions={0} | all-to-all | bytes 524288 | tf_op jit(solution)/shard_map/all_to_all | solution.py:100
  99.8 3.7 %model.12 = (f32[8,32,128]{2,1,0:T(8,128)S(1)}, bf16[8,32,128]{2,1,0:T(8,128)(2,1)S(1)}, bf16[8,32,128]{2,1,0:T(8,128)(2,1)S(1)}, bf16[8,32,128]{2,1,0:T(8,128)(2,1)S(1)}, f32[8,32,128]{2,1,0:T(8,128)}) custom-call(s32[92]{0:T(128)S(1)} %copy-done.6, s32[92]{0:T(128)S(1)} %fusion.2.places, s32[92]{0:T(128)S(1)} %copy-done.8, ...), custom_call_target="tpu_custom_call" | custom-call | tf_op jit(solution)/shard_map/model/pallas_call | solution.py:151
  103.5 1.3 collective-permute-start.13
  105.4 2.8 %collective-permute-done.13.refs_1_ = bf16[8,32,128]{2,1,0:T(8,128)(2,1)S(1)} collective-permute-done((bf16[8,32,128]{2,1,0:T(8,128)(2,1)S(1)}, bf16[8,32,128]{2,1,0:T(8,128)(2,1)S(1)}, u32[]{:S(2)}, u32[]{:S(2)}) %collective-permute-start.13) | collective-permute-done | bytes 65568 | tf_op jit(solution)/shard_map/ppermute | solution.py:97
  109.2 10.3 %all_to_all.44.refs_0_ = bf16[8,32,128]{2,1,0:T(8,128)(2,1)S(1)} all-to-all(bf16[8,32,128]{2,1,0:T(8,128)(2,1)S(1)} %reduce.6), channel_id=1, replica_groups=mesh['vox'=8,'chan'=4] {'vox'}, dimensions={0} | all-to-all | bytes 131072 | tf_op jit(solution)/shard_map/all_to_all | solution.py:100
  119.5 1.2 collective-permute-start.16
  121.4 2.5 %collective-permute-done.17.refs_3_ = bf16[8,32,128]{2,1,0:T(8,128)(2,1)S(1)} collective-permute-done((bf16[8,32,128]{2,1,0:T(8,128)(2,1)S(1)}, bf16[8,32,128]{2,1,0:T(8,128)(2,1)S(1)}, u32[]{:S(2)}, u32[]{:S(2)}) %collective-permute-start.17) | collective-permute-done | bytes 65568 | tf_op jit(solution)/shard_map/ppermute | solution.py:97
  125.7 11.9 %all_to_all.45.tiles = bf16[32,32,128]{2,1,0:T(8,128)(2,1)S(1)} all-to-all(bf16[32,32,128]{2,1,0:T(8,128)(2,1)S(1)} %get-tuple-element.42), channel_id=1, replica_groups=mesh['vox'=8,'chan'=4] {'vox'}, dimensions={0} | all-to-all | bytes 524288 | tf_op jit(solution)/shard_map/all_to_all | solution.py:100
  137.6 3.7 %model.14 = (f32[8,32,128]{2,1,0:T(8,128)S(1)}, bf16[8,32,128]{2,1,0:T(8,128)(2,1)S(1)}, bf16[8,32,128]{2,1,0:T(8,128)(2,1)S(1)}, bf16[8,32,128]{2,1,0:T(8,128)(2,1)S(1)}, f32[8,32,128]{2,1,0:T(8,128)}) custom-call(s32[92]{0:T(128)S(1)} %copy-done.6, s32[92]{0:T(128)S(1)} %fusion.2.places, s32[92]{0:T(128)S(1)} %copy-done.8, ...), custom_call_target="tpu_custom_call" | custom-call | tf_op jit(solution)/shard_map/model/pallas_call | solution.py:151
  143.2 3.0 %collective-permute-done.19.refs_1_ = bf16[8,32,128]{2,1,0:T(8,128)(2,1)S(1)} collective-permute-done((bf16[8,32,128]{2,1,0:T(8,128)(2,1)S(1)}, bf16[8,32,128]{2,1,0:T(8,128)(2,1)S(1)}, u32[]{:S(2)}, u32[]{:S(2)}) %collective-permute-start.19) | collective-permute-done | bytes 65568 | tf_op jit(solution)/shard_map/ppermute | solution.py:97
  146.9 10.3 %all_to_all.46.refs_0_ = bf16[8,32,128]{2,1,0:T(8,128)(2,1)S(1)} all-to-all(bf16[8,32,128]{2,1,0:T(8,128)(2,1)S(1)} %reduce.7), channel_id=1, replica_groups=mesh['vox'=8,'chan'=4] {'vox'}, dimensions={0} | all-to-all | bytes 131072 | tf_op jit(solution)/shard_map/all_to_all | solution.py:100
  159.0 2.2 %collective-permute-done.23.refs_3_ = bf16[8,32,128]{2,1,0:T(8,128)(2,1)S(1)} collective-permute-done((bf16[8,32,128]{2,1,0:T(8,128)(2,1)S(1)}, bf16[8,32,128]{2,1,0:T(8,128)(2,1)S(1)}, u32[]{:S(2)}, u32[]{:S(2)}) %collective-permute-start.23) | collective-permute-done | bytes 65568 | tf_op jit(solution)/shard_map/ppermute | solution.py:97
  162.1 1.7 %update.7 = f32[32,32,128]{2,1,0:T(8,128)} custom-call(s32[1]{0:T(128)} %bitcast.ids, s32[8,4]{1,0:T(8,128)S(1)} %copy.13.table, f32[32,128]{1,0:T(8,128)S(1)} %broadcast_in_dim.10.gains, f32[32,32,128]{2,1,0:T(8,128)S(1)} %get-tuple-element.41.image, bf16[8,32,128]{2,1,0:T(8,128)(2,1)S(1)} %all_to_all.46.refs_0_, ...), custom_call_target="tpu_custom_call" | custom-call | tf_op jit(solution)/shard_map/update/pallas_call | solution.py:157
  (61 shorter events, 19.7 us)
Async XLA Ops:
  0.6 49.0 %copy-start.9 = (f32[32]{0:T(128)S(1)}, f32[32]{0:T(128)}, u32[]{:S(2)}) copy-start(f32[32]{0:T(128)} %param.10) | copy-start | bytes 388
  1.4 1.0 copy-start.2
  2.4 47.2 %copy-start.3 = (f32[32,32,128]{2,1,0:T(8,128)S(1)}, f32[32,32,128]{2,1,0:T(8,128)}, u32[]{:S(2)}) copy-start(f32[32,32,128]{2,1,0:T(8,128)} %image.3) | copy-start | bytes 1572868
  3.8 58.7 %copy-start.6 = (s32[92]{0:T(128)S(1)}, s32[92]{0:T(128)}, u32[]{:S(2)}) copy-start(s32[92]{0:T(128)} %slots.7) | copy-start | bytes 1108
  3.8 58.7 %copy-start.8 = (s32[92]{0:T(128)S(1)}, s32[92]{0:T(128)}, u32[]{:S(2)}) copy-start(s32[92]{0:T(128)} %rows.7) | copy-start | bytes 1108
  3.8 16.3 %all-to-all-start = ((bf16[32,32,128]{2,1,0:T(8,128)(2,1)}), bf16[32,32,128]{2,1,0:T(8,128)(2,1)S(1)}, u32[]{:S(2)}, u32[]{:S(2)}) async-start(bf16[32,32,128]{2,1,0:T(8,128)(2,1)} %pick.1), calls=%async_computation | async-start | bytes 524288 | tf_op jit(solution)/shard_map/all_to_all | solution.py:100
  20.1 1.9 %copy-start = (bf16[92,128,128]{2,1,0:T(8,128)(2,1)S(1)}, bf16[92,128,128]{2,1,0:T(8,128)(2,1)}, u32[]{:S(2)}) copy-start(bf16[92,128,128]{2,1,0:T(8,128)(2,1)} %model.15) | copy-start | bytes 9043972
  24.2 38.3 %copy-start.1 = (bf16[92,128,128]{2,1,0:T(8,128)(2,1)S(1)}, bf16[92,128,128]{2,1,0:T(8,128)(2,1)}, u32[]{:S(2)}) copy-start(bf16[92,128,128]{2,1,0:T(8,128)(2,1)} %model.15) | copy-start | bytes 9043972
  27.9 1.9 %collective-permute-start = (bf16[8,32,128]{2,1,0:T(8,128)(2,1)S(1)}, bf16[8,32,128]{2,1,0:T(8,128)(2,1)S(1)}, u32[]{:S(2)}, u32[]{:S(2)}) collective-permute-start(bf16[8,32,128]{2,1,0:T(8,128)(2,1)S(1)} %get-tuple-element.26), channel_id=1, source_target_pairs={{0,1},{1,0},{2,3},{3,2},{4,5},{5,4},{6,7},{7,6},{8,9},{9,8},{10,11... | collective-permute-start | bytes 196616 | tf_op jit(solution)/shard_map/ppermute | solution.py:97
  27.9 4.5 %collective-permute-start.1 = (bf16[8,32,128]{2,1,0:T(8,128)(2,1)S(1)}, bf16[8,32,128]{2,1,0:T(8,128)(2,1)S(1)}, u32[]{:S(2)}, u32[]{:S(2)}) collective-permute-start(bf16[8,32,128]{2,1,0:T(8,128)(2,1)S(1)} %get-tuple-element.27), channel_id=1, source_target_pairs={{0,2},{1,3},{2,0},{3,1},{4,6},{5,7},{6,4},{7,5},{8,10},{9,11},{10,... | collective-permute-start | bytes 196616 | tf_op jit(solution)/shard_map/ppermute | solution.py:97
  29.4 4.1 %collective-permute-start.2 = (bf16[8,32,128]{2,1,0:T(8,128)(2,1)S(1)}, bf16[8,32,128]{2,1,0:T(8,128)(2,1)S(1)}, u32[]{:S(2)}, u32[]{:S(2)}) collective-permute-start(bf16[8,32,128]{2,1,0:T(8,128)(2,1)S(1)} %get-tuple-element.28), channel_id=1, source_target_pairs={{0,3},{1,2},{2,1},{3,0},{4,7},{5,6},{6,5},{7,4},{8,11},{9,10},{10,... | collective-permute-start | bytes 196616 | tf_op jit(solution)/shard_map/ppermute | solution.py:97
  43.8 4.4 %collective-permute-start.5 = (bf16[8,32,128]{2,1,0:T(8,128)(2,1)S(1)}, bf16[8,32,128]{2,1,0:T(8,128)(2,1)S(1)}, u32[]{:S(2)}, u32[]{:S(2)}) collective-permute-start(bf16[8,32,128]{2,1,0:T(8,128)(2,1)S(1)} %all_to_all.40.refs_0_), channel_id=1, source_target_pairs={{0,3},{1,2},{2,1},{3,0},{4,7},{5,6},{6,5},{7,4},{8,11},{9,10},{10,... | collective-permute-start | bytes 196616 | tf_op jit(solution)/shard_map/ppermute | solution.py:97
  43.8 5.8 %collective-permute-start.4 = (bf16[8,32,128]{2,1,0:T(8,128)(2,1)S(1)}, bf16[8,32,128]{2,1,0:T(8,128)(2,1)S(1)}, u32[]{:S(2)}, u32[]{:S(2)}) collective-permute-start(bf16[8,32,128]{2,1,0:T(8,128)(2,1)S(1)} %all_to_all.40.refs_0_), channel_id=1, source_target_pairs={{0,2},{1,3},{2,0},{3,1},{4,6},{5,7},{6,4},{7,5},{8,10},{9,11},{10,... | collective-permute-start | bytes 196616 | tf_op jit(solution)/shard_map/ppermute | solution.py:97
  45.3 4.3 %collective-permute-start.3 = (bf16[8,32,128]{2,1,0:T(8,128)(2,1)S(1)}, bf16[8,32,128]{2,1,0:T(8,128)(2,1)S(1)}, u32[]{:S(2)}, u32[]{:S(2)}) collective-permute-start(bf16[8,32,128]{2,1,0:T(8,128)(2,1)S(1)} %all_to_all.40.refs_0_), channel_id=1, source_target_pairs={{0,1},{1,0},{2,3},{3,2},{4,5},{5,4},{6,7},{7,6},{8,9},{9,8},{10,11... | collective-permute-start | bytes 196616 | tf_op jit(solution)/shard_map/ppermute | solution.py:97
  66.2 1.9 %collective-permute-start.6 = (bf16[8,32,128]{2,1,0:T(8,128)(2,1)S(1)}, bf16[8,32,128]{2,1,0:T(8,128)(2,1)S(1)}, u32[]{:S(2)}, u32[]{:S(2)}) collective-permute-start(bf16[8,32,128]{2,1,0:T(8,128)(2,1)S(1)} %get-tuple-element.32), channel_id=1, source_target_pairs={{0,1},{1,0},{2,3},{3,2},{4,5},{5,4},{6,7},{7,6},{8,9},{9,8},{10,11... | collective-permute-start | bytes 196616 | tf_op jit(solution)/shard_map/ppermute | solution.py:97
  66.2 4.9 %collective-permute-start.7 = (bf16[8,32,128]{2,1,0:T(8,128)(2,1)S(1)}, bf16[8,32,128]{2,1,0:T(8,128)(2,1)S(1)}, u32[]{:S(2)}, u32[]{:S(2)}) collective-permute-start(bf16[8,32,128]{2,1,0:T(8,128)(2,1)S(1)} %get-tuple-element.33), channel_id=1, source_target_pairs={{0,2},{1,3},{2,0},{3,1},{4,6},{5,7},{6,4},{7,5},{8,10},{9,11},{10,... | collective-permute-start | bytes 196616 | tf_op jit(solution)/shard_map/ppermute | solution.py:97
  66.8 4.9 %collective-permute-start.8 = (bf16[8,32,128]{2,1,0:T(8,128)(2,1)S(1)}, bf16[8,32,128]{2,1,0:T(8,128)(2,1)S(1)}, u32[]{:S(2)}, u32[]{:S(2)}) collective-permute-start(bf16[8,32,128]{2,1,0:T(8,128)(2,1)S(1)} %get-tuple-element.34), channel_id=1, source_target_pairs={{0,3},{1,2},{2,1},{3,0},{4,7},{5,6},{6,5},{7,4},{8,11},{9,10},{10,... | collective-permute-start | bytes 196616 | tf_op jit(solution)/shard_map/ppermute | solution.py:97
  82.0 3.8 %collective-permute-start.11 = (bf16[8,32,128]{2,1,0:T(8,128)(2,1)S(1)}, bf16[8,32,128]{2,1,0:T(8,128)(2,1)S(1)}, u32[]{:S(2)}, u32[]{:S(2)}) collective-permute-start(bf16[8,32,128]{2,1,0:T(8,128)(2,1)S(1)} %all_to_all.42.refs_0_), channel_id=1, source_target_pairs={{0,3},{1,2},{2,1},{3,0},{4,7},{5,6},{6,5},{7,4},{8,11},{9,10},{10,... | collective-permute-start | bytes 196616 | tf_op jit(solution)/shard_map/ppermute | solution.py:97
  82.0 4.9 %collective-permute-start.10 = (bf16[8,32,128]{2,1,0:T(8,128)(2,1)S(1)}, bf16[8,32,128]{2,1,0:T(8,128)(2,1)S(1)}, u32[]{:S(2)}, u32[]{:S(2)}) collective-permute-start(bf16[8,32,128]{2,1,0:T(8,128)(2,1)S(1)} %all_to_all.42.refs_0_), channel_id=1, source_target_pairs={{0,2},{1,3},{2,0},{3,1},{4,6},{5,7},{6,4},{7,5},{8,10},{9,11},{10,... | collective-permute-start | bytes 196616 | tf_op jit(solution)/shard_map/ppermute | solution.py:97
  82.7 4.2 %collective-permute-start.9 = (bf16[8,32,128]{2,1,0:T(8,128)(2,1)S(1)}, bf16[8,32,128]{2,1,0:T(8,128)(2,1)S(1)}, u32[]{:S(2)}, u32[]{:S(2)}) collective-permute-start(bf16[8,32,128]{2,1,0:T(8,128)(2,1)S(1)} %all_to_all.42.refs_0_), channel_id=1, source_target_pairs={{0,1},{1,0},{2,3},{3,2},{4,5},{5,4},{6,7},{7,6},{8,9},{9,8},{10,11... | collective-permute-start | bytes 196616 | tf_op jit(solution)/shard_map/ppermute | solution.py:97
  103.5 1.9 %collective-permute-start.12 = (bf16[8,32,128]{2,1,0:T(8,128)(2,1)S(1)}, bf16[8,32,128]{2,1,0:T(8,128)(2,1)S(1)}, u32[]{:S(2)}, u32[]{:S(2)}) collective-permute-start(bf16[8,32,128]{2,1,0:T(8,128)(2,1)S(1)} %get-tuple-element.38), channel_id=1, source_target_pairs={{0,1},{1,0},{2,3},{3,2},{4,5},{5,4},{6,7},{7,6},{8,9},{9,8},{10,11... | collective-permute-start | bytes 196616 | tf_op jit(solution)/shard_map/ppermute | solution.py:97
  103.5 4.7 %collective-permute-start.13 = (bf16[8,32,128]{2,1,0:T(8,128)(2,1)S(1)}, bf16[8,32,128]{2,1,0:T(8,128)(2,1)S(1)}, u32[]{:S(2)}, u32[]{:S(2)}) collective-permute-start(bf16[8,32,128]{2,1,0:T(8,128)(2,1)S(1)} %get-tuple-element.39), channel_id=1, source_target_pairs={{0,2},{1,3},{2,0},{3,1},{4,6},{5,7},{6,4},{7,5},{8,10},{9,11},{10,... | collective-permute-start | bytes 196616 | tf_op jit(solution)/shard_map/ppermute | solution.py:97
  104.9 4.3 %collective-permute-start.14 = (bf16[8,32,128]{2,1,0:T(8,128)(2,1)S(1)}, bf16[8,32,128]{2,1,0:T(8,128)(2,1)S(1)}, u32[]{:S(2)}, u32[]{:S(2)}) collective-permute-start(bf16[8,32,128]{2,1,0:T(8,128)(2,1)S(1)} %get-tuple-element.40), channel_id=1, source_target_pairs={{0,3},{1,2},{2,1},{3,0},{4,7},{5,6},{6,5},{7,4},{8,11},{9,10},{10,... | collective-permute-start | bytes 196616 | tf_op jit(solution)/shard_map/ppermute | solution.py:97
  119.5 4.4 %collective-permute-start.17 = (bf16[8,32,128]{2,1,0:T(8,128)(2,1)S(1)}, bf16[8,32,128]{2,1,0:T(8,128)(2,1)S(1)}, u32[]{:S(2)}, u32[]{:S(2)}) collective-permute-start(bf16[8,32,128]{2,1,0:T(8,128)(2,1)S(1)} %all_to_all.44.refs_0_), channel_id=1, source_target_pairs={{0,3},{1,2},{2,1},{3,0},{4,7},{5,6},{6,5},{7,4},{8,11},{9,10},{10,... | collective-permute-start | bytes 196616 | tf_op jit(solution)/shard_map/ppermute | solution.py:97
  119.5 5.3 %collective-permute-start.16 = (bf16[8,32,128]{2,1,0:T(8,128)(2,1)S(1)}, bf16[8,32,128]{2,1,0:T(8,128)(2,1)S(1)}, u32[]{:S(2)}, u32[]{:S(2)}) collective-permute-start(bf16[8,32,128]{2,1,0:T(8,128)(2,1)S(1)} %all_to_all.44.refs_0_), channel_id=1, source_target_pairs={{0,2},{1,3},{2,0},{3,1},{4,6},{5,7},{6,4},{7,5},{8,10},{9,11},{10,... | collective-permute-start | bytes 196616 | tf_op jit(solution)/shard_map/ppermute | solution.py:97
  120.7 4.1 %collective-permute-start.15 = (bf16[8,32,128]{2,1,0:T(8,128)(2,1)S(1)}, bf16[8,32,128]{2,1,0:T(8,128)(2,1)S(1)}, u32[]{:S(2)}, u32[]{:S(2)}) collective-permute-start(bf16[8,32,128]{2,1,0:T(8,128)(2,1)S(1)} %all_to_all.44.refs_0_), channel_id=1, source_target_pairs={{0,1},{1,0},{2,3},{3,2},{4,5},{5,4},{6,7},{7,6},{8,9},{9,8},{10,11... | collective-permute-start | bytes 196616 | tf_op jit(solution)/shard_map/ppermute | solution.py:97
  141.3 1.9 %collective-permute-start.18 = (bf16[8,32,128]{2,1,0:T(8,128)(2,1)S(1)}, bf16[8,32,128]{2,1,0:T(8,128)(2,1)S(1)}, u32[]{:S(2)}, u32[]{:S(2)}) collective-permute-start(bf16[8,32,128]{2,1,0:T(8,128)(2,1)S(1)} %get-tuple-element.44), channel_id=1, source_target_pairs={{0,1},{1,0},{2,3},{3,2},{4,5},{5,4},{6,7},{7,6},{8,9},{9,8},{10,11... | collective-permute-start | bytes 196616 | tf_op jit(solution)/shard_map/ppermute | solution.py:97
  141.3 4.9 %collective-permute-start.19 = (bf16[8,32,128]{2,1,0:T(8,128)(2,1)S(1)}, bf16[8,32,128]{2,1,0:T(8,128)(2,1)S(1)}, u32[]{:S(2)}, u32[]{:S(2)}) collective-permute-start(bf16[8,32,128]{2,1,0:T(8,128)(2,1)S(1)} %get-tuple-element.45), channel_id=1, source_target_pairs={{0,2},{1,3},{2,0},{3,1},{4,6},{5,7},{6,4},{7,5},{8,10},{9,11},{10,... | collective-permute-start | bytes 196616 | tf_op jit(solution)/shard_map/ppermute | solution.py:97
  142.2 4.7 %collective-permute-start.20 = (bf16[8,32,128]{2,1,0:T(8,128)(2,1)S(1)}, bf16[8,32,128]{2,1,0:T(8,128)(2,1)S(1)}, u32[]{:S(2)}, u32[]{:S(2)}) collective-permute-start(bf16[8,32,128]{2,1,0:T(8,128)(2,1)S(1)} %get-tuple-element.46), channel_id=1, source_target_pairs={{0,3},{1,2},{2,1},{3,0},{4,7},{5,6},{6,5},{7,4},{8,11},{9,10},{10,... | collective-permute-start | bytes 196616 | tf_op jit(solution)/shard_map/ppermute | solution.py:97
  157.1 4.0 %collective-permute-start.23 = (bf16[8,32,128]{2,1,0:T(8,128)(2,1)S(1)}, bf16[8,32,128]{2,1,0:T(8,128)(2,1)S(1)}, u32[]{:S(2)}, u32[]{:S(2)}) collective-permute-start(bf16[8,32,128]{2,1,0:T(8,128)(2,1)S(1)} %all_to_all.46.refs_0_), channel_id=1, source_target_pairs={{0,3},{1,2},{2,1},{3,0},{4,7},{5,6},{6,5},{7,4},{8,11},{9,10},{10,... | collective-permute-start | bytes 196616 | tf_op jit(solution)/shard_map/ppermute | solution.py:97
  157.1 4.9 %collective-permute-start.22 = (bf16[8,32,128]{2,1,0:T(8,128)(2,1)S(1)}, bf16[8,32,128]{2,1,0:T(8,128)(2,1)S(1)}, u32[]{:S(2)}, u32[]{:S(2)}) collective-permute-start(bf16[8,32,128]{2,1,0:T(8,128)(2,1)S(1)} %all_to_all.46.refs_0_), channel_id=1, source_target_pairs={{0,2},{1,3},{2,0},{3,1},{4,6},{5,7},{6,4},{7,5},{8,10},{9,11},{10,... | collective-permute-start | bytes 196616 | tf_op jit(solution)/shard_map/ppermute | solution.py:97
  158.0 4.1 %collective-permute-start.21 = (bf16[8,32,128]{2,1,0:T(8,128)(2,1)S(1)}, bf16[8,32,128]{2,1,0:T(8,128)(2,1)S(1)}, u32[]{:S(2)}, u32[]{:S(2)}) collective-permute-start(bf16[8,32,128]{2,1,0:T(8,128)(2,1)S(1)} %all_to_all.46.refs_0_), channel_id=1, source_target_pairs={{0,1},{1,0},{2,3},{3,2},{4,5},{5,4},{6,7},{7,6},{8,9},{9,8},{10,11... | collective-permute-start | bytes 196616 | tf_op jit(solution)/shard_map/ppermute | solution.py:97
  (3 other events, 2.2 us)

commit v4 on v3

v4 whole, which is shorter than its diff:
```python
import functools

import jax
import jax.numpy as jnp
from jax import lax
from jax.experimental import pallas as pl
from jax.experimental.pallas import tpu as pltpu
from jax.sharding import PartitionSpec as P

ITERATIONS = 4


VMEM = pl.BlockSpec(memory_space=pltpu.VMEM)
SMEM = pl.BlockSpec(memory_space=pltpu.SMEM)
PARAMS = pltpu.CompilerParams(vmem_limit_bytes=32 * 1024 * 1024)


def model_kernel(chan_count, places, rows, model, measured, *refs):
    arrived = refs[:chan_count]
    own, *sent = refs[chan_count : 2 * chan_count]
    residual, tiles, narrow, sums = refs[2 * chan_count :]
    wide = own.shape[0]
    count = model.shape[0]
    for d, piece in enumerate(arrived):
        tiles[d * wide : (d + 1) * wide] = piece[...]
    residual[...] = measured[...]
    sums[...] = jnp.zeros_like(sums)
    for k in range(count):
        part = lax.dot_general(
            tiles[places[k]],
            model[k],
            (((1,), (1,)), ((), ())),
            preferred_element_type=jnp.float32,
        )
        residual[rows[k]] -= part
    narrow[...] = residual[...].astype(jnp.bfloat16)
    for k in range(count):
        part = jnp.dot(narrow[rows[k]], model[k], preferred_element_type=jnp.float32)
        sums[places[k]] += part
    own[...] = sums[:wide]
    for d, out in enumerate(sent, 1):
        out[...] = sums[d * wide : (d + 1) * wide].astype(jnp.bfloat16)


def reduce_kernel(share, own, *refs):
    received, outs = refs[:-share], refs[-share:]
    total = own[...]
    for piece in received:
        total = total + piece[...].astype(jnp.float32)
    capacity = total.shape[0] // share
    for r, out in enumerate(outs):
        out[...] = total[r * capacity : (r + 1) * capacity].astype(jnp.bfloat16)


def tile_of(ids, table, share, d, r, s):
    return jnp.maximum(table[ids[0] ^ ((ids[1] ^ d) * share + r), s], 0)


def pick_kernel(ids, table, image, *outs):
    for r, out in enumerate(outs):
        for s in range(table.shape[1]):
            tile = tile_of(ids, table, len(outs), 0, r, s)
            out[s] = image[tile].astype(jnp.bfloat16)


def update_kernel(chan_count, ids, table, gains, image, *refs):
    received = refs[:chan_count]
    estimate, *outs = refs[chan_count:-1]
    gradient = refs[-1]
    vox_count, capacity = table.shape
    share = vox_count // chan_count
    gradient[...] = jnp.zeros_like(gradient)
    for d in range(chan_count):
        for r in range(share):
            for s in range(capacity):
                tile = tile_of(ids, table, share, d, r, s)
                gradient[tile] += received[d][r * capacity + s].astype(jnp.float32)
    estimate[...] = jnp.maximum(image[...] + gains[...][None] * gradient[...], 0.0)
    if outs:
        pick_kernel(ids, table, estimate, *outs)


def shards(model_blocks, start_image, measured, step_size, sent_tiles, block_rows, block_slots):
    vox_count = lax.axis_size("vox")
    chan_count = lax.axis_size("chan")
    vox, chan = lax.axis_index("vox"), lax.axis_index("chan")
    table = sent_tiles[0]
    capacity = table.shape[1]
    share = vox_count // chan_count
    tile_count, wave_count, width = start_image.shape
    row_count = measured.shape[0]
    slot_count = vox_count * capacity
    wide = share * capacity
    tile = (wave_count, width)
    ids = jnp.stack([vox, chan]).astype(jnp.int32)
    partner, slot = (block_slots // capacity) ^ vox, block_slots % capacity
    places = (((partner // share) ^ chan) * share + partner % share) * capacity + slot
    gains = jnp.broadcast_to(step_size[:, None], tile)

    def shape(count, dtype):
        return jax.ShapeDtypeStruct((count, *tile), dtype)

    def swap(array, d):
        pairs = [(i, i ^ d) for i in range(chan_count)]
        return lax.ppermute(array, "chan", pairs) if d else array

    def exchange(pieces):
        arrived = []
        for r, piece in enumerate(pieces):
            pairs = [
                (v * chan_count + c, (v ^ (c * share + r)) * chan_count + c)
                for v in range(vox_count)
                for c in range(chan_count)
            ]
            arrived.append(lax.ppermute(piece, ("vox", "chan"), pairs))
        joined = jnp.concatenate(arrived)
        return [swap(joined, d) for d in range(chan_count)]

    apply_model = pl.pallas_call(
        functools.partial(model_kernel, chan_count),
        out_shape=(
            shape(wide, jnp.float32),
            *[shape(wide, jnp.bfloat16)] * (chan_count - 1),
            shape(row_count, jnp.float32),
        ),
        in_specs=[SMEM, SMEM, VMEM, VMEM] + [VMEM] * chan_count,
        out_specs=[VMEM] * (chan_count + 1),
        scratch_shapes=[
            pltpu.VMEM((slot_count, *tile), jnp.bfloat16),
            pltpu.VMEM((row_count, *tile), jnp.bfloat16),
            pltpu.VMEM((slot_count, *tile), jnp.float32),
        ],
        compiler_params=PARAMS,
        name="model",
    )
    reduce_parts = pl.pallas_call(
        functools.partial(reduce_kernel, share),
        out_shape=[shape(capacity, jnp.bfloat16)] * share,
        in_specs=[VMEM] * chan_count,
        out_specs=[VMEM] * share,
        compiler_params=PARAMS,
        name="reduce",
    )
    pick = pl.pallas_call(
        pick_kernel,
        out_shape=[shape(capacity, jnp.bfloat16)] * share,
        in_specs=[SMEM, SMEM, VMEM],
        out_specs=[VMEM] * share,
        compiler_params=PARAMS,
        name="pick",
    )

    def update(last):
        outs = [] if last else [shape(capacity, jnp.bfloat16)] * share
        return pl.pallas_call(
            functools.partial(update_kernel, chan_count),
            out_shape=[shape(tile_count, jnp.float32)] + outs,
            in_specs=[SMEM, SMEM, VMEM, VMEM] + [VMEM] * chan_count,
            out_specs=[VMEM] * (len(outs) + 1),
            scratch_shapes=[pltpu.VMEM((tile_count, *tile), jnp.float32)],
            compiler_params=PARAMS,
            name="update",
        )

    estimate = start_image
    outgoing = pick(ids, table, start_image)
    for iteration in range(ITERATIONS):
        own, *partial, residual = apply_model(
            places, block_rows, model_blocks, measured, *exchange(outgoing)
        )
        totals = reduce_parts(own, *[swap(piece, d) for d, piece in enumerate(partial, 1)])
        estimate, *outgoing = update(iteration == ITERATIONS - 1)(
            ids, table, gains, estimate, *exchange(totals)
        )
    return (estimate, residual)


def solution(mesh):
    in_specs = (
        P(("vox", "chan"), None, None),
        P("vox", None, None),
        P(("vox", "chan"), None, None),
        P(),
        P("vox", None, None),
        P(("vox", "chan")),
        P(("vox", "chan")),
    )
    out_specs = (P("vox", None, None), P(("vox", "chan"), None, None))
    return jax.shard_map(shards, mesh=mesh, in_specs=in_specs, out_specs=out_specs, check_vma=False)
```

time: 164 us -> 169 us (1.030)
  blocking collectives: 76.8 us -> 0 us
  starting transfers between devices: 22.3 us -> 74.1 us
  waiting for transfers between devices: 36.6 us -> 68.1 us
    all_to_all x7 -> x0, blocking collectives: 76.8 us -> none  [exchange(): return lax.all_to_all(array, 'vox', split_axis=0, concat_axis=0, tiled=True)]
    ppermute x24 -> x52, starting transfers between devices: 14.9 us -> 74.1 us  [the longest x36 58.1 us: swap(): return lax.ppermute(array, 'chan', pairs) if d else array]
    ppermute x24 -> x52, waiting for transfers between devices: 28.4 us -> 68.1 us  [the longest x36 45.8 us: swap(): return lax.ppermute(array, 'chan', pairs) if d else array]
    all_to_all x1 -> x0, waiting for transfers between devices: 8.25 us -> none  [exchange(): return lax.all_to_all(array, 'vox', split_axis=0, concat_axis=0, tiled=True)]
    all_to_all x1 -> x0, starting transfers between devices: 7.38 us -> none  [exchange(): return lax.all_to_all(array, 'vox', split_axis=0, concat_axis=0, tiled=True)]
    unnamed x20 -> x24, local copies, waits for them, and re-layouts: 5.13 us -> 4.5 us
  transfers between devices with their start and end apart: 25 -> 52, of which waited for: 17 -> 32; matrix products, arithmetic and copies ran while one was open for 0% -> 0% of each run, Pallas kernels for 0% -> 0%
where the time goes in v4:
time: 169 us
  starting transfers between devices  74.1 us (44%)
  waiting for transfers between devices  68.1 us (40%)
  Pallas kernels  19.9 us (12%)
  local copies, waits for them, and re-layouts  5.4 us (3%)
    ppermute x36, starting transfers between devices, swap(): return lax.ppermute(array, 'chan', pairs) if d else array  58.1 us
    ppermute x36, waiting for transfers between devices, swap(): return lax.ppermute(array, 'chan', pairs) if d else array  45.8 us
    ppermute x16, waiting for transfers between devices, exchange(): arrived.append(lax.ppermute(piece, ('vox', 'chan'), pairs))  22.2 us
    ppermute x16, starting transfers between devices, exchange(): arrived.append(lax.ppermute(piece, ('vox', 'chan'), pairs))  16 us
    pallas_call x4, Pallas kernels, shards(): apply_model(places, block_rows, model_blocks, measured, *exchange(outgoing))  14.7 us
    unnamed x24, local copies, waits for them, and re-layouts  4.5 us
    pallas_call x4, Pallas kernels, shards(): update(iteration == ITERATIONS - 1)  4.46 us
  transfers between devices with their start and end apart: 52, of which 32 were waited for; matrix products, arithmetic and copies ran while one was open for 0% of the time, Pallas kernels for 0%

profile of v4, /device:TPU:0, one launch (start us, length us, event | category | flops | bytes accessed | tf_op | source)
XLA Modules:
  0.0 169.0 jit_solution(10994215260800311507)
XLA Ops:
  3.8 3.0 %collective-permute-start.1 = (bf16[4,32,128]{2,1,0:T(8,128)(2,1)S(1)}, bf16[4,32,128]{2,1,0:T(8,128)(2,1)S(1)}, u32[]{:S(2)}, u32[]{:S(2)}) collective-permute-start(bf16[4,32,128]{2,1,0:T(8,128)(2,1)S(1)} %get-tuple-element.39), channel_id=1, source_target_pairs={{0,4},{1,13},{2,22},{3,31},{4,0},{5,9},{6,18},{7,27},{8,12},{9,5},... | collective-permute-start | bytes 98312 | tf_op jit(solution)/shard_map/ppermute | solution.py:115
  6.9 1.9 %collective-permute-done.1 = bf16[4,32,128]{2,1,0:T(8,128)(2,1)S(1)} collective-permute-done((bf16[4,32,128]{2,1,0:T(8,128)(2,1)S(1)}, bf16[4,32,128]{2,1,0:T(8,128)(2,1)S(1)}, u32[]{:S(2)}, u32[]{:S(2)}) %collective-permute-start.1) | collective-permute-done | bytes 32800 | tf_op jit(solution)/shard_map/ppermute | solution.py:115
  8.8 7.6 %collective-permute-start.4 = (bf16[8,32,128]{2,1,0:T(8,128)(2,1)S(1)}, bf16[8,32,128]{2,1,0:T(8,128)(2,1)S(1)}, u32[]{:S(2)}, u32[]{:S(2)}) collective-permute-start(bf16[8,32,128]{2,1,0:T(8,128)(2,1)S(1)} %constant_dynamic-update-slice_fusion.refs_0_), channel_id=1, source_target_pairs={{0,3},{1,2},{2,1},{3,0},{4,7},{5,6},{6,5},{7,4},{8,11},{9,10},{10,... | collective-permute-start | bytes 196616 | tf_op jit(solution)/shard_map/ppermute | solution.py:105
  24.0 3.7 %model.8 = (f32[8,32,128]{2,1,0:T(8,128)S(1)}, bf16[8,32,128]{2,1,0:T(8,128)(2,1)S(1)}, bf16[8,32,128]{2,1,0:T(8,128)(2,1)S(1)}, bf16[8,32,128]{2,1,0:T(8,128)(2,1)S(1)}, f32[8,32,128]{2,1,0:T(8,128)}) custom-call(s32[92]{0:T(128)S(1)} %fusion.1.places, s32[92]{0:T(128)S(1)} %copy-done.5, bf16[92,128,128]{2,1,0:T(8,128)(2,1)S(1)} %copy-done, ...), custom_call_target="tpu_custom_call" | custom-call | tf_op jit(solution)/shard_map/model/pallas_call | solution.py:168
  29.6 2.6 %collective-permute-done.6.refs_1_ = bf16[8,32,128]{2,1,0:T(8,128)(2,1)S(1)} collective-permute-done((bf16[8,32,128]{2,1,0:T(8,128)(2,1)S(1)}, bf16[8,32,128]{2,1,0:T(8,128)(2,1)S(1)}, u32[]{:S(2)}, u32[]{:S(2)}) %collective-permute-start.6) | collective-permute-done | bytes 65568 | tf_op jit(solution)/shard_map/ppermute | solution.py:105
  35.7 2.4 %collective-permute-done.9 = bf16[4,32,128]{2,1,0:T(8,128)(2,1)S(1)} collective-permute-done((bf16[4,32,128]{2,1,0:T(8,128)(2,1)S(1)}, bf16[4,32,128]{2,1,0:T(8,128)(2,1)S(1)}, u32[]{:S(2)}, u32[]{:S(2)}) %collective-permute-start.9) | collective-permute-done | bytes 32800 | tf_op jit(solution)/shard_map/ppermute | solution.py:115
  38.1 5.7 %collective-permute-start.12 = (bf16[8,32,128]{2,1,0:T(8,128)(2,1)S(1)}, bf16[8,32,128]{2,1,0:T(8,128)(2,1)S(1)}, u32[]{:S(2)}, u32[]{:S(2)}) collective-permute-start(bf16[8,32,128]{2,1,0:T(8,128)(2,1)S(1)} %constant_dynamic-update-slice_fusion.2.refs_0_), channel_id=1, source_target_pairs={{0,3},{1,2},{2,1},{3,0},{4,7},{5,6},{6,5},{7,4},{8,11},{9,10},{10,... | collective-permute-start | bytes 196616 | tf_op jit(solution)/shard_map/ppermute | solution.py:105
  44.0 2.4 %collective-permute-done.12.refs_3_ = bf16[8,32,128]{2,1,0:T(8,128)(2,1)S(1)} collective-permute-done((bf16[8,32,128]{2,1,0:T(8,128)(2,1)S(1)}, bf16[8,32,128]{2,1,0:T(8,128)(2,1)S(1)}, u32[]{:S(2)}, u32[]{:S(2)}) %collective-permute-start.12) | collective-permute-done | bytes 65568 | tf_op jit(solution)/shard_map/ppermute | solution.py:105
  50.5 3.3 %collective-permute-done.14 = bf16[4,32,128]{2,1,0:T(8,128)(2,1)S(1)} collective-permute-done((bf16[4,32,128]{2,1,0:T(8,128)(2,1)S(1)}, bf16[4,32,128]{2,1,0:T(8,128)(2,1)S(1)}, u32[]{:S(2)}, u32[]{:S(2)}) %collective-permute-start.14) | collective-permute-done | bytes 32800 | tf_op jit(solution)/shard_map/ppermute | solution.py:115
  53.8 4.5 %collective-permute-start.17 = (bf16[8,32,128]{2,1,0:T(8,128)(2,1)S(1)}, bf16[8,32,128]{2,1,0:T(8,128)(2,1)S(1)}, u32[]{:S(2)}, u32[]{:S(2)}) collective-permute-start(bf16[8,32,128]{2,1,0:T(8,128)(2,1)S(1)} %constant_dynamic-update-slice_fusion.4.refs_0_), channel_id=1, source_target_pairs={{0,3},{1,2},{2,1},{3,0},{4,7},{5,6},{6,5},{7,4},{8,11},{9,10},{10,... | collective-permute-start | bytes 196616 | tf_op jit(solution)/shard_map/ppermute | solution.py:105
  60.2 2.7 %collective-permute-done.16.refs_2_ = bf16[8,32,128]{2,1,0:T(8,128)(2,1)S(1)} collective-permute-done((bf16[8,32,128]{2,1,0:T(8,128)(2,1)S(1)}, bf16[8,32,128]{2,1,0:T(8,128)(2,1)S(1)}, u32[]{:S(2)}, u32[]{:S(2)}) %collective-permute-start.16) | collective-permute-done | bytes 65568 | tf_op jit(solution)/shard_map/ppermute | solution.py:105
  62.9 3.7 %model.10 = (f32[8,32,128]{2,1,0:T(8,128)S(1)}, bf16[8,32,128]{2,1,0:T(8,128)(2,1)S(1)}, bf16[8,32,128]{2,1,0:T(8,128)(2,1)S(1)}, bf16[8,32,128]{2,1,0:T(8,128)(2,1)S(1)}, f32[8,32,128]{2,1,0:T(8,128)}) custom-call(s32[92]{0:T(128)S(1)} %fusion.1.places, s32[92]{0:T(128)S(1)} %copy-done.6, bf16[92,128,128]{2,1,0:T(8,128)(2,1)S(1)} %copy-done.1, ...), custom_call_target="tpu_custom_call" | custom-call | tf_op jit(solution)/shard_map/model/pallas_call | solution.py:168
  68.4 2.6 %collective-permute-done.19.refs_1_ = bf16[8,32,128]{2,1,0:T(8,128)(2,1)S(1)} collective-permute-done((bf16[8,32,128]{2,1,0:T(8,128)(2,1)S(1)}, bf16[8,32,128]{2,1,0:T(8,128)(2,1)S(1)}, u32[]{:S(2)}, u32[]{:S(2)}) %collective-permute-start.19) | collective-permute-done | bytes 65568 | tf_op jit(solution)/shard_map/ppermute | solution.py:105
  74.6 2.4 %collective-permute-done.22 = bf16[4,32,128]{2,1,0:T(8,128)(2,1)S(1)} collective-permute-done((bf16[4,32,128]{2,1,0:T(8,128)(2,1)S(1)}, bf16[4,32,128]{2,1,0:T(8,128)(2,1)S(1)}, u32[]{:S(2)}, u32[]{:S(2)}) %collective-permute-start.22) | collective-permute-done | bytes 32800 | tf_op jit(solution)/shard_map/ppermute | solution.py:115
  77.0 5.9 %collective-permute-start.25 = (bf16[8,32,128]{2,1,0:T(8,128)(2,1)S(1)}, bf16[8,32,128]{2,1,0:T(8,128)(2,1)S(1)}, u32[]{:S(2)}, u32[]{:S(2)}) collective-permute-start(bf16[8,32,128]{2,1,0:T(8,128)(2,1)S(1)} %constant_dynamic-update-slice_fusion.6.refs_0_), channel_id=1, source_target_pairs={{0,3},{1,2},{2,1},{3,0},{4,7},{5,6},{6,5},{7,4},{8,11},{9,10},{10,... | collective-permute-start | bytes 196616 | tf_op jit(solution)/shard_map/ppermute | solution.py:105
  85.3 2.5 %collective-permute-done.24.refs_2_ = bf16[8,32,128]{2,1,0:T(8,128)(2,1)S(1)} collective-permute-done((bf16[8,32,128]{2,1,0:T(8,128)(2,1)S(1)}, bf16[8,32,128]{2,1,0:T(8,128)(2,1)S(1)}, u32[]{:S(2)}, u32[]{:S(2)}) %collective-permute-start.24) | collective-permute-done | bytes 65568 | tf_op jit(solution)/shard_map/ppermute | solution.py:105
  89.9 3.4 %collective-permute-done.27 = bf16[4,32,128]{2,1,0:T(8,128)(2,1)S(1)} collective-permute-done((bf16[4,32,128]{2,1,0:T(8,128)(2,1)S(1)}, bf16[4,32,128]{2,1,0:T(8,128)(2,1)S(1)}, u32[]{:S(2)}, u32[]{:S(2)}) %collective-permute-start.27) | collective-permute-done | bytes 32800 | tf_op jit(solution)/shard_map/ppermute | solution.py:115
  93.3 4.6 %collective-permute-start.30 = (bf16[8,32,128]{2,1,0:T(8,128)(2,1)S(1)}, bf16[8,32,128]{2,1,0:T(8,128)(2,1)S(1)}, u32[]{:S(2)}, u32[]{:S(2)}) collective-permute-start(bf16[8,32,128]{2,1,0:T(8,128)(2,1)S(1)} %constant_dynamic-update-slice_fusion.8.refs_0_), channel_id=1, source_target_pairs={{0,3},{1,2},{2,1},{3,0},{4,7},{5,6},{6,5},{7,4},{8,11},{9,10},{10,... | collective-permute-start | bytes 196616 | tf_op jit(solution)/shard_map/ppermute | solution.py:105
  100.3 2.3 %collective-permute-done.29.refs_2_ = bf16[8,32,128]{2,1,0:T(8,128)(2,1)S(1)} collective-permute-done((bf16[8,32,128]{2,1,0:T(8,128)(2,1)S(1)}, bf16[8,32,128]{2,1,0:T(8,128)(2,1)S(1)}, u32[]{:S(2)}, u32[]{:S(2)}) %collective-permute-start.29) | collective-permute-done | bytes 65568 | tf_op jit(solution)/shard_map/ppermute | solution.py:105
  102.7 3.7 %model.12 = (f32[8,32,128]{2,1,0:T(8,128)S(1)}, bf16[8,32,128]{2,1,0:T(8,128)(2,1)S(1)}, bf16[8,32,128]{2,1,0:T(8,128)(2,1)S(1)}, bf16[8,32,128]{2,1,0:T(8,128)(2,1)S(1)}, f32[8,32,128]{2,1,0:T(8,128)}) custom-call(s32[92]{0:T(128)S(1)} %fusion.1.places, s32[92]{0:T(128)S(1)} %copy-done.6, bf16[92,128,128]{2,1,0:T(8,128)(2,1)S(1)} %copy-done.1, ...), custom_call_target="tpu_custom_call" | custom-call | tf_op jit(solution)/shard_map/model/pallas_call | solution.py:168
  108.2 2.6 %collective-permute-done.32.refs_1_ = bf16[8,32,128]{2,1,0:T(8,128)(2,1)S(1)} collective-permute-done((bf16[8,32,128]{2,1,0:T(8,128)(2,1)S(1)}, bf16[8,32,128]{2,1,0:T(8,128)(2,1)S(1)}, u32[]{:S(2)}, u32[]{:S(2)}) %collective-permute-start.32) | collective-permute-done | bytes 65568 | tf_op jit(solution)/shard_map/ppermute | solution.py:105
  114.3 2.5 %collective-permute-done.35 = bf16[4,32,128]{2,1,0:T(8,128)(2,1)S(1)} collective-permute-done((bf16[4,32,128]{2,1,0:T(8,128)(2,1)S(1)}, bf16[4,32,128]{2,1,0:T(8,128)(2,1)S(1)}, u32[]{:S(2)}, u32[]{:S(2)}) %collective-permute-start.35) | collective-permute-done | bytes 32800 | tf_op jit(solution)/shard_map/ppermute | solution.py:115
  116.8 5.9 %collective-permute-start.38 = (bf16[8,32,128]{2,1,0:T(8,128)(2,1)S(1)}, bf16[8,32,128]{2,1,0:T(8,128)(2,1)S(1)}, u32[]{:S(2)}, u32[]{:S(2)}) collective-permute-start(bf16[8,32,128]{2,1,0:T(8,128)(2,1)S(1)} %constant_dynamic-update-slice_fusion.10.refs_0_), channel_id=1, source_target_pairs={{0,3},{1,2},{2,1},{3,0},{4,7},{5,6},{6,5},{7,4},{8,11},{9,10},{10,... | collective-permute-start | bytes 196616 | tf_op jit(solution)/shard_map/ppermute | solution.py:105
  124.9 2.6 %collective-permute-done.37.refs_2_ = bf16[8,32,128]{2,1,0:T(8,128)(2,1)S(1)} collective-permute-done((bf16[8,32,128]{2,1,0:T(8,128)(2,1)S(1)}, bf16[8,32,128]{2,1,0:T(8,128)(2,1)S(1)}, u32[]{:S(2)}, u32[]{:S(2)}) %collective-permute-start.37) | collective-permute-done | bytes 65568 | tf_op jit(solution)/shard_map/ppermute | solution.py:105
  129.9 3.4 %collective-permute-done.40 = bf16[4,32,128]{2,1,0:T(8,128)(2,1)S(1)} collective-permute-done((bf16[4,32,128]{2,1,0:T(8,128)(2,1)S(1)}, bf16[4,32,128]{2,1,0:T(8,128)(2,1)S(1)}, u32[]{:S(2)}, u32[]{:S(2)}) %collective-permute-start.40) | collective-permute-done | bytes 32800 | tf_op jit(solution)/shard_map/ppermute | solution.py:115
  133.3 3.8 %collective-permute-start.43 = (bf16[8,32,128]{2,1,0:T(8,128)(2,1)S(1)}, bf16[8,32,128]{2,1,0:T(8,128)(2,1)S(1)}, u32[]{:S(2)}, u32[]{:S(2)}) collective-permute-start(bf16[8,32,128]{2,1,0:T(8,128)(2,1)S(1)} %constant_dynamic-update-slice_fusion.12.refs_0_), channel_id=1, source_target_pairs={{0,3},{1,2},{2,1},{3,0},{4,7},{5,6},{6,5},{7,4},{8,11},{9,10},{10,... | collective-permute-start | bytes 196616 | tf_op jit(solution)/shard_map/ppermute | solution.py:105
  139.2 2.7 %collective-permute-done.42.refs_2_ = bf16[8,32,128]{2,1,0:T(8,128)(2,1)S(1)} collective-permute-done((bf16[8,32,128]{2,1,0:T(8,128)(2,1)S(1)}, bf16[8,32,128]{2,1,0:T(8,128)(2,1)S(1)}, u32[]{:S(2)}, u32[]{:S(2)}) %collective-permute-start.42) | collective-permute-done | bytes 65568 | tf_op jit(solution)/shard_map/ppermute | solution.py:105
  141.9 3.7 %model.14 = (f32[8,32,128]{2,1,0:T(8,128)S(1)}, bf16[8,32,128]{2,1,0:T(8,128)(2,1)S(1)}, bf16[8,32,128]{2,1,0:T(8,128)(2,1)S(1)}, bf16[8,32,128]{2,1,0:T(8,128)(2,1)S(1)}, f32[8,32,128]{2,1,0:T(8,128)}) custom-call(s32[92]{0:T(128)S(1)} %fusion.1.places, s32[92]{0:T(128)S(1)} %copy-done.6, bf16[92,128,128]{2,1,0:T(8,128)(2,1)S(1)} %copy-done.1, ...), custom_call_target="tpu_custom_call" | custom-call | tf_op jit(solution)/shard_map/model/pallas_call | solution.py:168
  147.4 2.8 %collective-permute-done.45.refs_1_ = bf16[8,32,128]{2,1,0:T(8,128)(2,1)S(1)} collective-permute-done((bf16[8,32,128]{2,1,0:T(8,128)(2,1)S(1)}, bf16[8,32,128]{2,1,0:T(8,128)(2,1)S(1)}, u32[]{:S(2)}, u32[]{:S(2)}) %collective-permute-start.45) | collective-permute-done | bytes 65568 | tf_op jit(solution)/shard_map/ppermute | solution.py:105
  153.0 3.0 %collective-permute-done.48 = bf16[4,32,128]{2,1,0:T(8,128)(2,1)S(1)} collective-permute-done((bf16[4,32,128]{2,1,0:T(8,128)(2,1)S(1)}, bf16[4,32,128]{2,1,0:T(8,128)(2,1)S(1)}, u32[]{:S(2)}, u32[]{:S(2)}) %collective-permute-start.48) | collective-permute-done | bytes 32800 | tf_op jit(solution)/shard_map/ppermute | solution.py:115
  156.0 6.4 %collective-permute-start.51 = (bf16[8,32,128]{2,1,0:T(8,128)(2,1)S(1)}, bf16[8,32,128]{2,1,0:T(8,128)(2,1)S(1)}, u32[]{:S(2)}, u32[]{:S(2)}) collective-permute-start(bf16[8,32,128]{2,1,0:T(8,128)(2,1)S(1)} %constant_dynamic-update-slice_fusion.14.refs_0_), channel_id=1, source_target_pairs={{0,3},{1,2},{2,1},{3,0},{4,7},{5,6},{6,5},{7,4},{8,11},{9,10},{10,... | collective-permute-start | bytes 196616 | tf_op jit(solution)/shard_map/ppermute | solution.py:105
  164.7 2.6 %collective-permute-done.50.refs_2_ = bf16[8,32,128]{2,1,0:T(8,128)(2,1)S(1)} collective-permute-done((bf16[8,32,128]{2,1,0:T(8,128)(2,1)S(1)}, bf16[8,32,128]{2,1,0:T(8,128)(2,1)S(1)}, u32[]{:S(2)}, u32[]{:S(2)}) %collective-permute-start.50) | collective-permute-done | bytes 65568 | tf_op jit(solution)/shard_map/ppermute | solution.py:105
  (121 shorter events, 55.4 us)
Async XLA Ops:
  3.8 4.9 %collective-permute-start.1 = (bf16[4,32,128]{2,1,0:T(8,128)(2,1)S(1)}, bf16[4,32,128]{2,1,0:T(8,128)(2,1)S(1)}, u32[]{:S(2)}, u32[]{:S(2)}) collective-permute-start(bf16[4,32,128]{2,1,0:T(8,128)(2,1)S(1)} %get-tuple-element.39), channel_id=1, source_target_pairs={{0,4},{1,13},{2,22},{3,31},{4,0},{5,9},{6,18},{7,27},{8,12},{9,5},... | collective-permute-start | bytes 98312 | tf_op jit(solution)/shard_map/ppermute | solution.py:115
  8.8 10.0 %collective-permute-start.4 = (bf16[8,32,128]{2,1,0:T(8,128)(2,1)S(1)}, bf16[8,32,128]{2,1,0:T(8,128)(2,1)S(1)}, u32[]{:S(2)}, u32[]{:S(2)}) collective-permute-start(bf16[8,32,128]{2,1,0:T(8,128)(2,1)S(1)} %constant_dynamic-update-slice_fusion.refs_0_), channel_id=1, source_target_pairs={{0,3},{1,2},{2,1},{3,0},{4,7},{5,6},{6,5},{7,4},{8,11},{9,10},{10,... | collective-permute-start | bytes 196616 | tf_op jit(solution)/shard_map/ppermute | solution.py:105
  16.4 4.3 %collective-permute-start.3 = (bf16[8,32,128]{2,1,0:T(8,128)(2,1)S(1)}, bf16[8,32,128]{2,1,0:T(8,128)(2,1)S(1)}, u32[]{:S(2)}, u32[]{:S(2)}) collective-permute-start(bf16[8,32,128]{2,1,0:T(8,128)(2,1)S(1)} %constant_dynamic-update-slice_fusion.refs_0_), channel_id=1, source_target_pairs={{0,2},{1,3},{2,0},{3,1},{4,6},{5,7},{6,4},{7,5},{8,10},{9,11},{10,... | collective-permute-start | bytes 196616 | tf_op jit(solution)/shard_map/ppermute | solution.py:105
  16.5 4.1 %collective-permute-start.2 = (bf16[8,32,128]{2,1,0:T(8,128)(2,1)S(1)}, bf16[8,32,128]{2,1,0:T(8,128)(2,1)S(1)}, u32[]{:S(2)}, u32[]{:S(2)}) collective-permute-start(bf16[8,32,128]{2,1,0:T(8,128)(2,1)S(1)} %constant_dynamic-update-slice_fusion.refs_0_), channel_id=1, source_target_pairs={{0,1},{1,0},{2,3},{3,2},{4,5},{5,4},{6,7},{7,6},{8,9},{9,8},{10,11... | collective-permute-start | bytes 196616 | tf_op jit(solution)/shard_map/ppermute | solution.py:105
  27.7 4.5 %collective-permute-start.6 = (bf16[8,32,128]{2,1,0:T(8,128)(2,1)S(1)}, bf16[8,32,128]{2,1,0:T(8,128)(2,1)S(1)}, u32[]{:S(2)}, u32[]{:S(2)}) collective-permute-start(bf16[8,32,128]{2,1,0:T(8,128)(2,1)S(1)} %get-tuple-element.42), channel_id=1, source_target_pairs={{0,2},{1,3},{2,0},{3,1},{4,6},{5,7},{6,4},{7,5},{8,10},{9,11},{10,... | collective-permute-start | bytes 196616 | tf_op jit(solution)/shard_map/ppermute | solution.py:105
  29.3 4.1 %collective-permute-start.7 = (bf16[8,32,128]{2,1,0:T(8,128)(2,1)S(1)}, bf16[8,32,128]{2,1,0:T(8,128)(2,1)S(1)}, u32[]{:S(2)}, u32[]{:S(2)}) collective-permute-start(bf16[8,32,128]{2,1,0:T(8,128)(2,1)S(1)} %get-tuple-element.43), channel_id=1, source_target_pairs={{0,3},{1,2},{2,1},{3,0},{4,7},{5,6},{6,5},{7,4},{8,11},{9,10},{10,... | collective-permute-start | bytes 196616 | tf_op jit(solution)/shard_map/ppermute | solution.py:105
  34.1 4.0 %collective-permute-start.9 = (bf16[4,32,128]{2,1,0:T(8,128)(2,1)S(1)}, bf16[4,32,128]{2,1,0:T(8,128)(2,1)S(1)}, u32[]{:S(2)}, u32[]{:S(2)}) collective-permute-start(bf16[4,32,128]{2,1,0:T(8,128)(2,1)S(1)} %get-tuple-element.45), channel_id=1, source_target_pairs={{0,4},{1,13},{2,22},{3,31},{4,0},{5,9},{6,18},{7,27},{8,12},{9,5},... | collective-permute-start | bytes 98312 | tf_op jit(solution)/shard_map/ppermute | solution.py:115
  38.1 8.4 %collective-permute-start.12 = (bf16[8,32,128]{2,1,0:T(8,128)(2,1)S(1)}, bf16[8,32,128]{2,1,0:T(8,128)(2,1)S(1)}, u32[]{:S(2)}, u32[]{:S(2)}) collective-permute-start(bf16[8,32,128]{2,1,0:T(8,128)(2,1)S(1)} %constant_dynamic-update-slice_fusion.2.refs_0_), channel_id=1, source_target_pairs={{0,3},{1,2},{2,1},{3,0},{4,7},{5,6},{6,5},{7,4},{8,11},{9,10},{10,... | collective-permute-start | bytes 196616 | tf_op jit(solution)/shard_map/ppermute | solution.py:105
  43.9 4.3 %collective-permute-start.11 = (bf16[8,32,128]{2,1,0:T(8,128)(2,1)S(1)}, bf16[8,32,128]{2,1,0:T(8,128)(2,1)S(1)}, u32[]{:S(2)}, u32[]{:S(2)}) collective-permute-start(bf16[8,32,128]{2,1,0:T(8,128)(2,1)S(1)} %constant_dynamic-update-slice_fusion.2.refs_0_), channel_id=1, source_target_pairs={{0,2},{1,3},{2,0},{3,1},{4,6},{5,7},{6,4},{7,5},{8,10},{9,11},{10,... | collective-permute-start | bytes 196616 | tf_op jit(solution)/shard_map/ppermute | solution.py:105
  43.9 4.3 %collective-permute-start.10 = (bf16[8,32,128]{2,1,0:T(8,128)(2,1)S(1)}, bf16[8,32,128]{2,1,0:T(8,128)(2,1)S(1)}, u32[]{:S(2)}, u32[]{:S(2)}) collective-permute-start(bf16[8,32,128]{2,1,0:T(8,128)(2,1)S(1)} %constant_dynamic-update-slice_fusion.2.refs_0_), channel_id=1, source_target_pairs={{0,1},{1,0},{2,3},{3,2},{4,5},{5,4},{6,7},{7,6},{8,9},{9,8},{10,11... | collective-permute-start | bytes 196616 | tf_op jit(solution)/shard_map/ppermute | solution.py:105
  53.8 6.4 %collective-permute-start.17 = (bf16[8,32,128]{2,1,0:T(8,128)(2,1)S(1)}, bf16[8,32,128]{2,1,0:T(8,128)(2,1)S(1)}, u32[]{:S(2)}, u32[]{:S(2)}) collective-permute-start(bf16[8,32,128]{2,1,0:T(8,128)(2,1)S(1)} %constant_dynamic-update-slice_fusion.4.refs_0_), channel_id=1, source_target_pairs={{0,3},{1,2},{2,1},{3,0},{4,7},{5,6},{6,5},{7,4},{8,11},{9,10},{10,... | collective-permute-start | bytes 196616 | tf_op jit(solution)/shard_map/ppermute | solution.py:105
  58.3 4.6 %collective-permute-start.16 = (bf16[8,32,128]{2,1,0:T(8,128)(2,1)S(1)}, bf16[8,32,128]{2,1,0:T(8,128)(2,1)S(1)}, u32[]{:S(2)}, u32[]{:S(2)}) collective-permute-start(bf16[8,32,128]{2,1,0:T(8,128)(2,1)S(1)} %constant_dynamic-update-slice_fusion.4.refs_0_), channel_id=1, source_target_pairs={{0,2},{1,3},{2,0},{3,1},{4,6},{5,7},{6,4},{7,5},{8,10},{9,11},{10,... | collective-permute-start | bytes 196616 | tf_op jit(solution)/shard_map/ppermute | solution.py:105
  66.7 4.3 %collective-permute-start.19 = (bf16[8,32,128]{2,1,0:T(8,128)(2,1)S(1)}, bf16[8,32,128]{2,1,0:T(8,128)(2,1)S(1)}, u32[]{:S(2)}, u32[]{:S(2)}) collective-permute-start(bf16[8,32,128]{2,1,0:T(8,128)(2,1)S(1)} %get-tuple-element.51), channel_id=1, source_target_pairs={{0,2},{1,3},{2,0},{3,1},{4,6},{5,7},{6,4},{7,5},{8,10},{9,11},{10,... | collective-permute-start | bytes 196616 | tf_op jit(solution)/shard_map/ppermute | solution.py:105
  68.2 4.1 %collective-permute-start.20 = (bf16[8,32,128]{2,1,0:T(8,128)(2,1)S(1)}, bf16[8,32,128]{2,1,0:T(8,128)(2,1)S(1)}, u32[]{:S(2)}, u32[]{:S(2)}) collective-permute-start(bf16[8,32,128]{2,1,0:T(8,128)(2,1)S(1)} %get-tuple-element.52), channel_id=1, source_target_pairs={{0,3},{1,2},{2,1},{3,0},{4,7},{5,6},{6,5},{7,4},{8,11},{9,10},{10,... | collective-permute-start | bytes 196616 | tf_op jit(solution)/shard_map/ppermute | solution.py:105
  77.0 8.3 %collective-permute-start.25 = (bf16[8,32,128]{2,1,0:T(8,128)(2,1)S(1)}, bf16[8,32,128]{2,1,0:T(8,128)(2,1)S(1)}, u32[]{:S(2)}, u32[]{:S(2)}) collective-permute-start(bf16[8,32,128]{2,1,0:T(8,128)(2,1)S(1)} %constant_dynamic-update-slice_fusion.6.refs_0_), channel_id=1, source_target_pairs={{0,3},{1,2},{2,1},{3,0},{4,7},{5,6},{6,5},{7,4},{8,11},{9,10},{10,... | collective-permute-start | bytes 196616 | tf_op jit(solution)/shard_map/ppermute | solution.py:105
  82.9 4.8 %collective-permute-start.24 = (bf16[8,32,128]{2,1,0:T(8,128)(2,1)S(1)}, bf16[8,32,128]{2,1,0:T(8,128)(2,1)S(1)}, u32[]{:S(2)}, u32[]{:S(2)}) collective-permute-start(bf16[8,32,128]{2,1,0:T(8,128)(2,1)S(1)} %constant_dynamic-update-slice_fusion.6.refs_0_), channel_id=1, source_target_pairs={{0,2},{1,3},{2,0},{3,1},{4,6},{5,7},{6,4},{7,5},{8,10},{9,11},{10,... | collective-permute-start | bytes 196616 | tf_op jit(solution)/shard_map/ppermute | solution.py:105
  83.7 4.0 %collective-permute-start.23 = (bf16[8,32,128]{2,1,0:T(8,128)(2,1)S(1)}, bf16[8,32,128]{2,1,0:T(8,128)(2,1)S(1)}, u32[]{:S(2)}, u32[]{:S(2)}) collective-permute-start(bf16[8,32,128]{2,1,0:T(8,128)(2,1)S(1)} %constant_dynamic-update-slice_fusion.6.refs_0_), channel_id=1, source_target_pairs={{0,1},{1,0},{2,3},{3,2},{4,5},{5,4},{6,7},{7,6},{8,9},{9,8},{10,11... | collective-permute-start | bytes 196616 | tf_op jit(solution)/shard_map/ppermute | solution.py:105
  93.3 7.0 %collective-permute-start.30 = (bf16[8,32,128]{2,1,0:T(8,128)(2,1)S(1)}, bf16[8,32,128]{2,1,0:T(8,128)(2,1)S(1)}, u32[]{:S(2)}, u32[]{:S(2)}) collective-permute-start(bf16[8,32,128]{2,1,0:T(8,128)(2,1)S(1)} %constant_dynamic-update-slice_fusion.8.refs_0_), channel_id=1, source_target_pairs={{0,3},{1,2},{2,1},{3,0},{4,7},{5,6},{6,5},{7,4},{8,11},{9,10},{10,... | collective-permute-start | bytes 196616 | tf_op jit(solution)/shard_map/ppermute | solution.py:105
  97.9 4.7 %collective-permute-start.29 = (bf16[8,32,128]{2,1,0:T(8,128)(2,1)S(1)}, bf16[8,32,128]{2,1,0:T(8,128)(2,1)S(1)}, u32[]{:S(2)}, u32[]{:S(2)}) collective-permute-start(bf16[8,32,128]{2,1,0:T(8,128)(2,1)S(1)} %constant_dynamic-update-slice_fusion.8.refs_0_), channel_id=1, source_target_pairs={{0,2},{1,3},{2,0},{3,1},{4,6},{5,7},{6,4},{7,5},{8,10},{9,11},{10,... | collective-permute-start | bytes 196616 | tf_op jit(solution)/shard_map/ppermute | solution.py:105
  98.6 4.0 %collective-permute-start.28 = (bf16[8,32,128]{2,1,0:T(8,128)(2,1)S(1)}, bf16[8,32,128]{2,1,0:T(8,128)(2,1)S(1)}, u32[]{:S(2)}, u32[]{:S(2)}) collective-permute-start(bf16[8,32,128]{2,1,0:T(8,128)(2,1)S(1)} %constant_dynamic-update-slice_fusion.8.refs_0_), channel_id=1, source_target_pairs={{0,1},{1,0},{2,3},{3,2},{4,5},{5,4},{6,7},{7,6},{8,9},{9,8},{10,11... | collective-permute-start | bytes 196616 | tf_op jit(solution)/shard_map/ppermute | solution.py:105
  106.3 4.5 %collective-permute-start.32 = (bf16[8,32,128]{2,1,0:T(8,128)(2,1)S(1)}, bf16[8,32,128]{2,1,0:T(8,128)(2,1)S(1)}, u32[]{:S(2)}, u32[]{:S(2)}) collective-permute-start(bf16[8,32,128]{2,1,0:T(8,128)(2,1)S(1)} %get-tuple-element.60), channel_id=1, source_target_pairs={{0,2},{1,3},{2,0},{3,1},{4,6},{5,7},{6,4},{7,5},{8,10},{9,11},{10,... | collective-permute-start | bytes 196616 | tf_op jit(solution)/shard_map/ppermute | solution.py:105
  108.0 4.1 %collective-permute-start.33 = (bf16[8,32,128]{2,1,0:T(8,128)(2,1)S(1)}, bf16[8,32,128]{2,1,0:T(8,128)(2,1)S(1)}, u32[]{:S(2)}, u32[]{:S(2)}) collective-permute-start(bf16[8,32,128]{2,1,0:T(8,128)(2,1)S(1)} %get-tuple-element.61), channel_id=1, source_target_pairs={{0,3},{1,2},{2,1},{3,0},{4,7},{5,6},{6,5},{7,4},{8,11},{9,10},{10,... | collective-permute-start | bytes 196616 | tf_op jit(solution)/shard_map/ppermute | solution.py:105
  116.8 8.1 %collective-permute-start.38 = (bf16[8,32,128]{2,1,0:T(8,128)(2,1)S(1)}, bf16[8,32,128]{2,1,0:T(8,128)(2,1)S(1)}, u32[]{:S(2)}, u32[]{:S(2)}) collective-permute-start(bf16[8,32,128]{2,1,0:T(8,128)(2,1)S(1)} %constant_dynamic-update-slice_fusion.10.refs_0_), channel_id=1, source_target_pairs={{0,3},{1,2},{2,1},{3,0},{4,7},{5,6},{6,5},{7,4},{8,11},{9,10},{10,... | collective-permute-start | bytes 196616 | tf_op jit(solution)/shard_map/ppermute | solution.py:105
  122.6 4.9 %collective-permute-start.37 = (bf16[8,32,128]{2,1,0:T(8,128)(2,1)S(1)}, bf16[8,32,128]{2,1,0:T(8,128)(2,1)S(1)}, u32[]{:S(2)}, u32[]{:S(2)}) collective-permute-start(bf16[8,32,128]{2,1,0:T(8,128)(2,1)S(1)} %constant_dynamic-update-slice_fusion.10.refs_0_), channel_id=1, source_target_pairs={{0,2},{1,3},{2,0},{3,1},{4,6},{5,7},{6,4},{7,5},{8,10},{9,11},{10,... | collective-permute-start | bytes 196616 | tf_op jit(solution)/shard_map/ppermute | solution.py:105
  123.5 4.0 %collective-permute-start.36 = (bf16[8,32,128]{2,1,0:T(8,128)(2,1)S(1)}, bf16[8,32,128]{2,1,0:T(8,128)(2,1)S(1)}, u32[]{:S(2)}, u32[]{:S(2)}) collective-permute-start(bf16[8,32,128]{2,1,0:T(8,128)(2,1)S(1)} %constant_dynamic-update-slice_fusion.10.refs_0_), channel_id=1, source_target_pairs={{0,1},{1,0},{2,3},{3,2},{4,5},{5,4},{6,7},{7,6},{8,9},{9,8},{10,11... | collective-permute-start | bytes 196616 | tf_op jit(solution)/shard_map/ppermute | solution.py:105
  133.3 5.9 %collective-permute-start.43 = (bf16[8,32,128]{2,1,0:T(8,128)(2,1)S(1)}, bf16[8,32,128]{2,1,0:T(8,128)(2,1)S(1)}, u32[]{:S(2)}, u32[]{:S(2)}) collective-permute-start(bf16[8,32,128]{2,1,0:T(8,128)(2,1)S(1)} %constant_dynamic-update-slice_fusion.12.refs_0_), channel_id=1, source_target_pairs={{0,3},{1,2},{2,1},{3,0},{4,7},{5,6},{6,5},{7,4},{8,11},{9,10},{10,... | collective-permute-start | bytes 196616 | tf_op jit(solution)/shard_map/ppermute | solution.py:105
  137.1 4.8 %collective-permute-start.42 = (bf16[8,32,128]{2,1,0:T(8,128)(2,1)S(1)}, bf16[8,32,128]{2,1,0:T(8,128)(2,1)S(1)}, u32[]{:S(2)}, u32[]{:S(2)}) collective-permute-start(bf16[8,32,128]{2,1,0:T(8,128)(2,1)S(1)} %constant_dynamic-update-slice_fusion.12.refs_0_), channel_id=1, source_target_pairs={{0,2},{1,3},{2,0},{3,1},{4,6},{5,7},{6,4},{7,5},{8,10},{9,11},{10,... | collective-permute-start | bytes 196616 | tf_op jit(solution)/shard_map/ppermute | solution.py:105
  145.6 4.5 %collective-permute-start.45 = (bf16[8,32,128]{2,1,0:T(8,128)(2,1)S(1)}, bf16[8,32,128]{2,1,0:T(8,128)(2,1)S(1)}, u32[]{:S(2)}, u32[]{:S(2)}) collective-permute-start(bf16[8,32,128]{2,1,0:T(8,128)(2,1)S(1)} %get-tuple-element.69), channel_id=1, source_target_pairs={{0,2},{1,3},{2,0},{3,1},{4,6},{5,7},{6,4},{7,5},{8,10},{9,11},{10,... | collective-permute-start | bytes 196616 | tf_op jit(solution)/shard_map/ppermute | solution.py:105
  146.9 4.3 %collective-permute-start.46 = (bf16[8,32,128]{2,1,0:T(8,128)(2,1)S(1)}, bf16[8,32,128]{2,1,0:T(8,128)(2,1)S(1)}, u32[]{:S(2)}, u32[]{:S(2)}) collective-permute-start(bf16[8,32,128]{2,1,0:T(8,128)(2,1)S(1)} %get-tuple-element.70), channel_id=1, source_target_pairs={{0,3},{1,2},{2,1},{3,0},{4,7},{5,6},{6,5},{7,4},{8,11},{9,10},{10,... | collective-permute-start | bytes 196616 | tf_op jit(solution)/shard_map/ppermute | solution.py:105
  156.0 8.7 %collective-permute-start.51 = (bf16[8,32,128]{2,1,0:T(8,128)(2,1)S(1)}, bf16[8,32,128]{2,1,0:T(8,128)(2,1)S(1)}, u32[]{:S(2)}, u32[]{:S(2)}) collective-permute-start(bf16[8,32,128]{2,1,0:T(8,128)(2,1)S(1)} %constant_dynamic-update-slice_fusion.14.refs_0_), channel_id=1, source_target_pairs={{0,3},{1,2},{2,1},{3,0},{4,7},{5,6},{6,5},{7,4},{8,11},{9,10},{10,... | collective-permute-start | bytes 196616 | tf_op jit(solution)/shard_map/ppermute | solution.py:105
  162.4 4.9 %collective-permute-start.50 = (bf16[8,32,128]{2,1,0:T(8,128)(2,1)S(1)}, bf16[8,32,128]{2,1,0:T(8,128)(2,1)S(1)}, u32[]{:S(2)}, u32[]{:S(2)}) collective-permute-start(bf16[8,32,128]{2,1,0:T(8,128)(2,1)S(1)} %constant_dynamic-update-slice_fusion.14.refs_0_), channel_id=1, source_target_pairs={{0,2},{1,3},{2,0},{3,1},{4,6},{5,7},{6,4},{7,5},{8,10},{9,11},{10,... | collective-permute-start | bytes 196616 | tf_op jit(solution)/shard_map/ppermute | solution.py:105
  163.3 4.0 %collective-permute-start.49 = (bf16[8,32,128]{2,1,0:T(8,128)(2,1)S(1)}, bf16[8,32,128]{2,1,0:T(8,128)(2,1)S(1)}, u32[]{:S(2)}, u32[]{:S(2)}) collective-permute-start(bf16[8,32,128]{2,1,0:T(8,128)(2,1)S(1)} %constant_dynamic-update-slice_fusion.14.refs_0_), channel_id=1, source_target_pairs={{0,1},{1,0},{2,3},{3,2},{4,5},{5,4},{6,7},{7,6},{8,9},{9,8},{10,11... | collective-permute-start | bytes 196616 | tf_op jit(solution)/shard_map/ppermute | solution.py:105
  (28 other events, 253.2 us)

commit v5 on v3

v5 whole, which is shorter than its diff:
```python
import functools
import math

import jax
import jax.numpy as jnp
from jax import lax
from jax.experimental import pallas as pl
from jax.experimental.pallas import tpu as pltpu
from jax.sharding import Mesh, PartitionSpec as P

ITERATIONS = 4


VMEM = pl.BlockSpec(memory_space=pltpu.VMEM)
SMEM = pl.BlockSpec(memory_space=pltpu.SMEM)
PARAMS = pltpu.CompilerParams(vmem_limit_bytes=32 * 1024 * 1024)


def model_kernel(index, model, measured, tiles, own, *refs):
    *sent, residual, narrow, sums = refs
    wide = own.shape[0]
    count = model.shape[0]
    residual[...] = measured[...]
    sums[...] = jnp.zeros_like(sums)
    for k in range(count):
        part = lax.dot_general(
            tiles[index[0, k]],
            model[k],
            (((1,), (1,)), ((), ())),
            preferred_element_type=jnp.float32,
        )
        residual[index[2, k]] -= part
    narrow[...] = residual[...].astype(jnp.bfloat16)
    for k in range(count):
        part = jnp.dot(narrow[index[2, k]], model[k], preferred_element_type=jnp.float32)
        sums[index[1, k]] += part
    own[...] = sums[:wide]
    for d, out in enumerate(sent, 1):
        out[...] = sums[d * wide : (d + 1) * wide].astype(jnp.bfloat16)


def stage_kernel(*refs):
    *pairs, sems = refs
    half = len(pairs) // 2
    copies = [
        pltpu.make_async_copy(pairs[i], pairs[half + i], sems.at[i]) for i in range(half)
    ]
    for copy in copies:
        copy.start()
    for copy in copies:
        copy.wait()


def reduce_kernel(own, *refs):
    *received, out = refs
    vox_count, hi_count, per = out.shape[:3]
    total = own[...]
    for piece in received:
        total = total + piece[...].astype(jnp.float32)
    total = total.astype(jnp.bfloat16)
    for v in range(vox_count):
        for h in range(hi_count):
            out[v, h] = total[v * per : (v + 1) * per]


def merge_kernel(parts, out):
    vox_count, hi_count, per = parts.shape[:3]
    for v in range(vox_count):
        total = parts[v, 0].astype(jnp.float32)
        for h in range(1, hi_count):
            total = total + parts[v, h].astype(jnp.float32)
        out[v * per : (v + 1) * per] = total.astype(jnp.bfloat16)


def pick_kernel(table, image, out):
    vox_count, capacity = table.shape
    for v in range(vox_count):
        for s in range(capacity):
            tile = jnp.maximum(table[v, s], 0)
            out[v * capacity + s] = image[tile].astype(jnp.bfloat16)


def update_kernel(lo_count, ids, table, gains, image, *refs):
    received = refs[:lo_count]
    estimate, *outs = refs[lo_count:-1]
    gradient = refs[-1]
    vox_count, capacity = table.shape
    per = capacity // lo_count
    gradient[...] = jnp.zeros_like(gradient)
    for d in range(lo_count):
        first = (ids[0] ^ d) * per
        for v in range(vox_count):
            for p in range(per):
                tile = jnp.maximum(table[v, first + p], 0)
                gradient[tile] += received[d][v * per + p].astype(jnp.float32)
    estimate[...] = jnp.maximum(image[...] + gains[...][None] * gradient[...], 0.0)
    if outs:
        pick_kernel(table, estimate, *outs)


def shards(model_blocks, start_image, measured, step_size, sent_tiles, block_rows, block_slots):
    vox_count = lax.axis_size("vox")
    hi_count = lax.axis_size("hi")
    lo_count = lax.axis_size("lo")
    lo = lax.axis_index("lo")
    table = sent_tiles[0]
    capacity = table.shape[1]
    per = capacity // lo_count
    tile_count, wave_count, width = start_image.shape
    row_count = measured.shape[0]
    slot_count = vox_count * capacity
    wide = vox_count * per
    tile = (wave_count, width)
    ids = lo.astype(jnp.int32)[None]
    slab, slot = block_slots // capacity, block_slots % capacity
    places = (((slot // per) ^ lo) * vox_count + slab) * per + slot % per
    index = jnp.stack([block_slots, places, block_rows])
    gains = jnp.broadcast_to(step_size[:, None], tile)

    def shape(count, dtype):
        return jax.ShapeDtypeStruct((count, *tile), dtype)

    def swap(array, d):
        pairs = [(i, i ^ d) for i in range(lo_count)]
        return lax.ppermute(array, "lo", pairs) if d else array

    def exchange(array, axes):
        return lax.all_to_all(array, axes, split_axis=0, concat_axis=0, tiled=True)

    stage = pl.pallas_call(
        stage_kernel,
        out_shape=[
            jax.ShapeDtypeStruct(model_blocks.shape, model_blocks.dtype),
            jax.ShapeDtypeStruct(measured.shape, measured.dtype),
        ],
        in_specs=[pl.BlockSpec(memory_space=pltpu.HBM)] * 2,
        out_specs=[VMEM] * 2,
        scratch_shapes=[pltpu.SemaphoreType.DMA((2,))],
        compiler_params=PARAMS,
        cost_estimate=pl.CostEstimate(
            flops=0, bytes_accessed=2 * model_blocks.size * 2, transcendentals=0
        ),
        name="stage",
    )
    apply_model = pl.pallas_call(
        model_kernel,
        out_shape=(
            shape(wide, jnp.float32),
            *[shape(wide, jnp.bfloat16)] * (lo_count - 1),
            shape(row_count, jnp.float32),
        ),
        in_specs=[SMEM, VMEM, VMEM, VMEM],
        out_specs=[VMEM] * (lo_count + 1),
        scratch_shapes=[
            pltpu.VMEM((row_count, *tile), jnp.bfloat16),
            pltpu.VMEM((slot_count, *tile), jnp.float32),
        ],
        compiler_params=PARAMS,
        name="model",
    )
    reduce_parts = pl.pallas_call(
        reduce_kernel,
        out_shape=jax.ShapeDtypeStruct((vox_count, hi_count, per, *tile), jnp.bfloat16),
        in_specs=[VMEM] * lo_count,
        out_specs=VMEM,
        compiler_params=PARAMS,
        name="reduce",
    )
    merge = pl.pallas_call(
        merge_kernel,
        out_shape=shape(wide, jnp.bfloat16),
        in_specs=[VMEM],
        out_specs=VMEM,
        compiler_params=PARAMS,
        name="merge",
    )
    pick = pl.pallas_call(
        pick_kernel,
        out_shape=shape(slot_count, jnp.bfloat16),
        in_specs=[SMEM, VMEM],
        out_specs=VMEM,
        compiler_params=PARAMS,
        name="pick",
    )

    def update(last):
        outs = [] if last else [shape(slot_count, jnp.bfloat16)]
        return pl.pallas_call(
            functools.partial(update_kernel, lo_count),
            out_shape=[shape(tile_count, jnp.float32)] + outs,
            in_specs=[SMEM, SMEM, VMEM, VMEM] + [VMEM] * lo_count,
            out_specs=[VMEM] * (len(outs) + 1),
            scratch_shapes=[pltpu.VMEM((tile_count, *tile), jnp.float32)],
            compiler_params=PARAMS,
            name="update",
        )

    estimate = start_image
    outgoing = [pick(table, start_image)]
    model, signals = stage(model_blocks, measured)
    for iteration in range(ITERATIONS):
        tiles = exchange(*outgoing, "vox")
        own, *partial, residual = apply_model(index, model, signals, tiles)
        total = reduce_parts(own, *[swap(piece, d) for d, piece in enumerate(partial, 1)])
        total = total.reshape(vox_count * hi_count, per, *tile)
        parts = exchange(total, ("vox", "hi"))
        merged = merge(parts.reshape(vox_count, hi_count, per, *tile))
        estimate, *outgoing = update(iteration == ITERATIONS - 1)(
            ids, table, gains, estimate, *[swap(merged, d) for d in range(lo_count)]
        )
    return (estimate, residual)


def solution(mesh):
    vox_count, chan_count = mesh.devices.shape
    lo_count = math.gcd(chan_count, 2)
    cut = Mesh(
        mesh.devices.reshape(vox_count, chan_count // lo_count, lo_count), ("vox", "hi", "lo")
    )
    everywhere = ("vox", "hi", "lo")
    in_specs = (
        P(everywhere, None, None),
        P("vox", None, None),
        P(everywhere, None, None),
        P(),
        P("vox", None, None),
        P(everywhere),
        P(everywhere),
    )
    out_specs = (P("vox", None, None), P(everywhere, None, None))
    return jax.shard_map(shards, mesh=cut, in_specs=in_specs, out_specs=out_specs, check_vma=False)
```

time: 164 us -> 144 us (0.88)
  waiting for transfers between devices: 36.6 us -> 16.2 us
  blocking collectives: 76.8 us -> 93.1 us
  starting transfers between devices: 22.3 us -> 7.55 us
    ppermute x24 -> x8, waiting for transfers between devices: 28.4 us -> 10.7 us  [swap(): return lax.ppermute(array, 'lo', pairs) if d else array]
    all_to_all x7, blocking collectives: 76.8 us -> 93.1 us  [exchange(): return lax.all_to_all(array, axes, split_axis=0, concat_axis=0, tiled=True)]
    ppermute x24 -> x8, starting transfers between devices: 14.9 us -> 0.29 us  [swap(): return lax.ppermute(array, 'lo', pairs) if d else array]
    all_to_all x1, waiting for transfers between devices: 8.25 us -> 5.53 us  [exchange(): return lax.all_to_all(array, axes, split_axis=0, concat_axis=0, tiled=True)]
    unnamed x20 -> x14, local copies, waits for them, and re-layouts: 5.13 us -> 3.81 us
    pallas_call x8 -> x13, Pallas kernels: 19.3 us -> 20.1 us  [the longest x4 14.8 us: shards(): own, *partial, residual = apply_model(index, model, signals, tiles)]
  transfers between devices with their start and end apart: 25 -> 9, of which waited for: 17 -> 9; matrix products, arithmetic and copies ran while one was open for 0% -> 0% of each run, Pallas kernels for 0% -> 0%
where the time goes in v5:
time: 144 us
  blocking collectives  93.1 us (65%)
  Pallas kernels  21.5 us (15%)
  waiting for transfers between devices  16.2 us (11%)
  starting transfers between devices  7.55 us (5%)
  local copies, waits for them, and re-layouts  4.65 us (3%)
    all_to_all x7, blocking collectives, exchange(): return lax.all_to_all(array, axes, split_axis=0, concat_axis=0, tiled=True)  93.1 us
    pallas_call x4, Pallas kernels, shards(): own, *partial, residual = apply_model(index, model, signals, tiles)  14.8 us
    ppermute x8, waiting for transfers between devices, swap(): return lax.ppermute(array, 'lo', pairs) if d else array  10.7 us
    all_to_all x1, starting transfers between devices, exchange(): return lax.all_to_all(array, axes, split_axis=0, concat_axis=0, tiled=True)  7.25 us
    all_to_all x1, waiting for transfers between devices, exchange(): return lax.all_to_all(array, axes, split_axis=0, concat_axis=0, tiled=True)  5.53 us
    pallas_call x4, Pallas kernels, shards(): update(iteration == ITERATIONS - 1)  4.62 us
    unnamed x14, local copies, waits for them, and re-layouts  3.81 us
  transfers between devices with their start and end apart: 9, of which 9 were waited for; matrix products, arithmetic and copies ran while one was open for 0% of the time, Pallas kernels for 0%

profile of v5, /device:TPU:0, one launch (start us, length us, event | category | flops | bytes accessed | tf_op | source)
XLA Modules:
  0.0 143.8 jit_solution(2837316400576752797)
XLA Ops:
  0.7 0.8 copy.13.table
  1.4 1.0 copy-done.1
  2.5 1.3 pick.1
  3.8 7.3 %all-to-all-start = ((bf16[32,32,128]{2,1,0:T(8,128)(2,1)}), bf16[32,32,128]{2,1,0:T(8,128)(2,1)S(1)}, u32[]{:S(2)}, u32[]{:S(2)}) async-start(bf16[32,32,128]{2,1,0:T(8,128)(2,1)} %pick.1), calls=%async_computation | async-start | bytes 524288 | tf_op jit(solution)/shard_map/all_to_all | solution.py:128
  11.1 1.8 %copy-done = bf16[92,128,128]{2,1,0:T(8,128)(2,1)S(1)} copy-done((bf16[92,128,128]{2,1,0:T(8,128)(2,1)S(1)}, bf16[92,128,128]{2,1,0:T(8,128)(2,1)}, u32[]{:S(2)}) %copy-start) | copy-done | bytes 3014680
  12.9 0.9 copy-done.3
  13.8 0.5 stage.1
  14.4 5.5 %all-to-all-done.tiles = bf16[32,32,128]{2,1,0:T(8,128)(2,1)S(1)} async-done(((bf16[32,32,128]{2,1,0:T(8,128)(2,1)}), bf16[32,32,128]{2,1,0:T(8,128)(2,1)S(1)}, u32[]{:S(2)}, u32[]{:S(2)}) %all-to-all-start) | async-done | bytes 262176 | tf_op jit(solution)/shard_map/all_to_all | solution.py:128
  20.0 3.7 %model.4 = (f32[16,32,128]{2,1,0:T(8,128)S(1)}, bf16[16,32,128]{2,1,0:T(8,128)(2,1)S(1)}, f32[8,32,128]{2,1,0:T(8,128)}) custom-call(s32[3,92]{1,0:T(4,128)S(1)} %pad_add_fusion.index, bf16[92,128,128]{2,1,0:T(8,128)(2,1)S(1)} %get-tuple-element.19.model, f32[8,32,128]{2,1,0:T(8,128)S(1)} %get-tuple-element.20.measured, ...), custom_call_target="tpu_custom_call" | custom-call | tf_op jit(solution)/shard_map/model/pallas_call | solution.py:203
  23.7 1.3 collective-permute-done.refs_0_
  25.0 14.6 %all_to_all.40 = bf16[16,2,32,128]{3,2,1,0:T(8,128)(2,1)S(1)} all-to-all(bf16[16,2,32,128]{3,2,1,0:T(8,128)(2,1)S(1)} %bitcast.14), channel_id=1, replica_groups=mesh['vox'=8,'hi'=2,'lo'=2] {'vox','hi'}, dimensions={0} | all-to-all | bytes 524288 | tf_op jit(solution)/shard_map/all_to_all | solution.py:128
  39.8 1.3 collective-permute-done.1.refs_1_
  41.2 1.0 update.4
  42.2 12.5 %all_to_all.41.tiles = bf16[32,32,128]{2,1,0:T(8,128)(2,1)S(1)} all-to-all(bf16[32,32,128]{2,1,0:T(8,128)(2,1)S(1)} %get-tuple-element.24), channel_id=1, replica_groups=mesh['vox'=8,'hi'=2,'lo'=2] {'vox'}, dimensions={0} | all-to-all | bytes 524288 | tf_op jit(solution)/shard_map/all_to_all | solution.py:128
  54.6 3.7 %model.5 = (f32[16,32,128]{2,1,0:T(8,128)S(1)}, bf16[16,32,128]{2,1,0:T(8,128)(2,1)S(1)}, f32[8,32,128]{2,1,0:T(8,128)}) custom-call(s32[3,92]{1,0:T(4,128)S(1)} %pad_add_fusion.index, bf16[92,128,128]{2,1,0:T(8,128)(2,1)S(1)} %get-tuple-element.19.model, f32[8,32,128]{2,1,0:T(8,128)S(1)} %get-tuple-element.20.measured, ...), custom_call_target="tpu_custom_call" | custom-call | tf_op jit(solution)/shard_map/model/pallas_call | solution.py:203
  58.3 1.3 collective-permute-done.2.refs_0_
  59.7 13.7 %all_to_all.42 = bf16[16,2,32,128]{3,2,1,0:T(8,128)(2,1)S(1)} all-to-all(bf16[16,2,32,128]{3,2,1,0:T(8,128)(2,1)S(1)} %bitcast.15), channel_id=1, replica_groups=mesh['vox'=8,'hi'=2,'lo'=2] {'vox','hi'}, dimensions={0} | all-to-all | bytes 524288 | tf_op jit(solution)/shard_map/all_to_all | solution.py:128
  73.4 0.1 collective-permute-start.3
  73.5 1.3 collective-permute-done.3.refs_1_
  74.8 1.0 update.5
  75.8 12.5 %all_to_all.43.tiles = bf16[32,32,128]{2,1,0:T(8,128)(2,1)S(1)} all-to-all(bf16[32,32,128]{2,1,0:T(8,128)(2,1)S(1)} %get-tuple-element.28), channel_id=1, replica_groups=mesh['vox'=8,'hi'=2,'lo'=2] {'vox'}, dimensions={0} | all-to-all | bytes 524288 | tf_op jit(solution)/shard_map/all_to_all | solution.py:128
  88.3 3.7 %model.6 = (f32[16,32,128]{2,1,0:T(8,128)S(1)}, bf16[16,32,128]{2,1,0:T(8,128)(2,1)S(1)}, f32[8,32,128]{2,1,0:T(8,128)}) custom-call(s32[3,92]{1,0:T(4,128)S(1)} %pad_add_fusion.index, bf16[92,128,128]{2,1,0:T(8,128)(2,1)S(1)} %get-tuple-element.19.model, f32[8,32,128]{2,1,0:T(8,128)S(1)} %get-tuple-element.20.measured, ...), custom_call_target="tpu_custom_call" | custom-call | tf_op jit(solution)/shard_map/model/pallas_call | solution.py:203
  92.0 1.3 collective-permute-done.4.refs_0_
  93.3 13.7 %all_to_all.44 = bf16[16,2,32,128]{3,2,1,0:T(8,128)(2,1)S(1)} all-to-all(bf16[16,2,32,128]{3,2,1,0:T(8,128)(2,1)S(1)} %bitcast.16), channel_id=1, replica_groups=mesh['vox'=8,'hi'=2,'lo'=2] {'vox','hi'}, dimensions={0} | all-to-all | bytes 524288 | tf_op jit(solution)/shard_map/all_to_all | solution.py:128
  107.1 1.3 collective-permute-done.5.refs_1_
  108.5 1.0 update.6
  109.4 12.5 %all_to_all.45.tiles = bf16[32,32,128]{2,1,0:T(8,128)(2,1)S(1)} all-to-all(bf16[32,32,128]{2,1,0:T(8,128)(2,1)S(1)} %get-tuple-element.32), channel_id=1, replica_groups=mesh['vox'=8,'hi'=2,'lo'=2] {'vox'}, dimensions={0} | all-to-all | bytes 524288 | tf_op jit(solution)/shard_map/all_to_all | solution.py:128
  121.9 3.7 %model.7 = (f32[16,32,128]{2,1,0:T(8,128)S(1)}, bf16[16,32,128]{2,1,0:T(8,128)(2,1)S(1)}, f32[8,32,128]{2,1,0:T(8,128)}) custom-call(s32[3,92]{1,0:T(4,128)S(1)} %pad_add_fusion.index, bf16[92,128,128]{2,1,0:T(8,128)(2,1)S(1)} %get-tuple-element.19.model, f32[8,32,128]{2,1,0:T(8,128)S(1)} %get-tuple-element.20.measured, ...), custom_call_target="tpu_custom_call" | custom-call | tf_op jit(solution)/shard_map/model/pallas_call | solution.py:203
  125.6 1.3 collective-permute-done.6.refs_0_
  127.0 13.7 %all_to_all.46 = bf16[16,2,32,128]{3,2,1,0:T(8,128)(2,1)S(1)} all-to-all(bf16[16,2,32,128]{3,2,1,0:T(8,128)(2,1)S(1)} %bitcast.17), channel_id=1, replica_groups=mesh['vox'=8,'hi'=2,'lo'=2] {'vox','hi'}, dimensions={0} | all-to-all | bytes 524288 | tf_op jit(solution)/shard_map/all_to_all | solution.py:128
  140.8 1.3 collective-permute-done.7.refs_1_
  142.1 1.7 %update.7 = f32[32,32,128]{2,1,0:T(8,128)} custom-call(s32[1]{0:T(128)} %bitcast.ids, s32[8,4]{1,0:T(8,128)S(1)} %copy.13.table, f32[32,128]{1,0:T(8,128)S(1)} %broadcast_in_dim.10.gains, f32[32,32,128]{2,1,0:T(8,128)S(1)} %get-tuple-element.31.image, bf16[16,32,128]{2,1,0:T(8,128)(2,1)S(1)} %merge.7.refs_0_, ...), custom_call_target="tpu_custom_call" | custom-call | tf_op jit(solution)/shard_map/update/pallas_call | solution.py:208
  (29 shorter events, 0.6 us)
Async XLA Ops:
  0.6 13.7 %copy-start.5 = (s32[92]{0:T(128)S(1)}, s32[92]{0:T(128)}, u32[]{:S(2)}) copy-start(s32[92]{0:T(128)} %param.13) | copy-start | bytes 1108
  0.6 13.8 %copy-start.4 = (s32[92]{0:T(128)S(1)}, s32[92]{0:T(128)}, u32[]{:S(2)}) copy-start(s32[92]{0:T(128)} %param.12) | copy-start | bytes 1108
  1.4 1.0 copy-start.1
  3.8 16.2 %all-to-all-start = ((bf16[32,32,128]{2,1,0:T(8,128)(2,1)}), bf16[32,32,128]{2,1,0:T(8,128)(2,1)S(1)}, u32[]{:S(2)}, u32[]{:S(2)}) async-start(bf16[32,32,128]{2,1,0:T(8,128)(2,1)} %pick.1), calls=%async_computation | async-start | bytes 524288 | tf_op jit(solution)/shard_map/all_to_all | solution.py:128
  11.1 1.9 %copy-start = (bf16[92,128,128]{2,1,0:T(8,128)(2,1)S(1)}, bf16[92,128,128]{2,1,0:T(8,128)(2,1)}, u32[]{:S(2)}) copy-start(bf16[92,128,128]{2,1,0:T(8,128)(2,1)} %refs_0_.1) | copy-start | bytes 9043972
  12.9 0.9 copy-start.3
  14.4 26.7 %copy-start.6 = (f32[32]{0:T(128)S(1)}, f32[32]{0:T(128)}, u32[]{:S(2)}) copy-start(f32[32]{0:T(128)} %param.10) | copy-start | bytes 388
  20.0 21.2 %copy-start.2 = (f32[32,32,128]{2,1,0:T(8,128)S(1)}, f32[32,32,128]{2,1,0:T(8,128)}, u32[]{:S(2)}) copy-start(f32[32,32,128]{2,1,0:T(8,128)} %image.3) | copy-start | bytes 1572868
  23.7 1.3 collective-permute-start
  39.7 1.4 collective-permute-start.1
  58.3 1.3 collective-permute-start.2
  73.4 1.4 collective-permute-start.3
  92.0 1.3 collective-permute-start.4
  107.1 1.4 collective-permute-start.5
  125.6 1.3 collective-permute-start.6
  140.7 1.4 collective-permute-start.7

commit v6 on v5

--- a/solution.py
+++ b/solution.py
@@ -16,24 +16,50 @@
 PARAMS = pltpu.CompilerParams(vmem_limit_bytes=32 * 1024 * 1024)
 
 
+def grouped(source, index, column, model, k, size, dims):
+    left = [source[index[column, k + i]] for i in range(size)]
+    blocks = [model[k + i] for i in range(size)]
+    if size < 4:
+        return [
+            lax.dot_general(x, block, dims, preferred_element_type=jnp.float32)
+            for x, block in zip(left, blocks)
+        ]
+    zero = jnp.zeros_like(left[0])
+    rows = jnp.concatenate(
+        [
+            jnp.concatenate([x, zero] if i % 2 == 0 else [zero, x], axis=1)
+            for i, x in enumerate(left)
+        ],
+        axis=0,
+    )
+    depth = dims[0][1][0]
+    halves = [jnp.concatenate(blocks[n : n + 2], axis=depth) for n in (0, 2)]
+    whole = jnp.concatenate(halves, axis=1 - depth)
+    out = lax.dot_general(rows, whole, dims, preferred_element_type=jnp.float32)
+    height, width = left[0].shape[0], out.shape[1] // 2
+    return [
+        out[i * height : (i + 1) * height, i // 2 * width : (i // 2 + 1) * width]
+        for i in range(4)
+    ]
+
+
 def model_kernel(index, model, measured, tiles, own, *refs):
     *sent, residual, narrow, sums = refs
     wide = own.shape[0]
     count = model.shape[0]
     residual[...] = measured[...]
     sums[...] = jnp.zeros_like(sums)
-    for k in range(count):
-        part = lax.dot_general(
-            tiles[index[0, k]],
-            model[k],
-            (((1,), (1,)), ((), ())),
-            preferred_element_type=jnp.float32,
-        )
-        residual[index[2, k]] -= part
+    for k in range(0, count, 4):
+        for i, part in enumerate(
+            grouped(tiles, index, 0, model, k, min(4, count - k), (((1,), (1,)), ((), ())))
+        ):
+            residual[index[2, k + i]] -= part
     narrow[...] = residual[...].astype(jnp.bfloat16)
-    for k in range(count):
-        part = jnp.dot(narrow[index[2, k]], model[k], preferred_element_type=jnp.float32)
-        sums[index[1, k]] += part
+    for k in range(0, count, 4):
+        for i, part in enumerate(
+            grouped(narrow, index, 2, model, k, min(4, count - k), (((1,), (0,)), ((), ())))
+        ):
+            sums[index[1, k + i]] += part
     own[...] = sums[:wide]
     for d, out in enumerate(sent, 1):
         out[...] = sums[d * wide : (d + 1) * wide].astype(jnp.bfloat16)
@@ -73,10 +99,10 @@
 
 
 def pick_kernel(table, image, out):
-    vox_count, capacity = table.shape
+    _, vox_count, capacity = table.shape
     for v in range(vox_count):
         for s in range(capacity):
-            tile = jnp.maximum(table[v, s], 0)
+            tile = jnp.maximum(table[0, v, s], 0)
             out[v * capacity + s] = image[tile].astype(jnp.bfloat16)
 
 
@@ -84,14 +110,14 @@
     received = refs[:lo_count]
     estimate, *outs = refs[lo_count:-1]
     gradient = refs[-1]
-    vox_count, capacity = table.shape
+    _, vox_count, capacity = table.shape
     per = capacity // lo_count
     gradient[...] = jnp.zeros_like(gradient)
     for d in range(lo_count):
         first = (ids[0] ^ d) * per
         for v in range(vox_count):
             for p in range(per):
-                tile = jnp.maximum(table[v, first + p], 0)
+                tile = jnp.maximum(table[0, v, first + p], 0)
                 gradient[tile] += received[d][v * per + p].astype(jnp.float32)
     estimate[...] = jnp.maximum(image[...] + gains[...][None] * gradient[...], 0.0)
     if outs:
@@ -103,8 +129,7 @@
     hi_count = lax.axis_size("hi")
     lo_count = lax.axis_size("lo")
     lo = lax.axis_index("lo")
-    table = sent_tiles[0]
-    capacity = table.shape[1]
+    capacity = sent_tiles.shape[2]
     per = capacity // lo_count
     tile_count, wave_count, width = start_image.shape
     row_count = measured.shape[0]
@@ -196,7 +221,7 @@
         )
 
     estimate = start_image
-    outgoing = [pick(table, start_image)]
+    outgoing = [pick(sent_tiles, start_image)]
     model, signals = stage(model_blocks, measured)
     for iteration in range(ITERATIONS):
         tiles = exchange(*outgoing, "vox")
@@ -206,7 +231,7 @@
         parts = exchange(total, ("vox", "hi"))
         merged = merge(parts.reshape(vox_count, hi_count, per, *tile))
         estimate, *outgoing = update(iteration == ITERATIONS - 1)(
-            ids, table, gains, estimate, *[swap(merged, d) for d in range(lo_count)]
+            ids, sent_tiles, gains, estimate, *[swap(merged, d) for d in range(lo_count)]
         )
     return (estimate, residual)
 

time: 144 us -> 142 us (0.986)
  Pallas kernels: 21.5 us -> 18.7 us
    pallas_call x4, Pallas kernels: 14.8 us -> 11.9 us  [shards(): own, *partial, residual = apply_model(index, model, signals, tiles)]
    unnamed x14 -> x15, local copies, waits for them, and re-layouts: 3.81 us -> 4.58 us
where the time goes in v6:
time: 142 us; the launch traced here: 141 us
  blocking collectives  93 us (65%)
  Pallas kernels  18.7 us (13%)
  waiting for transfers between devices  16.2 us (11%)
  starting transfers between devices  7.55 us (5%)
  local copies, waits for them, and re-layouts  4.65 us (3%)
    all_to_all x7, blocking collectives, exchange(): return lax.all_to_all(array, axes, split_axis=0, concat_axis=0, tiled=True)  93 us
    pallas_call x4, Pallas kernels, shards(): own, *partial, residual = apply_model(index, model, signals, tiles)  11.9 us
    ppermute x8, waiting for transfers between devices, swap(): return lax.ppermute(array, 'lo', pairs) if d else array  10.7 us
    all_to_all x1, starting transfers between devices, exchange(): return lax.all_to_all(array, axes, split_axis=0, concat_axis=0, tiled=True)  7.25 us
    all_to_all x1, waiting for transfers between devices, exchange(): return lax.all_to_all(array, axes, split_axis=0, concat_axis=0, tiled=True)  5.53 us
    pallas_call x4, Pallas kernels, shards(): update(iteration == ITERATIONS - 1)  4.58 us
    unnamed x15, local copies, waits for them, and re-layouts  4.58 us
  transfers between devices with their start and end apart: 9, of which 9 were waited for; matrix products, arithmetic and copies ran while one was open for 0% of the time, Pallas kernels for 0%

profile of v6, /device:TPU:0, one launch (start us, length us, event | category | flops | bytes accessed | tf_op | source)
XLA Modules:
  0.0 140.9 jit_solution(5466541526385933958)
XLA Ops:
  0.7 0.8 copy.13.table
  1.4 1.0 copy-done.1
  2.5 1.3 pick.1
  3.8 7.3 %all-to-all-start = ((bf16[32,32,128]{2,1,0:T(8,128)(2,1)}), bf16[32,32,128]{2,1,0:T(8,128)(2,1)S(1)}, u32[]{:S(2)}, u32[]{:S(2)}) async-start(bf16[32,32,128]{2,1,0:T(8,128)(2,1)} %pick.1), calls=%async_computation | async-start | bytes 524288 | tf_op jit(solution)/shard_map/all_to_all | solution.py:153
  11.1 1.8 %copy-done = bf16[92,128,128]{2,1,0:T(8,128)(2,1)S(1)} copy-done((bf16[92,128,128]{2,1,0:T(8,128)(2,1)S(1)}, bf16[92,128,128]{2,1,0:T(8,128)(2,1)}, u32[]{:S(2)}) %copy-start) | copy-done | bytes 3014680
  12.9 0.9 copy-done.3
  13.8 0.5 stage.1
  14.4 5.5 %all-to-all-done.tiles = bf16[32,32,128]{2,1,0:T(8,128)(2,1)S(1)} async-done(((bf16[32,32,128]{2,1,0:T(8,128)(2,1)}), bf16[32,32,128]{2,1,0:T(8,128)(2,1)S(1)}, u32[]{:S(2)}, u32[]{:S(2)}) %all-to-all-start) | async-done | bytes 262176 | tf_op jit(solution)/shard_map/all_to_all | solution.py:153
  20.0 3.0 %model.4 = (f32[16,32,128]{2,1,0:T(8,128)S(1)}, bf16[16,32,128]{2,1,0:T(8,128)(2,1)S(1)}, f32[8,32,128]{2,1,0:T(8,128)}) custom-call(s32[3,92]{1,0:T(4,128)S(1)} %pad_add_fusion.index, bf16[92,128,128]{2,1,0:T(8,128)(2,1)S(1)} %get-tuple-element.19.model, f32[8,32,128]{2,1,0:T(8,128)S(1)} %get-tuple-element.20.measured, ...), custom_call_target="tpu_custom_call" | custom-call | tf_op jit(solution)/shard_map/model/pallas_call | solution.py:228
  23.0 1.3 collective-permute-done.refs_0_
  24.3 14.6 %all_to_all.40 = bf16[16,2,32,128]{3,2,1,0:T(8,128)(2,1)S(1)} all-to-all(bf16[16,2,32,128]{3,2,1,0:T(8,128)(2,1)S(1)} %bitcast.13), channel_id=1, replica_groups=mesh['vox'=8,'hi'=2,'lo'=2] {'vox','hi'}, dimensions={0} | all-to-all | bytes 524288 | tf_op jit(solution)/shard_map/all_to_all | solution.py:153
  39.1 1.3 collective-permute-done.1.refs_1_
  40.5 1.0 update.4
  41.4 12.5 %all_to_all.41.tiles = bf16[32,32,128]{2,1,0:T(8,128)(2,1)S(1)} all-to-all(bf16[32,32,128]{2,1,0:T(8,128)(2,1)S(1)} %get-tuple-element.24), channel_id=1, replica_groups=mesh['vox'=8,'hi'=2,'lo'=2] {'vox'}, dimensions={0} | all-to-all | bytes 524288 | tf_op jit(solution)/shard_map/all_to_all | solution.py:153
  53.9 3.0 %model.5 = (f32[16,32,128]{2,1,0:T(8,128)S(1)}, bf16[16,32,128]{2,1,0:T(8,128)(2,1)S(1)}, f32[8,32,128]{2,1,0:T(8,128)}) custom-call(s32[3,92]{1,0:T(4,128)S(1)} %pad_add_fusion.index, bf16[92,128,128]{2,1,0:T(8,128)(2,1)S(1)} %get-tuple-element.19.model, f32[8,32,128]{2,1,0:T(8,128)S(1)} %get-tuple-element.20.measured, ...), custom_call_target="tpu_custom_call" | custom-call | tf_op jit(solution)/shard_map/model/pallas_call | solution.py:228
  56.9 1.3 collective-permute-done.2.refs_0_
  58.3 13.7 %all_to_all.42 = bf16[16,2,32,128]{3,2,1,0:T(8,128)(2,1)S(1)} all-to-all(bf16[16,2,32,128]{3,2,1,0:T(8,128)(2,1)S(1)} %bitcast.14), channel_id=1, replica_groups=mesh['vox'=8,'hi'=2,'lo'=2] {'vox','hi'}, dimensions={0} | all-to-all | bytes 524288 | tf_op jit(solution)/shard_map/all_to_all | solution.py:153
  72.0 0.1 collective-permute-start.3
  72.1 1.3 collective-permute-done.3.refs_1_
  73.4 1.0 update.5
  74.4 12.5 %all_to_all.43.tiles = bf16[32,32,128]{2,1,0:T(8,128)(2,1)S(1)} all-to-all(bf16[32,32,128]{2,1,0:T(8,128)(2,1)S(1)} %get-tuple-element.28), channel_id=1, replica_groups=mesh['vox'=8,'hi'=2,'lo'=2] {'vox'}, dimensions={0} | all-to-all | bytes 524288 | tf_op jit(solution)/shard_map/all_to_all | solution.py:153
  86.8 3.0 %model.6 = (f32[16,32,128]{2,1,0:T(8,128)S(1)}, bf16[16,32,128]{2,1,0:T(8,128)(2,1)S(1)}, f32[8,32,128]{2,1,0:T(8,128)}) custom-call(s32[3,92]{1,0:T(4,128)S(1)} %pad_add_fusion.index, bf16[92,128,128]{2,1,0:T(8,128)(2,1)S(1)} %get-tuple-element.19.model, f32[8,32,128]{2,1,0:T(8,128)S(1)} %get-tuple-element.20.measured, ...), custom_call_target="tpu_custom_call" | custom-call | tf_op jit(solution)/shard_map/model/pallas_call | solution.py:228
  89.8 1.3 collective-permute-done.4.refs_0_
  91.2 13.7 %all_to_all.44 = bf16[16,2,32,128]{3,2,1,0:T(8,128)(2,1)S(1)} all-to-all(bf16[16,2,32,128]{3,2,1,0:T(8,128)(2,1)S(1)} %bitcast.15), channel_id=1, replica_groups=mesh['vox'=8,'hi'=2,'lo'=2] {'vox','hi'}, dimensions={0} | all-to-all | bytes 524288 | tf_op jit(solution)/shard_map/all_to_all | solution.py:153
  105.0 1.3 collective-permute-done.5.refs_1_
  106.3 1.0 update.6
  107.3 12.5 %all_to_all.45.tiles = bf16[32,32,128]{2,1,0:T(8,128)(2,1)S(1)} all-to-all(bf16[32,32,128]{2,1,0:T(8,128)(2,1)S(1)} %get-tuple-element.32), channel_id=1, replica_groups=mesh['vox'=8,'hi'=2,'lo'=2] {'vox'}, dimensions={0} | all-to-all | bytes 524288 | tf_op jit(solution)/shard_map/all_to_all | solution.py:153
  119.7 3.0 %model.7 = (f32[16,32,128]{2,1,0:T(8,128)S(1)}, bf16[16,32,128]{2,1,0:T(8,128)(2,1)S(1)}, f32[8,32,128]{2,1,0:T(8,128)}) custom-call(s32[3,92]{1,0:T(4,128)S(1)} %pad_add_fusion.index, bf16[92,128,128]{2,1,0:T(8,128)(2,1)S(1)} %get-tuple-element.19.model, f32[8,32,128]{2,1,0:T(8,128)S(1)} %get-tuple-element.20.measured, ...), custom_call_target="tpu_custom_call" | custom-call | tf_op jit(solution)/shard_map/model/pallas_call | solution.py:228
  122.7 1.3 collective-permute-done.6.refs_0_
  124.1 13.7 %all_to_all.46 = bf16[16,2,32,128]{3,2,1,0:T(8,128)(2,1)S(1)} all-to-all(bf16[16,2,32,128]{3,2,1,0:T(8,128)(2,1)S(1)} %bitcast.16), channel_id=1, replica_groups=mesh['vox'=8,'hi'=2,'lo'=2] {'vox','hi'}, dimensions={0} | all-to-all | bytes 524288 | tf_op jit(solution)/shard_map/all_to_all | solution.py:153
  137.9 1.3 collective-permute-done.7.refs_1_
  139.2 1.7 %update.7 = f32[32,32,128]{2,1,0:T(8,128)} custom-call(s32[1]{0:T(128)} %bitcast.ids, s32[1,8,4]{2,1,0:T(8,128)S(1)} %copy.13.table, f32[32,128]{1,0:T(8,128)S(1)} %broadcast_in_dim.10.gains, f32[32,32,128]{2,1,0:T(8,128)S(1)} %get-tuple-element.31.image, bf16[16,32,128]{2,1,0:T(8,128)(2,1)S(1)} %merge.7.refs_0_, ...), custom_call_target="tpu_custom_call" | custom-call | tf_op jit(solution)/shard_map/update/pallas_call | solution.py:233
  (29 shorter events, 0.6 us)
Async XLA Ops:
  0.6 13.7 %copy-start.5 = (s32[92]{0:T(128)S(1)}, s32[92]{0:T(128)}, u32[]{:S(2)}) copy-start(s32[92]{0:T(128)} %param.13) | copy-start | bytes 1108
  0.6 13.8 %copy-start.4 = (s32[92]{0:T(128)S(1)}, s32[92]{0:T(128)}, u32[]{:S(2)}) copy-start(s32[92]{0:T(128)} %param.12) | copy-start | bytes 1108
  1.4 1.0 copy-start.1
  3.8 16.2 %all-to-all-start = ((bf16[32,32,128]{2,1,0:T(8,128)(2,1)}), bf16[32,32,128]{2,1,0:T(8,128)(2,1)S(1)}, u32[]{:S(2)}, u32[]{:S(2)}) async-start(bf16[32,32,128]{2,1,0:T(8,128)(2,1)} %pick.1), calls=%async_computation | async-start | bytes 524288 | tf_op jit(solution)/shard_map/all_to_all | solution.py:153
  11.1 1.9 %copy-start = (bf16[92,128,128]{2,1,0:T(8,128)(2,1)S(1)}, bf16[92,128,128]{2,1,0:T(8,128)(2,1)}, u32[]{:S(2)}) copy-start(bf16[92,128,128]{2,1,0:T(8,128)(2,1)} %refs_0_.1) | copy-start | bytes 9043972
  12.9 0.9 copy-start.3
  14.4 26.0 %copy-start.6 = (f32[32]{0:T(128)S(1)}, f32[32]{0:T(128)}, u32[]{:S(2)}) copy-start(f32[32]{0:T(128)} %param.10) | copy-start | bytes 388
  20.0 20.5 %copy-start.2 = (f32[32,32,128]{2,1,0:T(8,128)S(1)}, f32[32,32,128]{2,1,0:T(8,128)}, u32[]{:S(2)}) copy-start(f32[32,32,128]{2,1,0:T(8,128)} %image.3) | copy-start | bytes 1572868
  23.0 1.3 collective-permute-start
  39.0 1.4 %collective-permute-start.1 = (bf16[16,32,128]{2,1,0:T(8,128)(2,1)S(1)}, bf16[16,32,128]{2,1,0:T(8,128)(2,1)S(1)}, u32[]{:S(2)}, u32[]{:S(2)}) collective-permute-start(bf16[16,32,128]{2,1,0:T(8,128)(2,1)S(1)} %merge.4.refs_0_), channel_id=1, source_target_pairs={{0,1},{1,0},{2,3},{3,2},{4,5},{5,4},{6,7},{7,6},{8,9},{9,8},{10,11... | collective-permute-start | bytes 393224 | tf_op jit(solution)/shard_map/ppermute | solution.py:150
  56.9 1.3 collective-permute-start.2
  72.0 1.4 %collective-permute-start.3 = (bf16[16,32,128]{2,1,0:T(8,128)(2,1)S(1)}, bf16[16,32,128]{2,1,0:T(8,128)(2,1)S(1)}, u32[]{:S(2)}, u32[]{:S(2)}) collective-permute-start(bf16[16,32,128]{2,1,0:T(8,128)(2,1)S(1)} %merge.5.refs_0_), channel_id=1, source_target_pairs={{0,1},{1,0},{2,3},{3,2},{4,5},{5,4},{6,7},{7,6},{8,9},{9,8},{10,11... | collective-permute-start | bytes 393224 | tf_op jit(solution)/shard_map/ppermute | solution.py:150
  89.8 1.3 collective-permute-start.4
  104.9 1.4 %collective-permute-start.5 = (bf16[16,32,128]{2,1,0:T(8,128)(2,1)S(1)}, bf16[16,32,128]{2,1,0:T(8,128)(2,1)S(1)}, u32[]{:S(2)}, u32[]{:S(2)}) collective-permute-start(bf16[16,32,128]{2,1,0:T(8,128)(2,1)S(1)} %merge.6.refs_0_), channel_id=1, source_target_pairs={{0,1},{1,0},{2,3},{3,2},{4,5},{5,4},{6,7},{7,6},{8,9},{9,8},{10,11... | collective-permute-start | bytes 393224 | tf_op jit(solution)/shard_map/ppermute | solution.py:150
  122.7 1.3 collective-permute-start.6
  137.8 1.4 %collective-permute-start.7 = (bf16[16,32,128]{2,1,0:T(8,128)(2,1)S(1)}, bf16[16,32,128]{2,1,0:T(8,128)(2,1)S(1)}, u32[]{:S(2)}, u32[]{:S(2)}) collective-permute-start(bf16[16,32,128]{2,1,0:T(8,128)(2,1)S(1)} %merge.7.refs_0_), channel_id=1, source_target_pairs={{0,1},{1,0},{2,3},{3,2},{4,5},{5,4},{6,7},{7,6},{8,9},{9,8},{10,11... | collective-permute-start | bytes 393224 | tf_op jit(solution)/shard_map/ppermute | solution.py:150

commit v7 on v6

v7 whole, which is shorter than its diff:
```python
import functools
import math

import jax
import jax.numpy as jnp
from jax import lax
from jax.experimental import pallas as pl
from jax.experimental.pallas import tpu as pltpu
from jax.sharding import Mesh, PartitionSpec as P

ITERATIONS = 4


VMEM = pl.BlockSpec(memory_space=pltpu.VMEM)
SMEM = pl.BlockSpec(memory_space=pltpu.SMEM)
PARAMS = pltpu.CompilerParams(vmem_limit_bytes=32 * 1024 * 1024)


def grouped(source, index, column, d, model, k, size, dims):
    left = [source[index[d, column, k + i]] for i in range(size)]
    blocks = [model[k + i] for i in range(size)]
    if size < 4:
        return [
            lax.dot_general(x, block, dims, preferred_element_type=jnp.float32)
            for x, block in zip(left, blocks)
        ]
    zero = jnp.zeros_like(left[0])
    rows = jnp.concatenate(
        [
            jnp.concatenate([x, zero] if i % 2 == 0 else [zero, x], axis=1)
            for i, x in enumerate(left)
        ],
        axis=0,
    )
    depth = dims[0][1][0]
    halves = [jnp.concatenate(blocks[n : n + 2], axis=depth) for n in (0, 2)]
    whole = jnp.concatenate(halves, axis=1 - depth)
    out = lax.dot_general(rows, whole, dims, preferred_element_type=jnp.float32)
    height, width = left[0].shape[0], out.shape[1] // 2
    return [
        out[i * height : (i + 1) * height, i // 2 * width : (i // 2 + 1) * width]
        for i in range(4)
    ]


def model_kernel(lo_count, index, measured, tiles, *refs):
    models = refs[:lo_count]
    out, residual, narrow, sums = refs[lo_count:]
    vox_count, hi_count, capacity = out.shape[:3]
    count = models[0].shape[0]
    residual[...] = measured[...]
    sums[...] = jnp.zeros_like(sums)
    for d, model in enumerate(models):
        for k in range(0, count, 4):
            for i, part in enumerate(
                grouped(
                    tiles, index, 0, d, model, k, min(4, count - k), (((1,), (1,)), ((), ()))
                )
            ):
                residual[index[d, 1, k + i]] -= part
    narrow[...] = residual[...].astype(jnp.bfloat16)
    for d, model in enumerate(models):
        for k in range(0, count, 4):
            for i, part in enumerate(
                grouped(
                    narrow, index, 1, d, model, k, min(4, count - k), (((1,), (0,)), ((), ()))
                )
            ):
                sums[index[d, 0, k + i]] += part
    for v in range(vox_count):
        piece = sums[v * capacity : (v + 1) * capacity].astype(jnp.bfloat16)
        for h in range(hi_count):
            out[v, h] = piece


def stage_kernel(*refs):
    *pairs, sems = refs
    half = len(pairs) // 2
    copies = [
        pltpu.make_async_copy(pairs[i], pairs[half + i], sems.at[i]) for i in range(half)
    ]
    for copy in copies:
        copy.start()
    for copy in copies:
        copy.wait()


def pick_tiles(table, image, out):
    _, vox_count, capacity = table.shape
    for v in range(vox_count):
        for s in range(capacity):
            tile = jnp.maximum(table[0, v, s], 0)
            out[v * capacity + s] = image[tile].astype(jnp.bfloat16)


def part_of(lo, size):
    return (slice(None), pl.ds(pl.multiple_of(lo * size, size), size))


def pick_kernel(lo, table, image, part, out):
    part[...] = image[part_of(lo[0], part.shape[1])]
    pick_tiles(table, part, out)


def update_kernel(table, gains, image, parts, estimate, *refs):
    *outs, gradient = refs
    vox_count, hi_count, capacity = parts.shape[:3]
    gradient[...] = jnp.zeros_like(gradient)
    for v in range(vox_count):
        for s in range(capacity):
            tile = jnp.maximum(table[0, v, s], 0)
            total = parts[v, 0, s].astype(jnp.float32)
            for h in range(1, hi_count):
                total = total + parts[v, h, s].astype(jnp.float32)
            gradient[tile] += total
    estimate[...] = jnp.maximum(image[...] + gains[...][None] * gradient[...], 0.0)
    if outs:
        pick_tiles(table, estimate, *outs)


def join_kernel(lo, *refs):
    *parts, out = refs
    for d, part in enumerate(parts):
        out[part_of(lo[0] ^ d, part.shape[1])] = part[...]


def shards(model_blocks, start_image, measured, step_size, sent_tiles, block_rows, block_slots):
    vox_count = lax.axis_size("vox")
    hi_count = lax.axis_size("hi")
    lo_count = lax.axis_size("lo")
    lo = lax.axis_index("lo")
    capacity = sent_tiles.shape[2]
    tile_count, wave_count, width = start_image.shape
    row_count = measured.shape[0]
    slot_count = vox_count * capacity
    waves = wave_count // lo_count
    tile = (waves, width)
    ids = lo.astype(jnp.int32)[None]

    def shape(count, dtype):
        return jax.ShapeDtypeStruct((count, *tile), dtype)

    def swap(array, d):
        pairs = [(i, i ^ d) for i in range(lo_count)]
        return lax.ppermute(array, "lo", pairs) if d else array

    def exchange(array, axes):
        return lax.all_to_all(array, axes, split_axis=0, concat_axis=0, tiled=True)

    def call(kernel, out_shape, in_specs, scratch, name, **options):
        return pl.pallas_call(
            kernel,
            out_shape=out_shape,
            in_specs=in_specs,
            out_specs=[VMEM] * len(out_shape),
            scratch_shapes=scratch,
            compiler_params=PARAMS,
            name=name,
            **options,
        )

    pick = call(
        pick_kernel,
        [shape(tile_count, jnp.float32), shape(slot_count, jnp.bfloat16)],
        [SMEM, SMEM, VMEM],
        [],
        "pick",
    )
    stage = call(
        stage_kernel,
        [jax.ShapeDtypeStruct(model_blocks.shape, model_blocks.dtype)] * lo_count,
        [pl.BlockSpec(memory_space=pltpu.HBM)] * lo_count,
        [pltpu.SemaphoreType.DMA((lo_count,))],
        "stage",
        cost_estimate=pl.CostEstimate(
            flops=0, bytes_accessed=4 * lo_count * model_blocks.size, transcendentals=0
        ),
    )
    apply_model = call(
        functools.partial(model_kernel, lo_count),
        [
            jax.ShapeDtypeStruct((vox_count, hi_count, capacity, *tile), jnp.bfloat16),
            shape(lo_count * row_count, jnp.float32),
        ],
        [SMEM, VMEM, VMEM] + [VMEM] * lo_count,
        [
            pltpu.VMEM((lo_count * row_count, *tile), jnp.bfloat16),
            pltpu.VMEM((slot_count, *tile), jnp.float32),
        ],
        "model",
    )

    def update(last):
        outs = [] if last else [shape(slot_count, jnp.bfloat16)]
        return call(
            update_kernel,
            [shape(tile_count, jnp.float32)] + outs,
            [SMEM, VMEM, VMEM, VMEM],
            [pltpu.VMEM((tile_count, *tile), jnp.float32)],
            "update",
        )

    def join(parts):
        count = parts[0].shape[0]
        whole = jax.ShapeDtypeStruct((count, wave_count, width), jnp.float32)
        return call(join_kernel, [whole], [SMEM] + [VMEM] * lo_count, [], "join")(ids, *parts)[0]

    def waves_of(array, d):
        cut = array.reshape(array.shape[0], lo_count, *tile)
        return lax.dynamic_index_in_dim(cut, lo ^ d, 1, keepdims=False)

    shared = [swap(model_blocks, d) for d in range(lo_count)]
    estimate, outgoing = pick(ids, sent_tiles, start_image)
    tiles = exchange(outgoing, "vox")
    models = stage(*shared)
    signals = jnp.concatenate([swap(waves_of(measured, d), d) for d in range(lo_count)])
    index = jnp.stack([block_slots, block_rows])
    index = jnp.stack(
        [swap(index, d) + jnp.array([[0], [d * row_count]], jnp.int32) for d in range(lo_count)]
    )
    gains = jnp.broadcast_to(
        lax.dynamic_slice_in_dim(step_size, lo * waves, waves)[:, None], tile
    )
    for iteration in range(ITERATIONS):
        total, residual = apply_model(index, signals, tiles, *models)
        total = total.reshape(vox_count * hi_count, capacity, *tile)
        parts = exchange(total, ("vox", "hi")).reshape(vox_count, hi_count, capacity, *tile)
        estimate, *outgoing = update(iteration == ITERATIONS - 1)(
            sent_tiles, gains, estimate, parts
        )
        if outgoing:
            tiles = exchange(*outgoing, "vox")
    residual = join(
        [swap(residual[d * row_count : (d + 1) * row_count], d) for d in range(lo_count)]
    )
    estimate = join([swap(estimate, d) for d in range(lo_count)])
    return (estimate, residual)


def solution(mesh):
    vox_count, chan_count = mesh.devices.shape
    lo_count = math.gcd(chan_count, 2)
    cut = Mesh(
        mesh.devices.reshape(vox_count, chan_count // lo_count, lo_count), ("vox", "hi", "lo")
    )
    everywhere = ("vox", "hi", "lo")
    in_specs = (
        P(everywhere, None, None),
        P("vox", None, None),
        P(everywhere, None, None),
        P(),
        P("vox", None, None),
        P(everywhere),
        P(everywhere),
    )
    out_specs = (P("vox", None, None), P(everywhere, None, None))
    return jax.shard_map(shards, mesh=cut, in_specs=in_specs, out_specs=out_specs, check_vma=False)
```

time: 142 us -> 136 us (0.958)
  blocking collectives: 93 us -> 64.8 us
  local copies, waits for them, and re-layouts: 4.65 us -> 15.8 us
  starting transfers between devices: 7.55 us -> 15.6 us
  Pallas kernels: 18.7 us -> 24.1 us
  waiting for transfers between devices: 16.2 us -> 12.3 us
    all_to_all x7 -> x6, blocking collectives: 93 us -> 64.8 us  [exchange(): return lax.all_to_all(array, axes, split_axis=0, concat_axis=0, tiled=True)]
    unnamed x15 -> x25, local copies, waits for them, and re-layouts: 4.58 us -> 14.7 us
    ppermute x8 -> x5, waiting for transfers between devices: 10.7 us -> 2.17 us  [swap(): return lax.ppermute(array, 'lo', pairs) if d else array]
    all_to_all x1 -> x2, starting transfers between devices: 7.25 us -> 14.3 us  [exchange(): return lax.all_to_all(array, axes, split_axis=0, concat_axis=0, tiled=True)]
    pallas_call x18 -> x12, Pallas kernels: 18.7 us -> 24.1 us  [the longest x4 17.1 us: shards(): total, residual = apply_model(index, signals, tiles, *models)]
    all_to_all x1 -> x2, waiting for transfers between devices: 5.53 us -> 10.1 us  [exchange(): return lax.all_to_all(array, axes, split_axis=0, concat_axis=0, tiled=True)]
  transfers between devices with their start and end apart: 9 -> 7, of which waited for: 9 -> 3; matrix products, arithmetic and copies ran while one was open for 0% -> 2% of each run, Pallas kernels for 0% -> 2%
where the time goes in v7:
time: 136 us; the launch traced here: 135 us
  blocking collectives  64.8 us (48%)
  Pallas kernels  24.1 us (18%)
  local copies, waits for them, and re-layouts  15.8 us (12%)
  starting transfers between devices  15.6 us (11%)
  waiting for transfers between devices  12.3 us (9%)
  other arithmetic  1.44 us (1%)
    all_to_all x6, blocking collectives, exchange(): return lax.all_to_all(array, axes, split_axis=0, concat_axis=0, tiled=True)  64.8 us
    pallas_call x4, Pallas kernels, shards(): total, residual = apply_model(index, signals, tiles, *models)  17.1 us
    unnamed x25, local copies, waits for them, and re-layouts  14.7 us
    all_to_all x2, starting transfers between devices, exchange(): return lax.all_to_all(array, axes, split_axis=0, concat_axis=0, tiled=True)  14.3 us
    all_to_all x2, waiting for transfers between devices, exchange(): return lax.all_to_all(array, axes, split_axis=0, concat_axis=0, tiled=True)  10.1 us
    pallas_call x4, Pallas kernels, shards(): update(iteration == ITERATIONS - 1)(sent_tiles, gains, estimate, parts)  3.41 us
  transfers between devices with their start and end apart: 7, of which 3 were waited for; matrix products, arithmetic and copies ran while one was open for 2% of the time, Pallas kernels for 2%

profile of v7, /device:TPU:0, one launch (start us, length us, event | category | flops | bytes accessed | tf_op | source)
XLA Modules:
  0.0 134.8 jit_solution(1629293699256821331)
XLA Ops:
  1.1 0.9 dynamic-slice_bitcast_fusion.1
  2.2 0.8 copy.17.table
  2.9 1.0 copy-done.7
  4.0 1.3 pick.1
  6.0 7.3 %all-to-all-start = ((bf16[32,16,128]{2,1,0:T(8,128)(2,1)}), bf16[32,16,128]{2,1,0:T(8,128)(2,1)S(1)}, u32[]{:S(2)}, u32[]{:S(2)}) async-start(bf16[32,16,128]{2,1,0:T(8,128)(2,1)} %get-tuple-element.18), calls=%async_computation | async-start | bytes 262144 | tf_op jit(solution)/shard_map/all_to_all | solution.py:148
  13.9 1.1 collective-permute-done
  15.8 1.6 %copy-done.5 = bf16[92,128,128]{2,1,0:T(8,128)(2,1)} copy-done((bf16[92,128,128]{2,1,0:T(8,128)(2,1)}, bf16[92,128,128]{2,1,0:T(8,128)(2,1)S(1)}, u32[]{:S(2)}) %copy-start.5) | copy-done | bytes 3014680
  17.4 1.9 %copy-done.4 = bf16[92,128,128]{2,1,0:T(8,128)(2,1)S(1)} copy-done((bf16[92,128,128]{2,1,0:T(8,128)(2,1)S(1)}, bf16[92,128,128]{2,1,0:T(8,128)(2,1)}, u32[]{:S(2)}) %copy-start.4) | copy-done | bytes 3014680
  19.3 1.9 %copy-done.6 = bf16[92,128,128]{2,1,0:T(8,128)(2,1)S(1)} copy-done((bf16[92,128,128]{2,1,0:T(8,128)(2,1)S(1)}, bf16[92,128,128]{2,1,0:T(8,128)(2,1)}, u32[]{:S(2)}) %copy-start.6) | copy-done | bytes 3014680
  21.1 0.7 stage.1
  21.9 1.6 %copy-done = bf16[92,128,128]{2,1,0:T(8,128)(2,1)} copy-done((bf16[92,128,128]{2,1,0:T(8,128)(2,1)}, bf16[92,128,128]{2,1,0:T(8,128)(2,1)S(1)}, u32[]{:S(2)}) %copy-start) | copy-done | bytes 3014680
  23.5 1.9 %copy-done.1 = bf16[92,128,128]{2,1,0:T(8,128)(2,1)S(1)} copy-done((bf16[92,128,128]{2,1,0:T(8,128)(2,1)S(1)}, bf16[92,128,128]{2,1,0:T(8,128)(2,1)}, u32[]{:S(2)}) %copy-start.1) | copy-done | bytes 3014680
  25.3 4.4 %model.4 = (bf16[8,2,4,16,128]{4,3,2,1,0:T(8,128)(2,1)S(1)}, f32[16,16,128]{2,1,0:T(8,128)}) custom-call(s32[2,2,92]{2,1,0:T(2,128)S(1)} %pad_add_fusion.index, f32[16,16,128]{2,1,0:T(8,128)S(1)} %pad_maximum_fusion.measured, bf16[32,16,128]{2,1,0:T(8,128)(2,1)S(1)} %all-to-all-done.tiles, bf16[92,128,128]{2,1,0:T(8,128)(2,1)S(1)} %get-tuple-element.19.refs_0_, ...), custom_call_target="tpu_custom_call" | custom-call | tf_op jit(solution)/shard_map/model/pallas_call | solution.py:225
  30.4 7.1 %all-to-all-start.1 = ((bf16[16,4,16,128]{3,2,1,0:T(8,128)(2,1)}), bf16[16,4,16,128]{3,2,1,0:T(8,128)(2,1)S(1)}, u32[]{:S(2)}, u32[]{:S(2)}) async-start(bf16[16,4,16,128]{3,2,1,0:T(8,128)(2,1)} %bitcast.28), calls=%async_computation.1 | async-start | bytes 524288 | tf_op jit(solution)/shard_map/all_to_all | solution.py:148
  37.6 10.1 %all-to-all-done.1 = bf16[16,4,16,128]{3,2,1,0:T(8,128)(2,1)S(1)} async-done(((bf16[16,4,16,128]{3,2,1,0:T(8,128)(2,1)}), bf16[16,4,16,128]{3,2,1,0:T(8,128)(2,1)S(1)}, u32[]{:S(2)}, u32[]{:S(2)}) %all-to-all-start.1) | async-done | bytes 262176 | tf_op jit(solution)/shard_map/all_to_all | solution.py:148
  47.8 0.9 copy-done.9
  48.8 0.9 update.4
  49.6 10.6 %all_to_all.40.tiles = bf16[32,16,128]{2,1,0:T(8,128)(2,1)S(1)} all-to-all(bf16[32,16,128]{2,1,0:T(8,128)(2,1)S(1)} %get-tuple-element.23), channel_id=1, replica_groups=mesh['vox'=8,'hi'=2,'lo'=2] {'vox'}, dimensions={0} | all-to-all | bytes 262144 | tf_op jit(solution)/shard_map/all_to_all | solution.py:148
  60.2 1.9 %copy-done.2 = bf16[92,128,128]{2,1,0:T(8,128)(2,1)S(1)} copy-done((bf16[92,128,128]{2,1,0:T(8,128)(2,1)S(1)}, bf16[92,128,128]{2,1,0:T(8,128)(2,1)}, u32[]{:S(2)}) %copy-start.2) | copy-done | bytes 3014680
  62.0 4.4 %model.5 = (bf16[8,2,4,16,128]{4,3,2,1,0:T(8,128)(2,1)S(1)}, f32[16,16,128]{2,1,0:T(8,128)}) custom-call(s32[2,2,92]{2,1,0:T(2,128)S(1)} %pad_add_fusion.index, f32[16,16,128]{2,1,0:T(8,128)S(1)} %pad_maximum_fusion.measured, bf16[32,16,128]{2,1,0:T(8,128)(2,1)S(1)} %all_to_all.40.tiles, bf16[92,128,128]{2,1,0:T(8,128)(2,1)S(1)} %get-tuple-element.19.refs_0_, ...), custom_call_target="tpu_custom_call" | custom-call | tf_op jit(solution)/shard_map/model/pallas_call | solution.py:225
  66.5 11.1 %all_to_all.41 = bf16[16,4,16,128]{3,2,1,0:T(8,128)(2,1)S(1)} all-to-all(bf16[16,4,16,128]{3,2,1,0:T(8,128)(2,1)S(1)} %bitcast.30), channel_id=1, replica_groups=mesh['vox'=8,'hi'=2,'lo'=2] {'vox','hi'}, dimensions={0} | all-to-all | bytes 524288 | tf_op jit(solution)/shard_map/all_to_all | solution.py:148
  77.5 0.9 update.5
  78.4 10.5 %all_to_all.42.tiles = bf16[32,16,128]{2,1,0:T(8,128)(2,1)S(1)} all-to-all(bf16[32,16,128]{2,1,0:T(8,128)(2,1)S(1)} %get-tuple-element.26), channel_id=1, replica_groups=mesh['vox'=8,'hi'=2,'lo'=2] {'vox'}, dimensions={0} | all-to-all | bytes 262144 | tf_op jit(solution)/shard_map/all_to_all | solution.py:148
  88.9 4.4 %model.6 = (bf16[8,2,4,16,128]{4,3,2,1,0:T(8,128)(2,1)S(1)}, f32[16,16,128]{2,1,0:T(8,128)}) custom-call(s32[2,2,92]{2,1,0:T(2,128)S(1)} %pad_add_fusion.index, f32[16,16,128]{2,1,0:T(8,128)S(1)} %pad_maximum_fusion.measured, bf16[32,16,128]{2,1,0:T(8,128)(2,1)S(1)} %all_to_all.42.tiles, bf16[92,128,128]{2,1,0:T(8,128)(2,1)S(1)} %get-tuple-element.19.refs_0_, ...), custom_call_target="tpu_custom_call" | custom-call | tf_op jit(solution)/shard_map/model/pallas_call | solution.py:225
  93.3 11.1 %all_to_all.43 = bf16[16,4,16,128]{3,2,1,0:T(8,128)(2,1)S(1)} all-to-all(bf16[16,4,16,128]{3,2,1,0:T(8,128)(2,1)S(1)} %bitcast.31), channel_id=1, replica_groups=mesh['vox'=8,'hi'=2,'lo'=2] {'vox','hi'}, dimensions={0} | all-to-all | bytes 524288 | tf_op jit(solution)/shard_map/all_to_all | solution.py:148
  104.4 0.9 update.6
  105.3 10.5 %all_to_all.44.tiles = bf16[32,16,128]{2,1,0:T(8,128)(2,1)S(1)} all-to-all(bf16[32,16,128]{2,1,0:T(8,128)(2,1)S(1)} %get-tuple-element.29), channel_id=1, replica_groups=mesh['vox'=8,'hi'=2,'lo'=2] {'vox'}, dimensions={0} | all-to-all | bytes 262144 | tf_op jit(solution)/shard_map/all_to_all | solution.py:148
  115.8 3.8 %model.7 = (bf16[8,2,4,16,128]{4,3,2,1,0:T(8,128)(2,1)S(1)}, f32[16,16,128]{2,1,0:T(8,128)S(1)}) custom-call(s32[2,2,92]{2,1,0:T(2,128)S(1)} %pad_add_fusion.index, f32[16,16,128]{2,1,0:T(8,128)S(1)} %pad_maximum_fusion.measured, bf16[32,16,128]{2,1,0:T(8,128)(2,1)S(1)} %all_to_all.44.tiles, bf16[92,128,128]{2,1,0:T(8,128)(2,1)S(1)} %get-tuple-element.19.refs_0_, ...), custom_call_target="tpu_custom_call" | custom-call | tf_op jit(solution)/shard_map/model/pallas_call | solution.py:225
  119.6 11.1 %all_to_all.45 = bf16[16,4,16,128]{3,2,1,0:T(8,128)(2,1)S(1)} all-to-all(bf16[16,4,16,128]{3,2,1,0:T(8,128)(2,1)S(1)} %bitcast.29), channel_id=1, replica_groups=mesh['vox'=8,'hi'=2,'lo'=2] {'vox','hi'}, dimensions={0} | all-to-all | bytes 524288 | tf_op jit(solution)/shard_map/all_to_all | solution.py:148
  130.7 0.8 update.7.refs_0_
  132.2 1.0 collective-permute-done.4.refs_1_
  133.9 0.8 join.2
  (34 shorter events, 5.0 us)
Async XLA Ops:
  0.6 15.2 %collective-permute-start.2 = (bf16[92,128,128]{2,1,0:T(8,128)(2,1)}, bf16[92,128,128]{2,1,0:T(8,128)(2,1)S(1)}, u32[]{:S(2)}, u32[]{:S(2)}) collective-permute-start(bf16[92,128,128]{2,1,0:T(8,128)(2,1)} %refs_0_.1), channel_id=1, source_target_pairs={{0,1},{1,0},{2,3},{3,2},{4,5},{5,4},{6,7},{7,6},{8,9},{9,8},{10,11... | collective-permute-start | bytes 9043976 | tf_op jit(solution)/shard_map/ppermute | solution.py:145
  2.0 13.8 %collective-permute-start.1 = (f32[8,16,128]{2,1,0:T(8,128)S(1)}, f32[8,16,128]{2,1,0:T(8,128)S(1)}, u32[]{:S(2)}, u32[]{:S(2)}) collective-permute-start(f32[8,16,128]{2,1,0:T(8,128)S(1)} %get-tuple-element.35), channel_id=1, source_target_pairs={{0,1},{1,0},{2,3},{3,2},{4,5},{5,4},{6,7},{7,6},{8,9},{9,8},{10,11... | collective-permute-start | bytes 196616 | tf_op jit(solution)/shard_map/ppermute | solution.py:145
  2.9 1.0 copy-start.7
  5.3 0.7 copy-start.8
  6.0 17.5 %all-to-all-start = ((bf16[32,16,128]{2,1,0:T(8,128)(2,1)}), bf16[32,16,128]{2,1,0:T(8,128)(2,1)S(1)}, u32[]{:S(2)}, u32[]{:S(2)}) async-start(bf16[32,16,128]{2,1,0:T(8,128)(2,1)} %get-tuple-element.18), calls=%async_computation | async-start | bytes 262144 | tf_op jit(solution)/shard_map/all_to_all | solution.py:148
  13.9 1.1 collective-permute-start
  15.8 1.6 %copy-start.5 = (bf16[92,128,128]{2,1,0:T(8,128)(2,1)}, bf16[92,128,128]{2,1,0:T(8,128)(2,1)S(1)}, u32[]{:S(2)}) copy-start(bf16[92,128,128]{2,1,0:T(8,128)(2,1)S(1)} %collective-permute-done.2.refs_1_) | copy-start | bytes 9043972
  17.4 1.9 %copy-start.4 = (bf16[92,128,128]{2,1,0:T(8,128)(2,1)S(1)}, bf16[92,128,128]{2,1,0:T(8,128)(2,1)}, u32[]{:S(2)}) copy-start(bf16[92,128,128]{2,1,0:T(8,128)(2,1)} %refs_0_.1) | copy-start | bytes 9043972
  19.3 1.9 %copy-start.6 = (bf16[92,128,128]{2,1,0:T(8,128)(2,1)S(1)}, bf16[92,128,128]{2,1,0:T(8,128)(2,1)}, u32[]{:S(2)}) copy-start(bf16[92,128,128]{2,1,0:T(8,128)(2,1)} %copy-done.5) | copy-start | bytes 9043972
  21.9 1.6 %copy-start = (bf16[92,128,128]{2,1,0:T(8,128)(2,1)}, bf16[92,128,128]{2,1,0:T(8,128)(2,1)S(1)}, u32[]{:S(2)}) copy-start(bf16[92,128,128]{2,1,0:T(8,128)(2,1)S(1)} %get-tuple-element.20.refs_1_) | copy-start | bytes 9043972
  23.5 1.9 %copy-start.1 = (bf16[92,128,128]{2,1,0:T(8,128)(2,1)S(1)}, bf16[92,128,128]{2,1,0:T(8,128)(2,1)}, u32[]{:S(2)}) copy-start(bf16[92,128,128]{2,1,0:T(8,128)(2,1)} %copy-done) | copy-start | bytes 9043972
  25.3 12.2 %copy-start.11 = (f32[32]{0:T(128)S(1)}, f32[32]{0:T(128)}, u32[]{:S(2)}) copy-start(f32[32]{0:T(128)} %param.12) | copy-start | bytes 388
  29.8 0.7 copy-start.10
  30.4 17.3 %all-to-all-start.1 = ((bf16[16,4,16,128]{3,2,1,0:T(8,128)(2,1)}), bf16[16,4,16,128]{3,2,1,0:T(8,128)(2,1)S(1)}, u32[]{:S(2)}, u32[]{:S(2)}) async-start(bf16[16,4,16,128]{3,2,1,0:T(8,128)(2,1)} %bitcast.28), calls=%async_computation.1 | async-start | bytes 524288 | tf_op jit(solution)/shard_map/all_to_all | solution.py:148
  47.8 1.0 copy-start.9
  60.2 1.9 %copy-start.2 = (bf16[92,128,128]{2,1,0:T(8,128)(2,1)S(1)}, bf16[92,128,128]{2,1,0:T(8,128)(2,1)}, u32[]{:S(2)}) copy-start(bf16[92,128,128]{2,1,0:T(8,128)(2,1)} %copy-done) | copy-start | bytes 9043972
  62.0 26.9 %copy-start.3 = (bf16[92,128,128]{2,1,0:T(8,128)(2,1)S(1)}, bf16[92,128,128]{2,1,0:T(8,128)(2,1)}, u32[]{:S(2)}) copy-start(bf16[92,128,128]{2,1,0:T(8,128)(2,1)} %copy-done) | copy-start | bytes 9043972
  131.6 2.4 %collective-permute-start.3 = (f32[32,16,128]{2,1,0:T(8,128)S(1)}, f32[32,16,128]{2,1,0:T(8,128)S(1)}, u32[]{:S(2)}, u32[]{:S(2)}) collective-permute-start(f32[32,16,128]{2,1,0:T(8,128)S(1)} %update.7.refs_0_), channel_id=1, source_target_pairs={{0,1},{1,0},{2,3},{3,2},{4,5},{5,4},{6,7},{7,6},{8,9},{9,8},{10,11... | collective-permute-start | bytes 786440 | tf_op jit(solution)/shard_map/ppermute | solution.py:145
  131.7 1.6 %collective-permute-start.4 = (f32[8,16,128]{2,1,0:T(8,128)S(1)}, f32[8,16,128]{2,1,0:T(8,128)S(1)}, u32[]{:S(2)}, u32[]{:S(2)}) collective-permute-start(f32[8,16,128]{2,1,0:T(8,128)S(1)} %get-tuple-element.32), channel_id=1, source_target_pairs={{0,1},{1,0},{2,3},{3,2},{4,5},{5,4},{6,7},{7,6},{8,9},{9,8},{10,11... | collective-permute-start | bytes 196616 | tf_op jit(solution)/shard_map/ppermute | solution.py:145

commit v8 on v7

--- a/solution.py
+++ b/solution.py
@@ -13,7 +13,7 @@
 
 VMEM = pl.BlockSpec(memory_space=pltpu.VMEM)
 SMEM = pl.BlockSpec(memory_space=pltpu.SMEM)
-PARAMS = pltpu.CompilerParams(vmem_limit_bytes=32 * 1024 * 1024)
+PARAMS = pltpu.CompilerParams(vmem_limit_bytes=16 * 1024 * 1024)
 
 
 def grouped(source, index, column, d, model, k, size, dims):
@@ -73,18 +73,6 @@
             out[v, h] = piece
 
 
-def stage_kernel(*refs):
-    *pairs, sems = refs
-    half = len(pairs) // 2
-    copies = [
-        pltpu.make_async_copy(pairs[i], pairs[half + i], sems.at[i]) for i in range(half)
-    ]
-    for copy in copies:
-        copy.start()
-    for copy in copies:
-        copy.wait()
-
-
 def pick_tiles(table, image, out):
     _, vox_count, capacity = table.shape
     for v in range(vox_count):
@@ -147,7 +135,7 @@
     def exchange(array, axes):
         return lax.all_to_all(array, axes, split_axis=0, concat_axis=0, tiled=True)
 
-    def call(kernel, out_shape, in_specs, scratch, name, **options):
+    def call(kernel, out_shape, in_specs, scratch, name):
         return pl.pallas_call(
             kernel,
             out_shape=out_shape,
@@ -156,7 +144,6 @@
             scratch_shapes=scratch,
             compiler_params=PARAMS,
             name=name,
-            **options,
         )
 
     pick = call(
@@ -165,16 +152,6 @@
         [SMEM, SMEM, VMEM],
         [],
         "pick",
-    )
-    stage = call(
-        stage_kernel,
-        [jax.ShapeDtypeStruct(model_blocks.shape, model_blocks.dtype)] * lo_count,
-        [pl.BlockSpec(memory_space=pltpu.HBM)] * lo_count,
-        [pltpu.SemaphoreType.DMA((lo_count,))],
-        "stage",
-        cost_estimate=pl.CostEstimate(
-            flops=0, bytes_accessed=4 * lo_count * model_blocks.size, transcendentals=0
-        ),
     )
     apply_model = call(
         functools.partial(model_kernel, lo_count),
@@ -209,10 +186,9 @@
         cut = array.reshape(array.shape[0], lo_count, *tile)
         return lax.dynamic_index_in_dim(cut, lo ^ d, 1, keepdims=False)
 
-    shared = [swap(model_blocks, d) for d in range(lo_count)]
+    models = [swap(model_blocks, d) for d in range(lo_count)]
     estimate, outgoing = pick(ids, sent_tiles, start_image)
     tiles = exchange(outgoing, "vox")
-    models = stage(*shared)
     signals = jnp.concatenate([swap(waves_of(measured, d), d) for d in range(lo_count)])
     index = jnp.stack([block_slots, block_rows])
     index = jnp.stack(

time: 136 us -> 133 us (0.978)
  waiting for transfers between devices: 12.3 us -> 17.6 us
  local copies, waits for them, and re-layouts: 15.8 us -> 12.4 us
  starting transfers between devices: 15.6 us -> 12.3 us
    all_to_all x2, waiting for transfers between devices: 10.1 us -> 16.5 us  [exchange(): return lax.all_to_all(array, axes, split_axis=0, concat_axis=0, tiled=True)]
    all_to_all x2, starting transfers between devices: 14.3 us -> 10.6 us  [exchange(): return lax.all_to_all(array, axes, split_axis=0, concat_axis=0, tiled=True)]
    unnamed x25 -> x23, local copies, waits for them, and re-layouts: 14.7 us -> 11.3 us
  transfers between devices with their start and end apart: 7 -> 7, of which waited for: 3 -> 3; matrix products, arithmetic and copies ran while one was open for 2% -> 2% of each run, Pallas kernels for 2% -> 1%
where the time goes in v8:
time: 133 us
  blocking collectives  64.8 us (49%)
  Pallas kernels  23.3 us (18%)
  waiting for transfers between devices  17.6 us (13%)
  local copies, waits for them, and re-layouts  12.4 us (9%)
  starting transfers between devices  12.3 us (9%)
  other arithmetic  1.45 us (1%)
    all_to_all x6, blocking collectives, exchange(): return lax.all_to_all(array, axes, split_axis=0, concat_axis=0, tiled=True)  64.8 us
    pallas_call x4, Pallas kernels, shards(): total, residual = apply_model(index, signals, tiles, *models)  17.2 us
    all_to_all x2, waiting for transfers between devices, exchange(): return lax.all_to_all(array, axes, split_axis=0, concat_axis=0, tiled=True)  16.5 us
    unnamed x23, local copies, waits for them, and re-layouts  11.3 us
    all_to_all x2, starting transfers between devices, exchange(): return lax.all_to_all(array, axes, split_axis=0, concat_axis=0, tiled=True)  10.6 us
    pallas_call x4, Pallas kernels, shards(): update(iteration == ITERATIONS - 1)(sent_tiles, gains, estimate, parts)  3.33 us
  transfers between devices with their start and end apart: 7, of which 3 were waited for; matrix products, arithmetic and copies ran while one was open for 2% of the time, Pallas kernels for 1%

profile of v8, /device:TPU:0, one launch (start us, length us, event | category | flops | bytes accessed | tf_op | source)
XLA Modules:
  0.0 132.6 jit_solution(18281967337290930982)
XLA Ops:
  1.9 0.9 dynamic-slice_bitcast_fusion.1
  3.3 0.8 copy.17.table
  4.0 1.0 copy-done.6
  5.1 1.3 pick.1
  6.4 0.7 copy-done.7
  7.1 6.8 %all-to-all-start = ((bf16[32,16,128]{2,1,0:T(8,128)(2,1)}), bf16[32,16,128]{2,1,0:T(8,128)(2,1)S(1)}, u32[]{:S(2)}, u32[]{:S(2)}) async-start(bf16[32,16,128]{2,1,0:T(8,128)(2,1)} %get-tuple-element.16), calls=%async_computation | async-start | bytes 262144 | tf_op jit(solution)/shard_map/all_to_all | solution.py:136
  14.0 0.7 pad_add_fusion.index
  14.7 6.8 %all-to-all-done.tiles = bf16[32,16,128]{2,1,0:T(8,128)(2,1)S(1)} async-done(((bf16[32,16,128]{2,1,0:T(8,128)(2,1)}), bf16[32,16,128]{2,1,0:T(8,128)(2,1)S(1)}, u32[]{:S(2)}, u32[]{:S(2)}) %all-to-all-start) | async-done | bytes 131104 | tf_op jit(solution)/shard_map/all_to_all | solution.py:136
  21.6 1.6 %copy-done.2 = bf16[92,128,128]{2,1,0:T(8,128)(2,1)} copy-done((bf16[92,128,128]{2,1,0:T(8,128)(2,1)}, bf16[92,128,128]{2,1,0:T(8,128)(2,1)S(1)}, u32[]{:S(2)}) %copy-start.2) | copy-done | bytes 3014680
  23.2 1.9 %copy-done = bf16[92,128,128]{2,1,0:T(8,128)(2,1)S(1)} copy-done((bf16[92,128,128]{2,1,0:T(8,128)(2,1)S(1)}, bf16[92,128,128]{2,1,0:T(8,128)(2,1)}, u32[]{:S(2)}) %copy-start) | copy-done | bytes 3014680
  25.0 1.9 %copy-done.3 = bf16[92,128,128]{2,1,0:T(8,128)(2,1)S(1)} copy-done((bf16[92,128,128]{2,1,0:T(8,128)(2,1)S(1)}, bf16[92,128,128]{2,1,0:T(8,128)(2,1)}, u32[]{:S(2)}) %copy-start.3) | copy-done | bytes 3014680
  26.9 4.4 %model.4 = (bf16[8,2,4,16,128]{4,3,2,1,0:T(8,128)(2,1)S(1)}, f32[16,16,128]{2,1,0:T(8,128)}) custom-call(s32[2,2,92]{2,1,0:T(2,128)S(1)} %pad_add_fusion.index, f32[16,16,128]{2,1,0:T(8,128)S(1)} %pad_maximum_fusion.measured, bf16[32,16,128]{2,1,0:T(8,128)(2,1)S(1)} %all-to-all-done.tiles, bf16[92,128,128]{2,1,0:T(8,128)(2,1)S(1)} %copy-done, ...), custom_call_target="tpu_custom_call" | custom-call | tf_op jit(solution)/shard_map/model/pallas_call | solution.py:201
  31.3 0.7 copy-done.9
  32.0 3.8 %all-to-all-start.1 = ((bf16[16,4,16,128]{3,2,1,0:T(8,128)(2,1)}), bf16[16,4,16,128]{3,2,1,0:T(8,128)(2,1)S(1)}, u32[]{:S(2)}, u32[]{:S(2)}) async-start(bf16[16,4,16,128]{3,2,1,0:T(8,128)(2,1)} %bitcast.28), calls=%async_computation.1 | async-start | bytes 524288 | tf_op jit(solution)/shard_map/all_to_all | solution.py:136
  35.9 9.7 %all-to-all-done.1 = bf16[16,4,16,128]{3,2,1,0:T(8,128)(2,1)S(1)} async-done(((bf16[16,4,16,128]{3,2,1,0:T(8,128)(2,1)}), bf16[16,4,16,128]{3,2,1,0:T(8,128)(2,1)S(1)}, u32[]{:S(2)}, u32[]{:S(2)}) %all-to-all-start.1) | async-done | bytes 262176 | tf_op jit(solution)/shard_map/all_to_all | solution.py:136
  45.6 0.9 copy-done.8
  46.6 0.8 update.4
  47.4 10.6 %all_to_all.40.tiles = bf16[32,16,128]{2,1,0:T(8,128)(2,1)S(1)} all-to-all(bf16[32,16,128]{2,1,0:T(8,128)(2,1)S(1)} %get-tuple-element.19), channel_id=1, replica_groups=mesh['vox'=8,'hi'=2,'lo'=2] {'vox'}, dimensions={0} | all-to-all | bytes 262144 | tf_op jit(solution)/shard_map/all_to_all | solution.py:136
  58.0 1.9 %copy-done.4 = bf16[92,128,128]{2,1,0:T(8,128)(2,1)S(1)} copy-done((bf16[92,128,128]{2,1,0:T(8,128)(2,1)S(1)}, bf16[92,128,128]{2,1,0:T(8,128)(2,1)}, u32[]{:S(2)}) %copy-start.4) | copy-done | bytes 3014680
  59.9 4.4 %model.5 = (bf16[8,2,4,16,128]{4,3,2,1,0:T(8,128)(2,1)S(1)}, f32[16,16,128]{2,1,0:T(8,128)}) custom-call(s32[2,2,92]{2,1,0:T(2,128)S(1)} %pad_add_fusion.index, f32[16,16,128]{2,1,0:T(8,128)S(1)} %pad_maximum_fusion.measured, bf16[32,16,128]{2,1,0:T(8,128)(2,1)S(1)} %all_to_all.40.tiles, bf16[92,128,128]{2,1,0:T(8,128)(2,1)S(1)} %copy-done.1, ...), custom_call_target="tpu_custom_call" | custom-call | tf_op jit(solution)/shard_map/model/pallas_call | solution.py:201
  64.3 11.1 %all_to_all.41 = bf16[16,4,16,128]{3,2,1,0:T(8,128)(2,1)S(1)} all-to-all(bf16[16,4,16,128]{3,2,1,0:T(8,128)(2,1)S(1)} %bitcast.30), channel_id=1, replica_groups=mesh['vox'=8,'hi'=2,'lo'=2] {'vox','hi'}, dimensions={0} | all-to-all | bytes 524288 | tf_op jit(solution)/shard_map/all_to_all | solution.py:136
  75.4 0.8 update.5
  76.2 10.5 %all_to_all.42.tiles = bf16[32,16,128]{2,1,0:T(8,128)(2,1)S(1)} all-to-all(bf16[32,16,128]{2,1,0:T(8,128)(2,1)S(1)} %get-tuple-element.22), channel_id=1, replica_groups=mesh['vox'=8,'hi'=2,'lo'=2] {'vox'}, dimensions={0} | all-to-all | bytes 262144 | tf_op jit(solution)/shard_map/all_to_all | solution.py:136
  86.8 4.4 %model.6 = (bf16[8,2,4,16,128]{4,3,2,1,0:T(8,128)(2,1)S(1)}, f32[16,16,128]{2,1,0:T(8,128)}) custom-call(s32[2,2,92]{2,1,0:T(2,128)S(1)} %pad_add_fusion.index, f32[16,16,128]{2,1,0:T(8,128)S(1)} %pad_maximum_fusion.measured, bf16[32,16,128]{2,1,0:T(8,128)(2,1)S(1)} %all_to_all.42.tiles, bf16[92,128,128]{2,1,0:T(8,128)(2,1)S(1)} %copy-done.1, ...), custom_call_target="tpu_custom_call" | custom-call | tf_op jit(solution)/shard_map/model/pallas_call | solution.py:201
  91.2 11.1 %all_to_all.43 = bf16[16,4,16,128]{3,2,1,0:T(8,128)(2,1)S(1)} all-to-all(bf16[16,4,16,128]{3,2,1,0:T(8,128)(2,1)S(1)} %bitcast.31), channel_id=1, replica_groups=mesh['vox'=8,'hi'=2,'lo'=2] {'vox','hi'}, dimensions={0} | all-to-all | bytes 524288 | tf_op jit(solution)/shard_map/all_to_all | solution.py:136
  102.3 0.8 update.6
  103.1 10.5 %all_to_all.44.tiles = bf16[32,16,128]{2,1,0:T(8,128)(2,1)S(1)} all-to-all(bf16[32,16,128]{2,1,0:T(8,128)(2,1)S(1)} %get-tuple-element.25), channel_id=1, replica_groups=mesh['vox'=8,'hi'=2,'lo'=2] {'vox'}, dimensions={0} | all-to-all | bytes 262144 | tf_op jit(solution)/shard_map/all_to_all | solution.py:136
  113.6 3.9 %model.7 = (bf16[8,2,4,16,128]{4,3,2,1,0:T(8,128)(2,1)S(1)}, f32[16,16,128]{2,1,0:T(8,128)S(1)}) custom-call(s32[2,2,92]{2,1,0:T(2,128)S(1)} %pad_add_fusion.index, f32[16,16,128]{2,1,0:T(8,128)S(1)} %pad_maximum_fusion.measured, bf16[32,16,128]{2,1,0:T(8,128)(2,1)S(1)} %all_to_all.44.tiles, bf16[92,128,128]{2,1,0:T(8,128)(2,1)S(1)} %copy-done.1, ...), custom_call_target="tpu_custom_call" | custom-call | tf_op jit(solution)/shard_map/model/pallas_call | solution.py:201
  117.5 11.1 %all_to_all.45 = bf16[16,4,16,128]{3,2,1,0:T(8,128)(2,1)S(1)} all-to-all(bf16[16,4,16,128]{3,2,1,0:T(8,128)(2,1)S(1)} %bitcast.29), channel_id=1, replica_groups=mesh['vox'=8,'hi'=2,'lo'=2] {'vox','hi'}, dimensions={0} | all-to-all | bytes 524288 | tf_op jit(solution)/shard_map/all_to_all | solution.py:136
  128.6 0.8 update.7.refs_0_
  130.1 1.0 collective-permute-done.4.refs_1_
  131.8 0.8 join.2
  (31 shorter events, 3.3 us)
Async XLA Ops:
  0.6 20.9 %collective-permute-start.2 = (bf16[92,128,128]{2,1,0:T(8,128)(2,1)}, bf16[92,128,128]{2,1,0:T(8,128)(2,1)S(1)}, u32[]{:S(2)}, u32[]{:S(2)}) collective-permute-start(bf16[92,128,128]{2,1,0:T(8,128)(2,1)} %refs_0_.7), channel_id=1, source_target_pairs={{0,1},{1,0},{2,3},{3,2},{4,5},{5,4},{6,7},{7,6},{8,9},{9,8},{10,11... | collective-permute-start | bytes 9043976 | tf_op jit(solution)/shard_map/ppermute | solution.py:133
  1.8 12.1 %collective-permute-start = (s32[2,92]{1,0:T(2,128)S(1)}, s32[2,92]{1,0:T(2,128)S(1)}, u32[]{:S(2)}, u32[]{:S(2)}) collective-permute-start(s32[2,92]{1,0:T(2,128)S(1)} %pad_add_fusion.1), channel_id=1, source_target_pairs={{0,1},{1,0},{2,3},{3,2},{4,5},{5,4},{6,7},{7,6},{8,9},{9,8},{10,11... | collective-permute-start | bytes 2216 | tf_op jit(solution)/shard_map/ppermute | solution.py:133
  2.8 11.9 %collective-permute-start.1 = (f32[8,16,128]{2,1,0:T(8,128)S(1)}, f32[8,16,128]{2,1,0:T(8,128)S(1)}, u32[]{:S(2)}, u32[]{:S(2)}) collective-permute-start(f32[8,16,128]{2,1,0:T(8,128)S(1)} %get-tuple-element.31), channel_id=1, source_target_pairs={{0,1},{1,0},{2,3},{3,2},{4,5},{5,4},{6,7},{7,6},{8,9},{9,8},{10,11... | collective-permute-start | bytes 196616 | tf_op jit(solution)/shard_map/ppermute | solution.py:133
  4.0 1.0 copy-start.6
  6.4 0.7 copy-start.7
  7.1 14.5 %all-to-all-start = ((bf16[32,16,128]{2,1,0:T(8,128)(2,1)}), bf16[32,16,128]{2,1,0:T(8,128)(2,1)S(1)}, u32[]{:S(2)}, u32[]{:S(2)}) async-start(bf16[32,16,128]{2,1,0:T(8,128)(2,1)} %get-tuple-element.16), calls=%async_computation | async-start | bytes 262144 | tf_op jit(solution)/shard_map/all_to_all | solution.py:136
  14.7 21.1 %copy-start.10 = (f32[32]{0:T(128)S(1)}, f32[32]{0:T(128)}, u32[]{:S(2)}) copy-start(f32[32]{0:T(128)} %param.12) | copy-start | bytes 388
  21.5 1.6 %copy-start.2 = (bf16[92,128,128]{2,1,0:T(8,128)(2,1)}, bf16[92,128,128]{2,1,0:T(8,128)(2,1)S(1)}, u32[]{:S(2)}) copy-start(bf16[92,128,128]{2,1,0:T(8,128)(2,1)S(1)} %collective-permute-done.2.refs_1_) | copy-start | bytes 9043972
  23.2 1.9 %copy-start = (bf16[92,128,128]{2,1,0:T(8,128)(2,1)S(1)}, bf16[92,128,128]{2,1,0:T(8,128)(2,1)}, u32[]{:S(2)}) copy-start(bf16[92,128,128]{2,1,0:T(8,128)(2,1)} %refs_0_.7) | copy-start | bytes 9043972
  25.0 1.9 %copy-start.3 = (bf16[92,128,128]{2,1,0:T(8,128)(2,1)S(1)}, bf16[92,128,128]{2,1,0:T(8,128)(2,1)}, u32[]{:S(2)}) copy-start(bf16[92,128,128]{2,1,0:T(8,128)(2,1)} %copy-done.2) | copy-start | bytes 9043972
  26.9 31.1 %copy-start.1 = (bf16[92,128,128]{2,1,0:T(8,128)(2,1)S(1)}, bf16[92,128,128]{2,1,0:T(8,128)(2,1)}, u32[]{:S(2)}) copy-start(bf16[92,128,128]{2,1,0:T(8,128)(2,1)} %refs_0_.7) | copy-start | bytes 9043972
  31.3 0.7 copy-start.9
  32.0 13.6 %all-to-all-start.1 = ((bf16[16,4,16,128]{3,2,1,0:T(8,128)(2,1)}), bf16[16,4,16,128]{3,2,1,0:T(8,128)(2,1)S(1)}, u32[]{:S(2)}, u32[]{:S(2)}) async-start(bf16[16,4,16,128]{3,2,1,0:T(8,128)(2,1)} %bitcast.28), calls=%async_computation.1 | async-start | bytes 524288 | tf_op jit(solution)/shard_map/all_to_all | solution.py:136
  45.6 1.0 copy-start.8
  58.0 1.9 %copy-start.4 = (bf16[92,128,128]{2,1,0:T(8,128)(2,1)S(1)}, bf16[92,128,128]{2,1,0:T(8,128)(2,1)}, u32[]{:S(2)}) copy-start(bf16[92,128,128]{2,1,0:T(8,128)(2,1)} %copy-done.2) | copy-start | bytes 9043972
  59.9 26.9 %copy-start.5 = (bf16[92,128,128]{2,1,0:T(8,128)(2,1)S(1)}, bf16[92,128,128]{2,1,0:T(8,128)(2,1)}, u32[]{:S(2)}) copy-start(bf16[92,128,128]{2,1,0:T(8,128)(2,1)} %copy-done.2) | copy-start | bytes 9043972
  129.4 2.4 %collective-permute-start.3 = (f32[32,16,128]{2,1,0:T(8,128)S(1)}, f32[32,16,128]{2,1,0:T(8,128)S(1)}, u32[]{:S(2)}, u32[]{:S(2)}) collective-permute-start(f32[32,16,128]{2,1,0:T(8,128)S(1)} %update.7.refs_0_), channel_id=1, source_target_pairs={{0,1},{1,0},{2,3},{3,2},{4,5},{5,4},{6,7},{7,6},{8,9},{9,8},{10,11... | collective-permute-start | bytes 786440 | tf_op jit(solution)/shard_map/ppermute | solution.py:133
  129.5 1.6 %collective-permute-start.4 = (f32[8,16,128]{2,1,0:T(8,128)S(1)}, f32[8,16,128]{2,1,0:T(8,128)S(1)}, u32[]{:S(2)}, u32[]{:S(2)}) collective-permute-start(f32[8,16,128]{2,1,0:T(8,128)S(1)} %get-tuple-element.28), channel_id=1, source_target_pairs={{0,1},{1,0},{2,3},{3,2},{4,5},{5,4},{6,7},{7,6},{8,9},{9,8},{10,11... | collective-permute-start | bytes 196616 | tf_op jit(solution)/shard_map/ppermute | solution.py:133

commit v9 on v8

--- a/solution.py
+++ b/solution.py
@@ -189,6 +189,9 @@
     models = [swap(model_blocks, d) for d in range(lo_count)]
     estimate, outgoing = pick(ids, sent_tiles, start_image)
     tiles = exchange(outgoing, "vox")
+    _, measured, block_slots, block_rows = lax.optimization_barrier(
+        (outgoing, measured, block_slots, block_rows)
+    )
     signals = jnp.concatenate([swap(waves_of(measured, d), d) for d in range(lo_count)])
     index = jnp.stack([block_slots, block_rows])
     index = jnp.stack(

time: 133 us -> 131 us (0.985)
  waiting for transfers between devices: 17.6 us -> 15.5 us
    all_to_all x2, waiting for transfers between devices: 16.5 us -> 14.2 us  [exchange(): return lax.all_to_all(array, axes, split_axis=0, concat_axis=0, tiled=True)]
  transfers between devices with their start and end apart: 7 -> 7, of which waited for: 3 -> 4; matrix products, arithmetic and copies ran while one was open for 2% -> 2% of each run, Pallas kernels for 1% -> 2%
where the time goes in v9:
time: 131 us; the launch traced here: 130 us
  blocking collectives  64.8 us (49%)
  Pallas kernels  23.4 us (18%)
  waiting for transfers between devices  15.5 us (12%)
  local copies, waits for them, and re-layouts  12.4 us (9%)
  starting transfers between devices  12.3 us (9%)
  other arithmetic  1.44 us (1%)
    all_to_all x6, blocking collectives, exchange(): return lax.all_to_all(array, axes, split_axis=0, concat_axis=0, tiled=True)  64.8 us
    pallas_call x4, Pallas kernels, shards(): total, residual = apply_model(index, signals, tiles, *models)  17.2 us
    all_to_all x2, waiting for transfers between devices, exchange(): return lax.all_to_all(array, axes, split_axis=0, concat_axis=0, tiled=True)  14.2 us
    unnamed x23, local copies, waits for them, and re-layouts  11.3 us
    all_to_all x2, starting transfers between devices, exchange(): return lax.all_to_all(array, axes, split_axis=0, concat_axis=0, tiled=True)  10.6 us
    pallas_call x4, Pallas kernels, shards(): update(iteration == ITERATIONS - 1)(sent_tiles, gains, estimate, parts)  3.35 us
  transfers between devices with their start and end apart: 7, of which 4 were waited for; matrix products, arithmetic and copies ran while one was open for 2% of the time, Pallas kernels for 2%

profile of v9, /device:TPU:0, one launch (start us, length us, event | category | flops | bytes accessed | tf_op | source)
XLA Modules:
  0.0 130.5 jit_solution(13262413885017320733)
XLA Ops:
  1.1 0.8 copy.17.table
  1.9 1.0 copy-done.6
  2.9 1.3 pick.1
  4.2 0.7 copy-done.7
  4.9 6.8 %all-to-all-start = ((bf16[32,16,128]{2,1,0:T(8,128)(2,1)}), bf16[32,16,128]{2,1,0:T(8,128)(2,1)S(1)}, u32[]{:S(2)}, u32[]{:S(2)}) async-start(bf16[32,16,128]{2,1,0:T(8,128)(2,1)} %get-tuple-element.19), calls=%async_computation | async-start | bytes 262144 | tf_op jit(solution)/shard_map/all_to_all | solution.py:136
  12.7 0.9 dynamic-slice_bitcast_fusion.1
  14.0 0.7 pad_add_fusion.index
  14.9 4.5 %all-to-all-done.tiles = bf16[32,16,128]{2,1,0:T(8,128)(2,1)S(1)} async-done(((bf16[32,16,128]{2,1,0:T(8,128)(2,1)}), bf16[32,16,128]{2,1,0:T(8,128)(2,1)S(1)}, u32[]{:S(2)}, u32[]{:S(2)}) %all-to-all-start) | async-done | bytes 131104 | tf_op jit(solution)/shard_map/all_to_all | solution.py:136
  19.4 1.6 %copy-done.2 = bf16[92,128,128]{2,1,0:T(8,128)(2,1)} copy-done((bf16[92,128,128]{2,1,0:T(8,128)(2,1)}, bf16[92,128,128]{2,1,0:T(8,128)(2,1)S(1)}, u32[]{:S(2)}) %copy-start.2) | copy-done | bytes 3014680
  21.0 1.9 %copy-done = bf16[92,128,128]{2,1,0:T(8,128)(2,1)S(1)} copy-done((bf16[92,128,128]{2,1,0:T(8,128)(2,1)S(1)}, bf16[92,128,128]{2,1,0:T(8,128)(2,1)}, u32[]{:S(2)}) %copy-start) | copy-done | bytes 3014680
  22.9 1.9 %copy-done.3 = bf16[92,128,128]{2,1,0:T(8,128)(2,1)S(1)} copy-done((bf16[92,128,128]{2,1,0:T(8,128)(2,1)S(1)}, bf16[92,128,128]{2,1,0:T(8,128)(2,1)}, u32[]{:S(2)}) %copy-start.3) | copy-done | bytes 3014680
  24.7 4.4 %model.4 = (bf16[8,2,4,16,128]{4,3,2,1,0:T(8,128)(2,1)S(1)}, f32[16,16,128]{2,1,0:T(8,128)}) custom-call(s32[2,2,92]{2,1,0:T(2,128)S(1)} %pad_add_fusion.index, f32[16,16,128]{2,1,0:T(8,128)S(1)} %pad_maximum_fusion.measured, bf16[32,16,128]{2,1,0:T(8,128)(2,1)S(1)} %all-to-all-done.tiles, bf16[92,128,128]{2,1,0:T(8,128)(2,1)S(1)} %copy-done, ...), custom_call_target="tpu_custom_call" | custom-call | tf_op jit(solution)/shard_map/model/pallas_call | solution.py:204
  29.2 0.7 copy-done.9
  29.9 3.8 %all-to-all-start.1 = ((bf16[16,4,16,128]{3,2,1,0:T(8,128)(2,1)}), bf16[16,4,16,128]{3,2,1,0:T(8,128)(2,1)S(1)}, u32[]{:S(2)}, u32[]{:S(2)}) async-start(bf16[16,4,16,128]{3,2,1,0:T(8,128)(2,1)} %bitcast.28), calls=%async_computation.1 | async-start | bytes 524288 | tf_op jit(solution)/shard_map/all_to_all | solution.py:136
  33.7 9.7 %all-to-all-done.1 = bf16[16,4,16,128]{3,2,1,0:T(8,128)(2,1)S(1)} async-done(((bf16[16,4,16,128]{3,2,1,0:T(8,128)(2,1)}), bf16[16,4,16,128]{3,2,1,0:T(8,128)(2,1)S(1)}, u32[]{:S(2)}, u32[]{:S(2)}) %all-to-all-start.1) | async-done | bytes 262176 | tf_op jit(solution)/shard_map/all_to_all | solution.py:136
  43.5 0.9 copy-done.8
  44.5 0.8 update.4
  45.3 10.6 %all_to_all.40.tiles = bf16[32,16,128]{2,1,0:T(8,128)(2,1)S(1)} all-to-all(bf16[32,16,128]{2,1,0:T(8,128)(2,1)S(1)} %get-tuple-element.25), channel_id=1, replica_groups=mesh['vox'=8,'hi'=2,'lo'=2] {'vox'}, dimensions={0} | all-to-all | bytes 262144 | tf_op jit(solution)/shard_map/all_to_all | solution.py:136
  55.9 1.9 %copy-done.4 = bf16[92,128,128]{2,1,0:T(8,128)(2,1)S(1)} copy-done((bf16[92,128,128]{2,1,0:T(8,128)(2,1)S(1)}, bf16[92,128,128]{2,1,0:T(8,128)(2,1)}, u32[]{:S(2)}) %copy-start.4) | copy-done | bytes 3014680
  57.7 4.5 %model.5 = (bf16[8,2,4,16,128]{4,3,2,1,0:T(8,128)(2,1)S(1)}, f32[16,16,128]{2,1,0:T(8,128)}) custom-call(s32[2,2,92]{2,1,0:T(2,128)S(1)} %pad_add_fusion.index, f32[16,16,128]{2,1,0:T(8,128)S(1)} %pad_maximum_fusion.measured, bf16[32,16,128]{2,1,0:T(8,128)(2,1)S(1)} %all_to_all.40.tiles, bf16[92,128,128]{2,1,0:T(8,128)(2,1)S(1)} %copy-done.1, ...), custom_call_target="tpu_custom_call" | custom-call | tf_op jit(solution)/shard_map/model/pallas_call | solution.py:204
  62.2 11.1 %all_to_all.41 = bf16[16,4,16,128]{3,2,1,0:T(8,128)(2,1)S(1)} all-to-all(bf16[16,4,16,128]{3,2,1,0:T(8,128)(2,1)S(1)} %bitcast.30), channel_id=1, replica_groups=mesh['vox'=8,'hi'=2,'lo'=2] {'vox','hi'}, dimensions={0} | all-to-all | bytes 524288 | tf_op jit(solution)/shard_map/all_to_all | solution.py:136
  73.3 0.8 update.5
  74.1 10.5 %all_to_all.42.tiles = bf16[32,16,128]{2,1,0:T(8,128)(2,1)S(1)} all-to-all(bf16[32,16,128]{2,1,0:T(8,128)(2,1)S(1)} %get-tuple-element.28), channel_id=1, replica_groups=mesh['vox'=8,'hi'=2,'lo'=2] {'vox'}, dimensions={0} | all-to-all | bytes 262144 | tf_op jit(solution)/shard_map/all_to_all | solution.py:136
  84.6 4.5 %model.6 = (bf16[8,2,4,16,128]{4,3,2,1,0:T(8,128)(2,1)S(1)}, f32[16,16,128]{2,1,0:T(8,128)}) custom-call(s32[2,2,92]{2,1,0:T(2,128)S(1)} %pad_add_fusion.index, f32[16,16,128]{2,1,0:T(8,128)S(1)} %pad_maximum_fusion.measured, bf16[32,16,128]{2,1,0:T(8,128)(2,1)S(1)} %all_to_all.42.tiles, bf16[92,128,128]{2,1,0:T(8,128)(2,1)S(1)} %copy-done.1, ...), custom_call_target="tpu_custom_call" | custom-call | tf_op jit(solution)/shard_map/model/pallas_call | solution.py:204
  89.1 11.1 %all_to_all.43 = bf16[16,4,16,128]{3,2,1,0:T(8,128)(2,1)S(1)} all-to-all(bf16[16,4,16,128]{3,2,1,0:T(8,128)(2,1)S(1)} %bitcast.31), channel_id=1, replica_groups=mesh['vox'=8,'hi'=2,'lo'=2] {'vox','hi'}, dimensions={0} | all-to-all | bytes 524288 | tf_op jit(solution)/shard_map/all_to_all | solution.py:136
  100.1 0.8 update.6
  101.0 10.5 %all_to_all.44.tiles = bf16[32,16,128]{2,1,0:T(8,128)(2,1)S(1)} all-to-all(bf16[32,16,128]{2,1,0:T(8,128)(2,1)S(1)} %get-tuple-element.31), channel_id=1, replica_groups=mesh['vox'=8,'hi'=2,'lo'=2] {'vox'}, dimensions={0} | all-to-all | bytes 262144 | tf_op jit(solution)/shard_map/all_to_all | solution.py:136
  111.5 3.9 %model.7 = (bf16[8,2,4,16,128]{4,3,2,1,0:T(8,128)(2,1)S(1)}, f32[16,16,128]{2,1,0:T(8,128)S(1)}) custom-call(s32[2,2,92]{2,1,0:T(2,128)S(1)} %pad_add_fusion.index, f32[16,16,128]{2,1,0:T(8,128)S(1)} %pad_maximum_fusion.measured, bf16[32,16,128]{2,1,0:T(8,128)(2,1)S(1)} %all_to_all.44.tiles, bf16[92,128,128]{2,1,0:T(8,128)(2,1)S(1)} %copy-done.1, ...), custom_call_target="tpu_custom_call" | custom-call | tf_op jit(solution)/shard_map/model/pallas_call | solution.py:204
  115.4 11.1 %all_to_all.45 = bf16[16,4,16,128]{3,2,1,0:T(8,128)(2,1)S(1)} all-to-all(bf16[16,4,16,128]{3,2,1,0:T(8,128)(2,1)S(1)} %bitcast.29), channel_id=1, replica_groups=mesh['vox'=8,'hi'=2,'lo'=2] {'vox','hi'}, dimensions={0} | all-to-all | bytes 524288 | tf_op jit(solution)/shard_map/all_to_all | solution.py:136
  126.5 0.8 update.7.refs_0_
  128.0 1.0 collective-permute-done.4.refs_1_
  129.7 0.8 join.2
  (31 shorter events, 3.5 us)
Async XLA Ops:
  0.6 18.8 %collective-permute-start.2 = (bf16[92,128,128]{2,1,0:T(8,128)(2,1)}, bf16[92,128,128]{2,1,0:T(8,128)(2,1)S(1)}, u32[]{:S(2)}, u32[]{:S(2)}) collective-permute-start(bf16[92,128,128]{2,1,0:T(8,128)(2,1)} %refs_0_.7), channel_id=1, source_target_pairs={{0,1},{1,0},{2,3},{3,2},{4,5},{5,4},{6,7},{7,6},{8,9},{9,8},{10,11... | collective-permute-start | bytes 9043976 | tf_op jit(solution)/shard_map/ppermute | solution.py:133
  1.9 1.0 copy-start.6
  4.2 0.7 copy-start.7
  4.9 14.5 %all-to-all-start = ((bf16[32,16,128]{2,1,0:T(8,128)(2,1)}), bf16[32,16,128]{2,1,0:T(8,128)(2,1)S(1)}, u32[]{:S(2)}, u32[]{:S(2)}) async-start(bf16[32,16,128]{2,1,0:T(8,128)(2,1)} %get-tuple-element.19), calls=%async_computation | async-start | bytes 262144 | tf_op jit(solution)/shard_map/all_to_all | solution.py:136
  12.4 1.5 %collective-permute-start = (s32[2,92]{1,0:T(2,128)S(1)}, s32[2,92]{1,0:T(2,128)S(1)}, u32[]{:S(2)}, u32[]{:S(2)}) collective-permute-start(s32[2,92]{1,0:T(2,128)S(1)} %pad_add_fusion.1), channel_id=1, source_target_pairs={{0,1},{1,0},{2,3},{3,2},{4,5},{5,4},{6,7},{7,6},{8,9},{9,8},{10,11... | collective-permute-start | bytes 2216 | tf_op jit(solution)/shard_map/ppermute | solution.py:133
  13.5 1.3 %collective-permute-start.1 = (f32[8,16,128]{2,1,0:T(8,128)S(1)}, f32[8,16,128]{2,1,0:T(8,128)S(1)}, u32[]{:S(2)}, u32[]{:S(2)}) collective-permute-start(f32[8,16,128]{2,1,0:T(8,128)S(1)} %get-tuple-element.37), channel_id=1, source_target_pairs={{0,1},{1,0},{2,3},{3,2},{4,5},{5,4},{6,7},{7,6},{8,9},{9,8},{10,11... | collective-permute-start | bytes 196616 | tf_op jit(solution)/shard_map/ppermute | solution.py:133
  14.9 18.8 %copy-start.10 = (f32[32]{0:T(128)S(1)}, f32[32]{0:T(128)}, u32[]{:S(2)}) copy-start(f32[32]{0:T(128)} %param.12) | copy-start | bytes 388
  19.4 1.6 %copy-start.2 = (bf16[92,128,128]{2,1,0:T(8,128)(2,1)}, bf16[92,128,128]{2,1,0:T(8,128)(2,1)S(1)}, u32[]{:S(2)}) copy-start(bf16[92,128,128]{2,1,0:T(8,128)(2,1)S(1)} %collective-permute-done.2.refs_1_) | copy-start | bytes 9043972
  21.0 1.9 %copy-start = (bf16[92,128,128]{2,1,0:T(8,128)(2,1)S(1)}, bf16[92,128,128]{2,1,0:T(8,128)(2,1)}, u32[]{:S(2)}) copy-start(bf16[92,128,128]{2,1,0:T(8,128)(2,1)} %refs_0_.7) | copy-start | bytes 9043972
  22.9 1.9 %copy-start.3 = (bf16[92,128,128]{2,1,0:T(8,128)(2,1)S(1)}, bf16[92,128,128]{2,1,0:T(8,128)(2,1)}, u32[]{:S(2)}) copy-start(bf16[92,128,128]{2,1,0:T(8,128)(2,1)} %copy-done.2) | copy-start | bytes 9043972
  24.7 31.2 %copy-start.1 = (bf16[92,128,128]{2,1,0:T(8,128)(2,1)S(1)}, bf16[92,128,128]{2,1,0:T(8,128)(2,1)}, u32[]{:S(2)}) copy-start(bf16[92,128,128]{2,1,0:T(8,128)(2,1)} %refs_0_.7) | copy-start | bytes 9043972
  29.2 0.7 copy-start.9
  29.9 13.6 %all-to-all-start.1 = ((bf16[16,4,16,128]{3,2,1,0:T(8,128)(2,1)}), bf16[16,4,16,128]{3,2,1,0:T(8,128)(2,1)S(1)}, u32[]{:S(2)}, u32[]{:S(2)}) async-start(bf16[16,4,16,128]{3,2,1,0:T(8,128)(2,1)} %bitcast.28), calls=%async_computation.1 | async-start | bytes 524288 | tf_op jit(solution)/shard_map/all_to_all | solution.py:136
  43.5 1.0 copy-start.8
  55.9 1.9 %copy-start.4 = (bf16[92,128,128]{2,1,0:T(8,128)(2,1)S(1)}, bf16[92,128,128]{2,1,0:T(8,128)(2,1)}, u32[]{:S(2)}) copy-start(bf16[92,128,128]{2,1,0:T(8,128)(2,1)} %copy-done.2) | copy-start | bytes 9043972
  57.7 26.9 %copy-start.5 = (bf16[92,128,128]{2,1,0:T(8,128)(2,1)S(1)}, bf16[92,128,128]{2,1,0:T(8,128)(2,1)}, u32[]{:S(2)}) copy-start(bf16[92,128,128]{2,1,0:T(8,128)(2,1)} %copy-done.2) | copy-start | bytes 9043972
  127.3 2.4 %collective-permute-start.3 = (f32[32,16,128]{2,1,0:T(8,128)S(1)}, f32[32,16,128]{2,1,0:T(8,128)S(1)}, u32[]{:S(2)}, u32[]{:S(2)}) collective-permute-start(f32[32,16,128]{2,1,0:T(8,128)S(1)} %update.7.refs_0_), channel_id=1, source_target_pairs={{0,1},{1,0},{2,3},{3,2},{4,5},{5,4},{6,7},{7,6},{8,9},{9,8},{10,11... | collective-permute-start | bytes 786440 | tf_op jit(solution)/shard_map/ppermute | solution.py:133
  127.4 1.6 %collective-permute-start.4 = (f32[8,16,128]{2,1,0:T(8,128)S(1)}, f32[8,16,128]{2,1,0:T(8,128)S(1)}, u32[]{:S(2)}, u32[]{:S(2)}) collective-permute-start(f32[8,16,128]{2,1,0:T(8,128)S(1)} %get-tuple-element.34), channel_id=1, source_target_pairs={{0,1},{1,0},{2,3},{3,2},{4,5},{5,4},{6,7},{7,6},{8,9},{9,8},{10,11... | collective-permute-start | bytes 196616 | tf_op jit(solution)/shard_map/ppermute | solution.py:133
